TPU v7x, 32 devices: a whole 2x2x4 slice. The times are simulated.
32 devices in a mesh: seq: 4 (over z), exp: 8 (over y, x, core).
Axes of the slice: x: 2, y: 2, z: 4, core: 2. Of those that a mesh axis runs over, the one named last changes fastest.
Arguments:
- attn_inputs: bfloat16 [8, 512, 6144], P('exp', 'seq'), may hold values from -8 to 8
- residual: bfloat16 [8, 512, 2048], P('exp', 'seq'), may hold values from -6 to 6
- out_weight: bfloat16 [2048, 2048], P('exp'), may hold values from -0.125 to 0.125
- norm_gain: float32 [2048], replicated, may hold values from 0.1 to 1.9
- expert_ids: int32 [8, 512, 2], P('exp', 'seq'), may hold values from 0 to 7, all different within a row; in each aligned block of 128 rows (0 to 127, 128 to 255, ..., all dimensions but the last counted through in order) at most 40 rows name the same one
- gate_weights: float32 [8, 512, 2], P('exp', 'seq'), may hold values from 0.1 to 1
- gate_weight: bfloat16 [8, 2048, 5632], P('exp', None, 'seq'), may hold values from -0.125 to 0.125
- up_weight: bfloat16 [8, 2048, 5632], P('exp', None, 'seq'), may hold values from -0.125 to 0.125
- down_weight: bfloat16 [8, 5632, 2048], P('exp', 'seq'), may hold values from -0.078125 to 0.078125
Outputs:
- layer_out: bfloat16 [8, 512, 2048], P('exp', 'seq')
Inputs may be any that keep to these rules, and one draw needn't show every extreme that they name: `expert_ids`: each token names 2 different experts; in every draw no expert is named by more than 40 of the 128 tokens of one aligned block of rows (the rows of one device), and some block reaches 40.
All inputs are finite; a program needn't handle non-finite values.
Results may differ from a plain program's by a relative error of at most 0.013.
Values may be sent and summed in bfloat16 or wider, within the bound.
No kernel may reach another device: no remote copies, remote signals or barrier semaphores. Data moves between devices by JAX's collectives and lax.ppermute only.
A program may use at most 128 MiB of HBM per device.

v0:
```python
import jax
import jax.numpy as jnp
from jax import lax
from jax.sharding import PartitionSpec as P

HEADS = 16
HEAD_DIM = 128
TOP = 2


def attend_block(query_block, key_rows, value_rows):
    scores = jnp.einsum(
        "qhd,khd->hqk", query_block, key_rows, preferred_element_type=jnp.float32
    ) * HEAD_DIM ** (-0.5)
    attn_probs = jax.nn.softmax(scores, axis=-1).astype(jnp.bfloat16)
    mixed_heads = jnp.einsum(
        "hqk,khd->qhd", attn_probs, value_rows, preferred_element_type=jnp.float32
    )
    return mixed_heads.astype(jnp.bfloat16)


def expert_rows_apply(tok_rows, gate_mat, up_mat, down_mat):
    gate_val = jnp.dot(tok_rows, gate_mat, preferred_element_type=jnp.float32)
    up_val = jnp.dot(tok_rows, up_mat, preferred_element_type=jnp.float32)
    hidden = (jax.nn.silu(gate_val) * up_val).astype(jnp.bfloat16)
    return jnp.dot(hidden, down_mat, preferred_element_type=jnp.float32)


def per_device(
    attn_inputs,
    residual,
    out_weight,
    norm_gain,
    expert_ids,
    gate_weights,
    gate_weight,
    up_weight,
    down_weight,
):
    tok_count = attn_inputs.shape[1]
    seq_count = lax.axis_size("seq")
    expert_count = lax.axis_size("exp")
    model_width = residual.shape[-1]
    head_local = HEADS // seq_count
    laid = attn_inputs.reshape(tok_count, 3, seq_count, head_local * HEAD_DIM)
    by_heads = lax.all_to_all(laid, "seq", split_axis=2, concat_axis=0, tiled=True)
    clip_len = by_heads.shape[0]
    queries = by_heads[:, 0, 0].reshape(clip_len, head_local, HEAD_DIM)
    keys_all = by_heads[:, 1, 0].reshape(clip_len, head_local, HEAD_DIM)
    values_all = by_heads[:, 2, 0].reshape(clip_len, head_local, HEAD_DIM)
    block_rows = min(512, clip_len)
    query_blocks = queries.reshape(clip_len // block_rows, block_rows, head_local, HEAD_DIM)
    attended = lax.map(lambda block: attend_block(block, keys_all, values_all), query_blocks)
    attended = attended.reshape(clip_len, head_local * HEAD_DIM)
    merged = lax.all_to_all(attended, "seq", split_axis=0, concat_axis=1, tiled=True)
    projected = jnp.dot(
        merged,
        lax.all_gather(out_weight, "exp", axis=0, tiled=True),
        preferred_element_type=jnp.float32,
    )
    middle = lax.optimization_barrier(
        (residual.reshape(tok_count, model_width).astype(jnp.float32) + projected).astype(
            jnp.bfloat16
        )
    )
    mid_float = middle.astype(jnp.float32)
    normed = (
        mid_float
        * lax.rsqrt(jnp.mean(mid_float * mid_float, axis=-1, keepdims=True) + 1e-06)
        * norm_gain
    ).astype(jnp.bfloat16)
    capacity = 5 * tok_count // (2 * expert_count)
    route_ids = expert_ids.reshape(tok_count * TOP)
    one_hot = (route_ids[:, None] == jnp.arange(expert_count, dtype=jnp.int32)[None, :]).astype(
        jnp.int32
    )
    before = jnp.cumsum(one_hot, axis=0) - one_hot
    slot_ids = jnp.sum(before * one_hot, axis=-1)
    target = route_ids * capacity + slot_ids
    placing = (
        target[None, :] == jnp.arange(expert_count * capacity, dtype=jnp.int32)[:, None]
    ).astype(jnp.bfloat16)
    pair_rows = jnp.repeat(normed, TOP, axis=0)
    slotted = jnp.dot(placing, pair_rows, preferred_element_type=jnp.float32).astype(jnp.bfloat16)
    gate_mat = gate_weight[0]
    up_mat = up_weight[0]
    down_mat = down_weight[0]
    copies = jnp.broadcast_to(slotted[None], (seq_count, expert_count * capacity, model_width))
    copies = copies.reshape(seq_count * expert_count, capacity, model_width)
    arrived = lax.all_to_all(copies, ("seq", "exp"), split_axis=0, concat_axis=0, tiled=True)
    partial_value = expert_rows_apply(
        arrived.reshape(-1, model_width), gate_mat, up_mat, down_mat
    ).astype(jnp.bfloat16)
    partial_value = partial_value.reshape(seq_count * expert_count, capacity, model_width)
    returned = lax.all_to_all(
        partial_value, ("seq", "exp"), split_axis=0, concat_axis=0, tiled=True
    )
    returned = returned.reshape(seq_count, expert_count * capacity, model_width)
    expert_out = jnp.sum(returned.astype(jnp.float32), axis=0).astype(jnp.bfloat16)
    picked = jnp.dot(placing.T, expert_out, preferred_element_type=jnp.float32)
    weighted = picked.reshape(tok_count, TOP, model_width) * gate_weights.reshape(tok_count, TOP, 1)
    result = mid_float + jnp.sum(weighted, axis=1)
    return result.astype(jnp.bfloat16).reshape(1, tok_count, model_width)


def solution(mesh):
    placed = (
        P("exp", "seq", None),
        P("exp", "seq", None),
        P("exp", None),
        P(),
        P("exp", "seq", None),
        P("exp", "seq", None),
        P("exp", None, "seq"),
        P("exp", None, "seq"),
        P("exp", "seq", None),
    )
    return jax.shard_map(
        per_device, mesh=mesh, in_specs=placed, out_specs=P("exp", "seq", None), check_vma=False
    )
```

profile of v0, /device:TPU:0, one launch (start us, length us, event | category | flops | bytes accessed | tf_op | source)
XLA Modules:
  0.0 376.1 jit_solution(7040330754941334337)
XLA Ops:
  6.5 0.0 all-gather.2.cloned.1.call-start
  6.5 0.7 all-gather.2.cloned.1.call-update
  7.3 1.9 copy.39
  9.2 0.1 copy.40
  9.3 43.1 %all_to_all.47 = bf16[128,3,4,512]{0,3,1,2:T(8,128)(2,1)S(1)} all-to-all(bf16[128,3,4,512]{0,3,1,2:T(8,128)(2,1)S(1)} %copy.40), channel_id=1, replica_groups=mesh['seq'=4,'exp'=8] {'seq'}, dimensions={2} | all-to-all | bytes 3145728 | tf_op jit(solution)/shard_map/all_to_all | solution.py:46
  52.4 0.7 copy.41
  53.1 0.1 fusion.32
  53.2 0.2 copy.43
  53.4 0.2 copy.46
  53.6 0.2 copy.42
  53.8 3.5 fusion.33
  57.3 0.0 copy-start.3
  57.3 0.0 copy-start.1
  57.3 3.1 fusion.17
  60.5 0.4 copy.49
  60.9 1.0 all_to_all.37
  61.9 3.5 all-to-all-start.1
  65.4 0.0 copy-done.3
  65.4 0.1 copy.51
  65.5 0.1 reshape.85
  65.6 0.1 eq.47
  65.8 0.6 reduce-window.6
  66.4 0.2 slice_reduce_fusion
  66.6 0.1 fusion.28
  66.7 12.3 %all-to-all-done.1 = bf16[4,128,512]{2,1,0:T(8,128)(2,1)S(1)} async-done(((bf16[4,128,512]{2,1,0:T(8,128)(2,1)}), bf16[4,128,512]{2,1,0:T(8,128)(2,1)S(1)}, u32[]{:S(2)}, u32[]{:S(2)}) %all-to-all-start.1) | async-done | bytes 524320 | tf_op jit(solution)/shard_map/all_to_all | solution.py:55
  79.1 0.3 copy.50
  79.3 0.0 all-gather.2.cloned.1.call-done
  79.4 0.0 copy-done.1
  79.4 0.0 copy-start.2
  79.4 4.7 %fusion.11 = bf16[128,2048]{1,0:T(8,128)(2,1)S(1)} fusion(bf16[128,2048]{0,1:T(8,128)(2,1)S(1)} %bitcast.65, bf16[2048,2048]{1,0:T(8,128)(2,1)} %all-gather.2.cloned.1.call-done, bf16[1,128,2048]{2,1,0:T(8,128)(2,1)S(1)} %copy-done.1), kind=kOutput, calls=%fused_computation.16 | convolution fusion | flops 1074528256 | bytes 9961472 | tf_op jit(solution)/shard_map/dot_general | solution.py:56
  84.0 0.2 fusion.18
  84.2 0.0 copy-done.2
  84.3 0.2 fusion.20
  84.5 0.6 broadcast_in_dim.11
  85.1 0.4 reshape.87
  85.5 0.5 convolution_convert_fusion.1
  86.1 0.0 slice-start
  86.1 0.7 broadcast_in_dim.12
  86.7 0.0 slice-start.1
  86.8 119.6 %all_to_all.48 = bf16[32,40,2048]{2,1,0:T(8,128)(2,1)S(1)} all-to-all(bf16[32,40,2048]{2,1,0:T(8,128)(2,1)S(1)} %bitcast.59), channel_id=1, replica_groups=mesh['seq'=4,'exp'=8] {'seq','exp'}, dimensions={0} | all-to-all | bytes 10485760 | tf_op jit(solution)/shard_map/all_to_all | solution.py:90
  206.3 0.0 copy-start
  206.3 2.3 copy-done
  208.6 0.0 slice-done
  208.6 0.0 slice-done.1
  208.6 10.3 %fusion.4 = f32[1280,1408]{1,0:T(8,128)} fusion(bf16[1280,2048]{1,0:T(8,128)(2,1)S(1)} %bitcast.63, bf16[1,2048,1408]{2,1,0:T(8,128)(2,1)S(1)} %bitcast.71), kind=kOutput, calls=%fused_computation.6 | convolution fusion | flops 7381975040 | bytes 18219008 | tf_op jit(solution)/shard_map/dot_general | solution.py:23
  218.9 24.6 %convolution_convert_fusion = bf16[1280,2048]{1,0:T(8,128)(2,1)} fusion(bf16[1,1408,2048]{2,1,0:T(8,128)(2,1)} %param.17, bf16[1280,2048]{1,0:T(8,128)(2,1)} %bitcast.64, f32[1280,1408]{1,0:T(8,128)} %fusion.4, bf16[1,2048,1408]{2,1,0:T(8,128)(2,1)} %param.16), kind=kOutput, calls=%fused_computation.3 | convolution fusion | flops 14777384960 | bytes 29229056 | tf_op jit(solution)/shard_map/dot_general | solution.py:26
  243.5 3.9 %all-to-all-start.3 = ((bf16[32,40,2048]{2,1,0:T(8,128)(2,1)}), bf16[32,40,2048]{2,1,0:T(8,128)(2,1)}, u32[]{:S(2)}, u32[]{:S(2)}) async-start(bf16[32,40,2048]{2,1,0:T(8,128)(2,1)} %bitcast.62), calls=%async_computation.3 | async-start | bytes 10485760 | tf_op jit(solution)/shard_map/all_to_all | solution.py:95
  247.4 0.0 copy-start.4
  247.4 0.1 reduce_sum.53
  247.5 0.1 copy.54
  247.6 116.5 %all-to-all-done.3 = bf16[32,40,2048]{2,1,0:T(8,128)(2,1)} async-done(((bf16[32,40,2048]{2,1,0:T(8,128)(2,1)}), bf16[32,40,2048]{2,1,0:T(8,128)(2,1)}, u32[]{:S(2)}, u32[]{:S(2)}) %all-to-all-start.3) | async-done | bytes 5242912 | tf_op jit(solution)/shard_map/all_to_all | solution.py:95
  364.1 3.5 bitcast_reduce_fusion
  367.6 0.0 copy-done.4
  367.6 0.8 fusion.14
  368.4 0.9 fusion.22
  (7 shorter events, 0.1 us)
Async XLA Ops:
  6.5 72.8 %all-gather.2.cloned.1.call-start = ((), (), s32[]{:S(2)}) async-start(), calls=%async_computation.4 | async-start | bytes 9437184 | tf_op jit(solution)/shard_map/all_gather | solution.py:58
  57.3 8.0 %copy-start.3 = (s32[1,128,2]{1,2,0:T(2,128)S(1)}, s32[1,128,2]{1,2,0:T(2,128)}, u32[]{:S(2)}) copy-start(s32[1,128,2]{1,2,0:T(2,128)} %param.13) | copy-start | bytes 3076
  57.3 22.0 %copy-start.1 = (bf16[1,128,2048]{2,1,0:T(8,128)(2,1)S(1)}, bf16[1,128,2048]{2,1,0:T(8,128)(2,1)}, u32[]{:S(2)}) copy-start(bf16[1,128,2048]{2,1,0:T(8,128)(2,1)} %param.10) | copy-start | bytes 1572868
  61.9 17.2 %all-to-all-start.1 = ((bf16[4,128,512]{2,1,0:T(8,128)(2,1)}), bf16[4,128,512]{2,1,0:T(8,128)(2,1)S(1)}, u32[]{:S(2)}, u32[]{:S(2)}) async-start(bf16[4,128,512]{2,1,0:T(8,128)(2,1)} %all_to_all.37), calls=%async_computation.1 | async-start | bytes 1048576 | tf_op jit(solution)/shard_map/all_to_all | solution.py:55
  79.4 4.9 %copy-start.2 = (f32[2048]{0:T(1024)S(1)}, f32[2048]{0:T(1024)}, u32[]{:S(2)}) copy-start(f32[2048]{0:T(1024)} %param.12) | copy-start | bytes 24580
  86.1 122.6 %slice-start = ((s8[5767168]{0:T(1024)(128)(4,1)}), s8[1572864]{0:T(1024)(128)(4,1)S(1)}, s32[]{:S(2)}) async-start(s8[5767168]{0:T(1024)(128)(4,1)} %bitcast.70), calls=%async_computation.5 | async-start | bytes 3145728
  86.7 121.9 %slice-start.1 = ((s8[5767168]{0:T(1024)(128)(4,1)}), s8[4194304]{0:T(1024)(128)(4,1)S(1)}, s32[]{:S(2)}) async-start(s8[5767168]{0:T(1024)(128)(4,1)} %bitcast.70), calls=%async_computation.6 | async-start | bytes 8388608
  206.3 2.3 copy-start
  243.5 120.6 %all-to-all-start.3 = ((bf16[32,40,2048]{2,1,0:T(8,128)(2,1)}), bf16[32,40,2048]{2,1,0:T(8,128)(2,1)}, u32[]{:S(2)}, u32[]{:S(2)}) async-start(bf16[32,40,2048]{2,1,0:T(8,128)(2,1)} %bitcast.62), calls=%async_computation.3 | async-start | bytes 10485760 | tf_op jit(solution)/shard_map/all_to_all | solution.py:95
  247.4 120.2 %copy-start.4 = (f32[1,128,2]{1,2,0:T(2,128)S(1)}, f32[1,128,2]{1,2,0:T(2,128)}, u32[]{:S(2)}) copy-start(f32[1,128,2]{1,2,0:T(2,128)} %param.14) | copy-start | bytes 3076
Sparse Core Ops, SparseCore 0:
  9.2 57.0 all-gather.1
where the time goes:
time: 376 us
  blocking collectives  163 us (43%)
  waiting for transfers between devices  130 us (35%)
  matrix products  47.4 us (13%)
  between operations  13.6 us (4%)
  local copies, waits for them, and re-layouts  9.96 us (3%)
  starting transfers between devices  7.34 us (2%)
  other arithmetic  5.49 us (1%)
    all_to_all x1, blocking collectives, per_device(): lax.all_to_all(copies, ('seq', 'exp'), split_axis=0, concat_axis=0, tiled...  120 us
    all_to_all x1, waiting for transfers between devices, per_device(): lax.all_to_all(partial_value, ('seq', 'exp'), split_axis=0, concat_axis=0...  117 us
    all_to_all x1, blocking collectives, per_device(): lax.all_to_all(laid, 'seq', split_axis=2, concat_axis=0, tiled=True)  43.1 us
    dot_general x1, matrix products, expert_rows_apply(): return jnp.dot(hidden, down_mat, preferred_element_type=jnp.float32)  24.6 us
    all_to_all x1, waiting for transfers between devices, per_device(): lax.all_to_all(attended, 'seq', split_axis=0, concat_axis=1, tiled=True)  12.3 us
    dot_general x1, matrix products, expert_rows_apply(): gate_val = jnp.dot(tok_rows, gate_mat, preferred_element_type=jnp.float32)  10.3 us
  transfers between devices with their start and end apart: 3, of which 2 were waited for; matrix products, arithmetic and copies ran while one was open for 3% of the time, Pallas kernels for 0%

commit v1 on v0

v1 whole, which is shorter than its diff:
```python
import functools

import jax
import jax.numpy as jnp
from jax import lax
from jax.experimental import pallas as pl
from jax.experimental.pallas import tpu as pltpu
from jax.sharding import PartitionSpec as P

HEADS = 16
HEAD_DIM = 128
TOP = 2
TRADES = 8
AHEAD = 2
HID_TILE = 512
OUT_TILE = 1024
VMEM_LIMIT = 16 * 1024 * 1024
ANY = pl.BlockSpec(memory_space=pl.ANY)


def xor_pairs(count, offset):
    return [(i, i ^ offset) for i in range(count)]


def whole(shape):
    return pl.BlockSpec(shape, lambda *_: (0,) * len(shape))


def params():
    return pltpu.CompilerParams(vmem_limit_bytes=VMEM_LIMIT)


def cost(flops, bytes_accessed, transcendentals):
    return pl.CostEstimate(
        flops=0 * flops, bytes_accessed=0 * bytes_accessed, transcendentals=0 * transcendentals
    )


def after(arrays, deps):
    count = len(arrays)
    return pl.pallas_call(
        lambda *_: None,
        in_specs=[ANY] * (count + len(deps)),
        out_specs=[ANY] * count,
        out_shape=[jax.ShapeDtypeStruct(a.shape, a.dtype) for a in arrays],
        input_output_aliases={i: i for i in range(count)},
        compiler_params=pltpu.CompilerParams(vmem_limit_bytes=1024 * 1024),
        cost_estimate=cost(0, 0, 0),
        name="after",
    )(*arrays, *deps)


def attend_kernel(count, *refs):
    parts, outs = refs[: 3 * count], refs[3 * count :]
    block = outs[0].shape[0]
    query, key, value = (
        jnp.concatenate([p[...] for p in parts[w * count : (w + 1) * count]], axis=0)
        for w in range(3)
    )
    scores = lax.dot_general(
        query, key, (((1,), (1,)), ((), ())), preferred_element_type=jnp.float32
    ) * HEAD_DIM ** (-0.5)
    top = jnp.max(scores, axis=-1, keepdims=True)
    grown = jnp.exp(scores - top)
    probs = (grown / jnp.sum(grown, axis=-1, keepdims=True)).astype(jnp.bfloat16)
    mixed = jnp.dot(probs, value, preferred_element_type=jnp.float32).astype(jnp.bfloat16)
    for i in range(count):
        outs[i][...] = mixed[i * block : (i + 1) * block]


def attend(blocks, head_local):
    count = len(blocks)
    tok = blocks[0].shape[0]
    clip_len = count * tok

    def part(which):
        return pl.BlockSpec((tok, HEAD_DIM), lambda h: (0, which * head_local + h))

    return pl.pallas_call(
        functools.partial(attend_kernel, count),
        grid=(head_local,),
        in_specs=[part(which) for which in range(3) for _ in range(count)],
        out_specs=[pl.BlockSpec((tok, HEAD_DIM), lambda h: (0, h))] * count,
        out_shape=[jax.ShapeDtypeStruct((tok, head_local * HEAD_DIM), jnp.bfloat16)] * count,
        compiler_params=params(),
        cost_estimate=cost(
            4 * head_local * clip_len * clip_len * HEAD_DIM,
            8 * clip_len * head_local * HEAD_DIM,
            head_local * clip_len * clip_len,
        ),
        name="attend",
    )(*(list(blocks) * 3))


def project_kernel(count, seq_ref, *refs):
    parts = refs[:count]
    weight_ref, res_ref, gain_ref, mid_ref, norm_ref, acc_ref = refs[count:]
    step = pl.program_id(0)
    for i in range(count):

        @pl.when(step == i)
        def _(i=i):
            term = jnp.dot(parts[i][...], weight_ref[...], preferred_element_type=jnp.float32)
            acc_ref[...] = (res_ref[...].astype(jnp.float32) if i == 0 else acc_ref[...]) + term

    @pl.when(step == count - 1)
    def _():
        middle = acc_ref[...].astype(jnp.bfloat16)
        mid_ref[...] = middle
        mid_float = middle.astype(jnp.float32)
        mean = jnp.mean(mid_float * mid_float, axis=-1, keepdims=True)
        norm_ref[...] = (mid_float * lax.rsqrt(mean + 1e-06) * gain_ref[...]).astype(
            jnp.bfloat16
        )


def project(my_seq, parts, weight, residual, gain):
    count = len(parts)
    tok, depth = parts[0].shape
    width = weight.shape[1]
    out = jax.ShapeDtypeStruct((tok, width), jnp.bfloat16)
    return pl.pallas_call(
        functools.partial(project_kernel, count),
        grid_spec=pltpu.PrefetchScalarGridSpec(
            num_scalar_prefetch=1,
            grid=(count,),
            in_specs=[whole((tok, depth))] * count
            + [
                pl.BlockSpec((depth, width), lambda k, seq: (seq[0] ^ k, 0)),
                whole((tok, width)),
                whole((1, width)),
            ],
            out_specs=[whole((tok, width))] * 2,
            scratch_shapes=[pltpu.VMEM((tok, width), jnp.float32)],
        ),
        out_shape=[out, out],
        compiler_params=params(),
        cost_estimate=cost(2 * tok * count * depth * width, 2 * count * depth * width, 0),
        name="project",
    )(my_seq.reshape(1), *parts, weight, residual, gain.reshape(1, width))


def slot_kernel(hop, chips, place_ref, mine_ref, *rest):
    outs = rest[-chips:]
    piece = outs[0].shape[0]
    place = place_ref[hop]
    row = lax.broadcasted_iota(jnp.int32, (chips * piece, place.shape[-1]), 0)
    others = rest[:TRADES]
    halves = []
    for which in range(2):
        hit = (row == place[2 * which : 2 * which + 1]) | (
            row == place[2 * which + 1 : 2 * which + 2]
        )
        halves.append(jnp.where(hit, 1.0, 0.0).astype(jnp.bfloat16))
    slotted = jnp.dot(
        jnp.concatenate(halves, axis=1),
        jnp.concatenate([mine_ref[...]] + [o[...] for o in others], axis=0),
        preferred_element_type=jnp.float32,
    ).astype(jnp.bfloat16)
    for step in range(chips):
        outs[step][...] = slotted[step * piece : (step + 1) * piece]


def to_slots(hop, chips, piece, place, mine, others, deps):
    tok, width = mine.shape
    return pl.pallas_call(
        functools.partial(slot_kernel, hop, chips),
        in_specs=[whole(place.shape), whole(mine.shape)]
        + [whole(o.shape) for o in others]
        + [ANY] * len(deps),
        out_specs=[whole((piece, width))] * chips,
        out_shape=[jax.ShapeDtypeStruct((piece, width), jnp.bfloat16)] * chips,
        compiler_params=params(),
        cost_estimate=cost(4 * chips * piece * tok * width, 2 * width * (2 * tok + chips * piece), 0),
        name=f"slots{hop}",
    )(place, mine, *others, *deps)


def expert_kernel(chips, n_deps, *refs):
    pieces = refs[:chips]
    gate_hbm, up_hbm, down_hbm = refs[chips : chips + 3]
    outs = refs[chips + 3 + n_deps : 2 * chips + 3 + n_deps]
    rows_ref, hid_ref, gate_ref, up_ref, down_ref, sem = refs[-6:]
    piece = pieces[0].shape[0]
    hid, width = down_ref.shape
    hid_tiles = [slice(at, min(at + HID_TILE, hid)) for at in range(0, hid, HID_TILE)]
    out_tiles = [slice(at, at + OUT_TILE) for at in range(0, width, OUT_TILE)]
    stages = [[(gate_hbm, gate_ref, t), (up_hbm, up_ref, t)] for t in hid_tiles]
    stages += [[(down_hbm, down_ref, t)] for t in out_tiles]
    copies, count = [], 0
    for stage in stages:
        group = []
        for source, target, tile in stage:
            group.append(
                pltpu.make_async_copy(source.at[:, tile], target.at[:, tile], sem.at[count])
            )
            count += 1
        copies.append(group)

    def start(n):
        if n < len(copies):
            for copy in copies[n]:
                copy.start()

    def wait(n):
        for copy in copies[n]:
            copy.wait()
        start(n + AHEAD)

    for n in range(AHEAD):
        start(n)
    for i in range(chips):
        rows_ref[i * piece : (i + 1) * piece, :] = pieces[i][...]
    for n, tile in enumerate(hid_tiles):
        wait(n)
        gate_val = jnp.dot(rows_ref[...], gate_ref[:, tile], preferred_element_type=jnp.float32)
        up_val = jnp.dot(rows_ref[...], up_ref[:, tile], preferred_element_type=jnp.float32)
        hidden = gate_val / (1.0 + jnp.exp(-gate_val)) * up_val
        hid_ref[:, tile] = hidden.astype(jnp.bfloat16)
    for n, tile in enumerate(out_tiles):
        wait(len(hid_tiles) + n)
        out = jnp.dot(hid_ref[...], down_ref[:, tile], preferred_element_type=jnp.float32)
        out = out.astype(jnp.bfloat16)
        for i in range(chips):
            outs[i][:, tile] = out[i * piece : (i + 1) * piece]


def expert(hop, pieces, gate_mat, up_mat, down_mat, deps):
    chips = len(pieces)
    piece, width = pieces[0].shape
    hid = gate_mat.shape[-1]
    rows = chips * piece
    in_vmem = pl.BlockSpec(memory_space=pltpu.VMEM)
    in_hbm = pl.BlockSpec(memory_space=pltpu.HBM)
    n_sems = 2 * -(-hid // HID_TILE) + width // OUT_TILE
    return pl.pallas_call(
        functools.partial(expert_kernel, chips, len(deps)),
        in_specs=[in_vmem] * chips + [in_hbm] * 3 + [ANY] * len(deps),
        out_specs=[in_vmem] * chips,
        out_shape=[jax.ShapeDtypeStruct((piece, width), jnp.bfloat16)] * chips,
        scratch_shapes=[
            pltpu.VMEM((rows, width), jnp.bfloat16),
            pltpu.VMEM((rows, hid), jnp.bfloat16),
            pltpu.VMEM((width, hid), jnp.bfloat16),
            pltpu.VMEM((width, hid), jnp.bfloat16),
            pltpu.VMEM((hid, width), jnp.bfloat16),
            pltpu.SemaphoreType.DMA((n_sems,)),
        ],
        compiler_params=pltpu.CompilerParams(vmem_limit_bytes=56 * 1024 * 1024),
        cost_estimate=cost(6 * rows * width * hid, 6 * width * hid, rows * hid),
        name=f"expert{hop}",
    )(*pieces, gate_mat, up_mat, down_mat, *deps)


def combine_kernel(hop, chips, n_deps, place_ref, gates_ref, *refs):
    pieces = refs[:chips]
    mine_ref, other_ref = refs[chips + n_deps :]
    rows = jnp.concatenate([p[...] for p in pieces], axis=0)
    place = place_ref[hop]
    gates = gates_ref[hop]
    column = lax.broadcasted_iota(jnp.int32, (place.shape[0], rows.shape[0]), 1)
    for which, out_ref in ((0, mine_ref), (1, other_ref)):
        total = 0.0
        for choice in range(TOP):
            at = 2 * which + choice
            picking = jnp.where(column == place[:, at : at + 1], 1.0, 0.0).astype(jnp.bfloat16)
            picked = jnp.dot(picking, rows, preferred_element_type=jnp.float32)
            total = total + picked * gates[:, at : at + 1]
        out_ref[...] = total.astype(out_ref.dtype)


def combine(hop, pieces, place, gates, deps):
    chips = len(pieces)
    piece, width = pieces[0].shape
    tok = place.shape[1]
    tile = pl.BlockSpec((tok, OUT_TILE), lambda i: (0, i))
    return pl.pallas_call(
        functools.partial(combine_kernel, hop, chips, len(deps)),
        grid=(width // OUT_TILE,),
        in_specs=[whole(place.shape), whole(gates.shape)]
        + [pl.BlockSpec((piece, OUT_TILE), lambda i: (0, i))] * chips
        + [ANY] * len(deps),
        out_specs=[tile, tile],
        out_shape=[
            jax.ShapeDtypeStruct((tok, width), jnp.float32),
            jax.ShapeDtypeStruct((tok, width), jnp.bfloat16),
        ],
        compiler_params=params(),
        cost_estimate=cost(8 * tok * chips * piece * width, 2 * width * (chips * piece + 3 * tok), 0),
        name=f"combine{hop}",
    )(place, gates, *pieces, *deps)


def per_device(
    attn_inputs,
    residual,
    out_weight,
    norm_gain,
    expert_ids,
    gate_weights,
    gate_weight,
    up_weight,
    down_weight,
):
    tok_count = attn_inputs.shape[1]
    seq_count = lax.axis_size("seq")
    expert_count = lax.axis_size("exp")
    chips = expert_count // 2
    my_seq = lax.axis_index("seq")
    my_exp = lax.axis_index("exp")
    my_core, my_chip = my_exp % 2, my_exp // 2
    model_width = residual.shape[-1]
    head_local = HEADS // seq_count
    capacity = 5 * tok_count // (2 * expert_count)
    piece = -(-2 * capacity // 16) * 16

    def over_seq(value, hop):
        return lax.ppermute(value, "seq", xor_pairs(seq_count, hop))

    def over_chips(value, step):
        return lax.ppermute(value, "exp", xor_pairs(expert_count, 2 * step))

    def over_cores(value):
        return lax.ppermute(value, "exp", xor_pairs(expert_count, 1))

    gate_mat, up_mat, down_mat = gate_weight[0], up_weight[0], down_weight[0]

    def trade(value):
        part = value.shape[0] // TRADES
        return [over_cores(value[i * part : (i + 1) * part]) for i in range(TRADES)]

    head_cols = head_local * HEAD_DIM
    laid = attn_inputs.reshape(tok_count, 3, seq_count, head_cols)
    blocks = []
    for hop in range(seq_count):
        part = lax.dynamic_index_in_dim(laid, my_seq ^ hop, 2, keepdims=False)
        part = part.reshape(tok_count, 3 * head_cols)
        blocks.append(over_seq(part, hop) if hop else part)
    attended = attend(blocks, head_local)
    merged = [over_seq(p, hop) if hop else p for hop, p in enumerate(attended)]

    route_ids = expert_ids.reshape(tok_count * TOP)
    one_hot = (
        route_ids[:, None] == jnp.arange(expert_count, dtype=jnp.int32)[None, :]
    ).astype(jnp.int32)
    before = jnp.cumsum(one_hot, axis=0) - one_hot
    slot_ids = jnp.sum(before * one_hot, axis=-1)
    target = (route_ids * capacity + slot_ids).reshape(tok_count, TOP)
    route = jnp.concatenate([target.astype(jnp.float32), gate_weights[0]], axis=1).T
    route = jnp.stack([route] + [over_seq(route, hop) for hop in range(1, seq_count)])
    both = jnp.concatenate([route, over_cores(route)], axis=1)
    goal = jnp.concatenate([both[:, :TOP], both[:, 2 * TOP : 3 * TOP]], axis=1).astype(jnp.int32)
    gates = jnp.concatenate([both[:, TOP : 2 * TOP], both[:, 3 * TOP :]], axis=1)
    goal_exp = goal // capacity
    clip = (jnp.arange(2 * TOP, dtype=jnp.int32) // TOP)[None, :, None]
    place = jnp.where(
        goal_exp % 2 == my_core,
        ((goal_exp // 2) ^ my_chip) * piece + clip * capacity + goal % capacity,
        -1,
    )
    place_t = place.transpose(0, 2, 1)
    gates_t = gates.transpose(0, 2, 1)

    all_weight = lax.all_gather(out_weight, "exp", axis=0, tiled=True)
    middle, normed = project(
        my_seq, merged, all_weight, residual.reshape(tok_count, model_width), norm_gain
    )
    mid_float = middle.astype(jnp.float32)

    def dispatch(hop, block, deps):
        pieces = to_slots(hop, chips, piece, place, block, trade(block), deps)
        return [over_chips(p, s) if s else p for s, p in enumerate(pieces)], pieces[0]

    def run(hop, deps):
        return expert(hop, arrived[hop], gate_mat, up_mat, down_mat, deps)

    def give_back(hop, partial, after_deps, deps):
        if after_deps:
            partial = after(partial, after_deps)
        returned = [over_chips(p, s) if s else p for s, p in enumerate(partial)]
        mine, other = combine(hop, returned, place_t, gates_t, deps)
        total = mine + over_cores(other).astype(jnp.float32)
        if hop == 0:
            return total, mine
        total = total.astype(jnp.bfloat16)
        half = tok_count // 2
        return [over_seq(total[:half], hop), over_seq(total[half:], hop)], total

    arrived = {}
    arrived[0], own0 = dispatch(0, normed, [])
    (normed_out,) = after([normed], [own0])
    blocks = [normed] + [over_seq(normed_out, hop) for hop in range(1, seq_count)]
    arrived[1], own1 = dispatch(1, blocks[1], arrived[0])
    done0 = run(0, [own1])
    arrived[2], own2 = dispatch(2, blocks[2], arrived[1] + [done0[0]])
    done1 = run(1, [own2])
    arrived[3], own3 = dispatch(3, blocks[3], arrived[2] + [done1[0]])
    done2 = run(2, [own3])
    done3 = run(3, [done2[0]])
    back2, mark2 = give_back(2, done2, [], [done3[0]])
    back3, mark3 = give_back(3, done3, [], [mark2, back2[0]])
    back1, mark1 = give_back(1, done1, [mark2], [mark3, back2[1], back3[0]])
    back0, _ = give_back(0, done0, [mark3], [mark1, back3[1]])
    result = mid_float + back0
    for back in (back1, back2, back3):
        result = result + jnp.concatenate(back, axis=0).astype(jnp.float32)
    return result.astype(jnp.bfloat16).reshape(1, tok_count, model_width)


def solution(mesh):
    placed = (
        P("exp", "seq", None),
        P("exp", "seq", None),
        P("exp", None),
        P(),
        P("exp", "seq", None),
        P("exp", "seq", None),
        P("exp", None, "seq"),
        P("exp", None, "seq"),
        P("exp", "seq", None),
    )
    return jax.shard_map(
        per_device, mesh=mesh, in_specs=placed, out_specs=P("exp", "seq", None), check_vma=False
    )
```

time: 376 us -> 290 us (0.77)
  blocking collectives: 163 us -> 0 us
  starting transfers between devices: 7.34 us -> 71.5 us
  Pallas kernels: 0 us -> 62.5 us
  matrix products: 47.4 us -> 0 us
  waiting for transfers between devices: 130 us -> 120 us
  local copies, waits for them, and re-layouts: 9.96 us -> 17.6 us
    all_to_all x2 -> x0, blocking collectives: 163 us -> none  [the longest x1 120 us: per_device(): lax.all_to_all(copies, ('seq', 'exp'), split_axis=0, concat_axis=0, tiled...]
    all_to_all x2 -> x0, waiting for transfers between devices: 129 us -> none  [the longest x1 117 us: per_device(): lax.all_to_all(partial_value, ('seq', 'exp'), split_axis=0, concat_axis=0...]
    ppermute x0 -> x79, waiting for transfers between devices: none -> 120 us  [the longest x18 92.5 us: over_seq(): return lax.ppermute(value, 'seq', xor_pairs(seq_count, hop))]
    ppermute x0 -> x79, starting transfers between devices: none -> 71.4 us  [the longest x18 35.1 us: over_seq(): return lax.ppermute(value, 'seq', xor_pairs(seq_count, hop))]
    pallas_call x0 -> x17, Pallas kernels: none -> 62.5 us  [the longest x4 46.5 us: expert(): pl.pallas_call(functools.partial(expert_kernel, chips, len(deps)), in_spe...]
    dot_general x6 -> x0, matrix products: 44 us -> none  [the longest x1 24.6 us: expert_rows_apply(): return jnp.dot(hidden, down_mat, preferred_element_type=jnp.float32)]
    unnamed x16 -> x64, local copies, waits for them, and re-layouts: 4.33 us -> 11.8 us
    all_to_all x2 -> x0, starting transfers between devices: 7.34 us -> none  [the longest x1 3.87 us: per_device(): lax.all_to_all(partial_value, ('seq', 'exp'), split_axis=0, concat_axis=0...]
  transfers between devices with their start and end apart: 3 -> 80, of which waited for: 2 -> 25; matrix products, arithmetic and copies ran while one was open for 3% -> 4% of each run, Pallas kernels for 0% -> 18%
where the time goes in v1:
time: 290 us
  waiting for transfers between devices  120 us (41%)
  starting transfers between devices  71.5 us (25%)
  Pallas kernels  62.5 us (22%)
  local copies, waits for them, and re-layouts  17.6 us (6%)
  between operations  14.4 us (5%)
  other arithmetic  3.55 us (1%)
    ppermute x18, waiting for transfers between devices, over_seq(): return lax.ppermute(value, 'seq', xor_pairs(seq_count, hop))  92.5 us
    pallas_call x4, Pallas kernels, expert(): pl.pallas_call(functools.partial(expert_kernel, chips, len(deps)), in_spe...  46.5 us
    ppermute x18, starting transfers between devices, over_seq(): return lax.ppermute(value, 'seq', xor_pairs(seq_count, hop))  35.1 us
    ppermute x24, starting transfers between devices, over_chips(): return lax.ppermute(value, 'exp', xor_pairs(expert_count, 2 * step))  28.2 us
    ppermute x24, waiting for transfers between devices, over_chips(): return lax.ppermute(value, 'exp', xor_pairs(expert_count, 2 * step))  20.9 us
    unnamed x64, local copies, waits for them, and re-layouts  11.8 us
    ppermute x37, starting transfers between devices, over_cores(): return lax.ppermute(value, 'exp', xor_pairs(expert_count, 1))  8.2 us
    pallas_call x4, Pallas kernels, combine(): pl.pallas_call(functools.partial(combine_kernel, hop, chips, len(deps)),...  7.07 us
  transfers between devices with their start and end apart: 80, of which 25 were waited for; matrix products, arithmetic and copies ran while one was open for 4% of the time, Pallas kernels for 18%

profile of v1, /device:TPU:0, one launch (start us, length us, event | category | flops | bytes accessed | tf_op | source)
XLA Modules:
  0.0 289.9 jit_solution(17943028288668759959)
XLA Ops:
  10.2 3.0 %collective-permute-start.6 = (f32[4,128]{1,0:T(4,128)S(1)}, f32[4,128]{1,0:T(4,128)S(1)}, u32[]{:S(2)}, u32[]{:S(2)}) collective-permute-start(f32[4,128]{1,0:T(4,128)S(1)} %get-tuple-element.162), channel_id=1, source_target_pairs={{0,8},{8,0},{16,24},{24,16},{1,9},{9,1},{17,25},{25,17},{2,10},{10... | collective-permute-start | bytes 6152 | tf_op jit(solution)/shard_map/ppermute | solution.py:318
  13.2 2.6 collective-permute-start.7
  15.8 1.9 copy.75
  18.6 2.0 copy.76
  21.5 0.9 copy.77
  22.5 3.5 %collective-permute-start.1 = (bf16[128,1536]{1,0:T(8,128)(2,1)}, bf16[128,1536]{1,0:T(8,128)(2,1)S(1)}, u32[]{:S(2)}, u32[]{:S(2)}) collective-permute-start(bf16[128,1536]{1,0:T(8,128)(2,1)} %copy.77), channel_id=1, source_target_pairs={{0,16},{8,24},{16,0},{24,8},{1,17},{9,25},{17,1},{25,9},{2,18},{10... | collective-permute-start | bytes 1179656 | tf_op jit(solution)/shard_map/ppermute | solution.py:318
  26.6 11.4 %collective-permute-done.refs_1_.refs_5_.refs_9_ = bf16[128,1536]{1,0:T(8,128)(2,1)S(1)} collective-permute-done((bf16[128,1536]{1,0:T(8,128)(2,1)}, bf16[128,1536]{1,0:T(8,128)(2,1)S(1)}, u32[]{:S(2)}, u32[]{:S(2)}) %collective-permute-start) | collective-permute-done | bytes 393248 | tf_op jit(solution)/shard_map/ppermute | solution.py:318
  38.0 15.1 %collective-permute-done.1.refs_2_.refs_6_.refs_10_ = bf16[128,1536]{1,0:T(8,128)(2,1)S(1)} collective-permute-done((bf16[128,1536]{1,0:T(8,128)(2,1)}, bf16[128,1536]{1,0:T(8,128)(2,1)S(1)}, u32[]{:S(2)}, u32[]{:S(2)}) %collective-permute-start.1) | collective-permute-done | bytes 393248 | tf_op jit(solution)/shard_map/ppermute | solution.py:318
  53.1 4.5 %attend.1 = (bf16[128,512]{1,0:T(8,128)(2,1)S(1)}, bf16[128,512]{1,0:T(8,128)(2,1)S(1)}, bf16[128,512]{1,0:T(8,128)(2,1)S(1)}, bf16[128,512]{1,0:T(8,128)(2,1)S(1)}) custom-call(bf16[128,1536]{1,0:T(8,128)(2,1)S(1)} %copy.79.refs_0_.refs_4_.refs_8_, bf16[128,1536]{1,0:T(8,128)(2,1)S(1)} %collective-permute-done.refs_1_.refs_5_.refs_9_, ...), custom_call_target="tpu_custom_call" | custom-call | tf_op jit(solution)/shard_map/attend/pallas_call | solution.py:79
  57.5 7.0 %collective-permute-start.3 = (bf16[128,512]{1,0:T(8,128)(2,1)S(1)}, bf16[128,512]{1,0:T(8,128)(2,1)S(1)}, u32[]{:S(2)}, u32[]{:S(2)}) collective-permute-start(bf16[128,512]{1,0:T(8,128)(2,1)S(1)} %get-tuple-element.60), channel_id=1, source_target_pairs={{0,8},{8,0},{16,24},{24,16},{1,9},{9,1},{17,25},{25,17},{2,10},{10... | collective-permute-start | bytes 393224 | tf_op jit(solution)/shard_map/ppermute | solution.py:318
  64.6 1.0 collective-permute-start.4
  65.6 1.5 collective-permute-start.5
  67.2 1.4 collective-permute-done.3.refs_1_
  68.6 7.2 %collective-permute-done.4.refs_2_ = bf16[128,512]{1,0:T(8,128)(2,1)S(1)} collective-permute-done((bf16[128,512]{1,0:T(8,128)(2,1)S(1)}, bf16[128,512]{1,0:T(8,128)(2,1)S(1)}, u32[]{:S(2)}, u32[]{:S(2)}) %collective-permute-start.4) | collective-permute-done | bytes 131104 | tf_op jit(solution)/shard_map/ppermute | solution.py:318
  75.9 3.4 %copy-done = bf16[2048,2048]{1,0:T(8,128)(2,1)S(1)} copy-done((bf16[2048,2048]{1,0:T(8,128)(2,1)S(1)}, bf16[2048,2048]{1,0:T(8,128)(2,1)}, u32[]{:S(2)}) %copy-start) | copy-done | bytes 8388632
  79.2 2.5 project.1
  85.7 2.0 collective-permute-start.21
  87.7 1.0 collective-permute-start.39
  88.7 1.5 collective-permute-start.18
  90.2 1.5 collective-permute-start.19
  92.2 19.0 %collective-permute-done.21.mine_ref = bf16[128,2048]{1,0:T(8,128)(2,1)S(1)} collective-permute-done((bf16[128,2048]{1,0:T(8,128)(2,1)S(1)}, bf16[128,2048]{1,0:T(8,128)(2,1)S(1)}, u32[]{:S(2)}, u32[]{:S(2)}) %collective-permute-start.21) | collective-permute-done | bytes 524320 | tf_op jit(solution)/shard_map/ppermute | solution.py:318
  112.3 1.5 collective-permute-done.39.mine_ref
  113.8 2.4 collective-permute-start.30
  119.7 1.5 collective-permute-start.48
  121.2 1.5 collective-permute-start.49
  123.2 1.3 collective-permute-done.44.rest_4_
  124.7 1.1 collective-permute-done.45.rest_5_
  125.9 1.1 collective-permute-done.46.rest_6_
  127.2 11.6 %expert0.1 = (bf16[80,2048]{1,0:T(8,128)(2,1)}, bf16[80,2048]{1,0:T(8,128)(2,1)}, bf16[80,2048]{1,0:T(8,128)(2,1)}, bf16[80,2048]{1,0:T(8,128)(2,1)}) custom-call(bf16[80,2048]{1,0:T(8,128)(2,1)} %copy-done.5, bf16[80,2048]{1,0:T(8,128)(2,1)} %copy-done.11, bf16[80,2048]{1,0:T(8,128)(2,1)} %copy-done.12, bf16[80,2048]{1,0:T(8,128)(2,1)} %copy-done.13, ...), custom_call_target="tpu_custom_call" | custom-call | tf_op jit(solution)/shard_map/expert0/pallas_call | solution.py:236
  138.8 1.2 copy-done.1
  141.3 1.5 collective-permute-start.51
  142.8 1.5 collective-permute-start.52
  149.2 11.8 %expert1.1 = (bf16[80,2048]{1,0:T(8,128)(2,1)}, bf16[80,2048]{1,0:T(8,128)(2,1)}, bf16[80,2048]{1,0:T(8,128)(2,1)}, bf16[80,2048]{1,0:T(8,128)(2,1)}) custom-call(bf16[80,2048]{1,0:T(8,128)(2,1)} %copy-done.6, bf16[80,2048]{1,0:T(8,128)(2,1)} %copy-done.14, bf16[80,2048]{1,0:T(8,128)(2,1)} %copy-done.15, bf16[80,2048]{1,0:T(8,128)(2,1)} %copy-done.16, ...), custom_call_target="tpu_custom_call" | custom-call | tf_op jit(solution)/shard_map/expert1/pallas_call | solution.py:236
  161.1 1.2 copy-done.3
  163.6 1.5 collective-permute-start.54
  165.0 1.5 collective-permute-start.55
  167.1 11.5 %expert2.1 = (bf16[80,2048]{1,0:T(8,128)(2,1)}, bf16[80,2048]{1,0:T(8,128)(2,1)}, bf16[80,2048]{1,0:T(8,128)(2,1)}, bf16[80,2048]{1,0:T(8,128)(2,1)}) custom-call(bf16[80,2048]{1,0:T(8,128)(2,1)} %copy-done.8, bf16[80,2048]{1,0:T(8,128)(2,1)} %copy-done.17, bf16[80,2048]{1,0:T(8,128)(2,1)} %copy-done.18, bf16[80,2048]{1,0:T(8,128)(2,1)} %copy-done.19, ...), custom_call_target="tpu_custom_call" | custom-call | tf_op jit(solution)/shard_map/expert2/pallas_call | solution.py:236
  178.6 1.5 collective-permute-start.60
  180.1 1.5 collective-permute-start.61
  182.4 11.6 %expert3.1 = (bf16[80,2048]{1,0:T(8,128)(2,1)}, bf16[80,2048]{1,0:T(8,128)(2,1)}, bf16[80,2048]{1,0:T(8,128)(2,1)}, bf16[80,2048]{1,0:T(8,128)(2,1)}) custom-call(bf16[80,2048]{1,0:T(8,128)(2,1)} %copy-done.21, bf16[80,2048]{1,0:T(8,128)(2,1)} %copy-done.30, bf16[80,2048]{1,0:T(8,128)(2,1)} %collective-permute-done.55.refs_2_, ...), custom_call_target="tpu_custom_call" | custom-call | tf_op jit(solution)/shard_map/expert3/pallas_call | solution.py:236
  194.1 2.0 collective-permute-done.61.refs_2_
  196.0 1.0 copy-done.10
  197.0 1.8 combine2.1
  198.9 1.3 collective-permute-start.57
  201.0 1.4 collective-permute-start.59
  202.7 7.0 %collective-permute-done.57.refs_1_ = bf16[80,2048]{1,0:T(8,128)(2,1)S(1)} collective-permute-done((bf16[80,2048]{1,0:T(8,128)(2,1)}, bf16[80,2048]{1,0:T(8,128)(2,1)S(1)}, u32[]{:S(2)}, u32[]{:S(2)}) %collective-permute-start.57) | collective-permute-done | bytes 327712 | tf_op jit(solution)/shard_map/ppermute | solution.py:321
  209.6 6.0 %collective-permute-done.58.refs_2_ = bf16[80,2048]{1,0:T(8,128)(2,1)S(1)} collective-permute-done((bf16[80,2048]{1,0:T(8,128)(2,1)}, bf16[80,2048]{1,0:T(8,128)(2,1)S(1)}, u32[]{:S(2)}, u32[]{:S(2)}) %collective-permute-start.58) | collective-permute-done | bytes 327712 | tf_op jit(solution)/shard_map/ppermute | solution.py:321
  215.7 1.5 collective-permute-done.59.refs_3_
  217.2 1.8 combine3.1
  219.9 1.5 collective-permute-start.70
  221.5 1.2 collective-permute-start.71
  222.8 1.5 collective-permute-start.73
  224.3 17.2 %collective-permute-done.72.refs_5_ = bf16[64,2048]{1,0:T(8,128)(2,1)S(1)} collective-permute-done((bf16[64,2048]{1,0:T(8,128)(2,1)S(1)}, bf16[64,2048]{1,0:T(8,128)(2,1)S(1)}, u32[]{:S(2)}, u32[]{:S(2)}) %collective-permute-start.72) | collective-permute-done | bytes 262176 | tf_op jit(solution)/shard_map/ppermute | solution.py:318
  241.5 1.8 combine1.1
  244.3 1.5 collective-permute-start.67
  245.8 1.2 collective-permute-start.68
  247.0 2.4 collective-permute-start.75
  249.5 7.3 %collective-permute-done.75.refs_5_ = bf16[64,2048]{1,0:T(8,128)(2,1)S(1)} collective-permute-done((bf16[64,2048]{1,0:T(8,128)(2,1)S(1)}, bf16[64,2048]{1,0:T(8,128)(2,1)S(1)}, u32[]{:S(2)}, u32[]{:S(2)}) %collective-permute-start.75) | collective-permute-done | bytes 262176 | tf_op jit(solution)/shard_map/ppermute | solution.py:318
  256.8 3.5 %collective-permute-done.67.refs_2_ = bf16[80,2048]{1,0:T(8,128)(2,1)S(1)} collective-permute-done((bf16[80,2048]{1,0:T(8,128)(2,1)S(1)}, bf16[80,2048]{1,0:T(8,128)(2,1)S(1)}, u32[]{:S(2)}, u32[]{:S(2)}) %collective-permute-start.67) | collective-permute-done | bytes 327712 | tf_op jit(solution)/shard_map/ppermute | solution.py:321
  261.2 1.8 combine0.1
  263.1 6.1 %collective-permute-start.77 = (bf16[64,2048]{1,0:T(8,128)(2,1)S(1)}, bf16[64,2048]{1,0:T(8,128)(2,1)S(1)}, u32[]{:S(2)}, u32[]{:S(2)}) collective-permute-start(bf16[64,2048]{1,0:T(8,128)(2,1)S(1)} %get-tuple-element.119), channel_id=1, source_target_pairs={{0,8},{8,0},{16,24},{24,16},{1,9},{9,1},{17,25},{25,17},{2,10},{10... | collective-permute-start | bytes 786440 | tf_op jit(solution)/shard_map/ppermute | solution.py:318
  269.2 7.1 %collective-permute-done.77 = bf16[64,2048]{1,0:T(8,128)(2,1)S(1)} collective-permute-done((bf16[64,2048]{1,0:T(8,128)(2,1)S(1)}, bf16[64,2048]{1,0:T(8,128)(2,1)S(1)}, u32[]{:S(2)}, u32[]{:S(2)}) %collective-permute-start.77) | collective-permute-done | bytes 262176 | tf_op jit(solution)/shard_map/ppermute | solution.py:318
  276.3 5.4 %collective-permute-done.78 = bf16[64,2048]{1,0:T(8,128)(2,1)S(1)} collective-permute-done((bf16[64,2048]{1,0:T(8,128)(2,1)S(1)}, bf16[64,2048]{1,0:T(8,128)(2,1)S(1)}, u32[]{:S(2)}, u32[]{:S(2)}) %collective-permute-start.78) | collective-permute-done | bytes 262176 | tf_op jit(solution)/shard_map/ppermute | solution.py:318
  281.7 1.3 fusion
  (218 shorter events, 29.2 us)
Async XLA Ops:
  6.5 69.3 %all-gather.2.cloned.1.call-start = ((), (), s32[]{:S(2)}) async-start(), calls=%async_computation | async-start | bytes 9437184 | tf_op jit(solution)/shard_map/all_gather | solution.py:364
  10.2 15.9 %collective-permute-start.6 = (f32[4,128]{1,0:T(4,128)S(1)}, f32[4,128]{1,0:T(4,128)S(1)}, u32[]{:S(2)}, u32[]{:S(2)}) collective-permute-start(f32[4,128]{1,0:T(4,128)S(1)} %get-tuple-element.162), channel_id=1, source_target_pairs={{0,8},{8,0},{16,24},{24,16},{1,9},{9,1},{17,25},{25,17},{2,10},{10... | collective-permute-start | bytes 6152 | tf_op jit(solution)/shard_map/ppermute | solution.py:318
  13.2 13.2 %collective-permute-start.7 = (f32[4,128]{1,0:T(4,128)S(1)}, f32[4,128]{1,0:T(4,128)S(1)}, u32[]{:S(2)}, u32[]{:S(2)}) collective-permute-start(f32[4,128]{1,0:T(4,128)S(1)} %get-tuple-element.162), channel_id=1, source_target_pairs={{0,16},{8,24},{16,0},{24,8},{1,17},{9,25},{17,1},{25,9},{2,18},{10... | collective-permute-start | bytes 6152 | tf_op jit(solution)/shard_map/ppermute | solution.py:318
  15.8 10.7 %collective-permute-start.8 = (f32[4,128]{1,0:T(4,128)S(1)}, f32[4,128]{1,0:T(4,128)S(1)}, u32[]{:S(2)}, u32[]{:S(2)}) collective-permute-start(f32[4,128]{1,0:T(4,128)S(1)} %get-tuple-element.162), channel_id=1, source_target_pairs={{0,24},{8,16},{16,8},{24,0},{1,25},{9,17},{17,9},{25,1},{2,26},{10... | collective-permute-start | bytes 6152 | tf_op jit(solution)/shard_map/ppermute | solution.py:318
  20.6 17.3 %collective-permute-start = (bf16[128,1536]{1,0:T(8,128)(2,1)}, bf16[128,1536]{1,0:T(8,128)(2,1)S(1)}, u32[]{:S(2)}, u32[]{:S(2)}) collective-permute-start(bf16[128,1536]{1,0:T(8,128)(2,1)} %copy.76), channel_id=1, source_target_pairs={{0,8},{8,0},{16,24},{24,16},{1,9},{9,1},{17,25},{25,17},{2,10},{10... | collective-permute-start | bytes 1179656 | tf_op jit(solution)/shard_map/ppermute | solution.py:318
  22.5 30.6 %collective-permute-start.1 = (bf16[128,1536]{1,0:T(8,128)(2,1)}, bf16[128,1536]{1,0:T(8,128)(2,1)S(1)}, u32[]{:S(2)}, u32[]{:S(2)}) collective-permute-start(bf16[128,1536]{1,0:T(8,128)(2,1)} %copy.77), channel_id=1, source_target_pairs={{0,16},{8,24},{16,0},{24,8},{1,17},{9,25},{17,1},{25,9},{2,18},{10... | collective-permute-start | bytes 1179656 | tf_op jit(solution)/shard_map/ppermute | solution.py:318
  26.2 26.9 %collective-permute-start.2 = (bf16[128,1536]{1,0:T(8,128)(2,1)S(1)}, bf16[128,1536]{1,0:T(8,128)(2,1)S(1)}, u32[]{:S(2)}, u32[]{:S(2)}) collective-permute-start(bf16[128,1536]{1,0:T(8,128)(2,1)S(1)} %copy.78), channel_id=1, source_target_pairs={{0,24},{8,16},{16,8},{24,0},{1,25},{9,17},{17,9},{25,1},{2,26},{10... | collective-permute-start | bytes 1179656 | tf_op jit(solution)/shard_map/ppermute | solution.py:318
  26.5 40.5 %collective-permute-start.9 = (f32[4,4,128]{2,1,0:T(4,128)S(1)}, f32[4,4,128]{2,1,0:T(4,128)S(1)}, u32[]{:S(2)}, u32[]{:S(2)}) collective-permute-start(f32[4,4,128]{2,1,0:T(4,128)S(1)} %pad_maximum_fusion), channel_id=1, source_target_pairs={{0,1},{1,0},{2,3},{3,2},{4,5},{5,4},{6,7},{7,6},{8,9},{9,8},{10,11... | collective-permute-start | bytes 24584 | tf_op jit(solution)/shard_map/ppermute | solution.py:324
  57.5 11.1 %collective-permute-start.3 = (bf16[128,512]{1,0:T(8,128)(2,1)S(1)}, bf16[128,512]{1,0:T(8,128)(2,1)S(1)}, u32[]{:S(2)}, u32[]{:S(2)}) collective-permute-start(bf16[128,512]{1,0:T(8,128)(2,1)S(1)} %get-tuple-element.60), channel_id=1, source_target_pairs={{0,8},{8,0},{16,24},{24,16},{1,9},{9,1},{17,25},{25,17},{2,10},{10... | collective-permute-start | bytes 393224 | tf_op jit(solution)/shard_map/ppermute | solution.py:318
  64.6 11.3 %collective-permute-start.4 = (bf16[128,512]{1,0:T(8,128)(2,1)S(1)}, bf16[128,512]{1,0:T(8,128)(2,1)S(1)}, u32[]{:S(2)}, u32[]{:S(2)}) collective-permute-start(bf16[128,512]{1,0:T(8,128)(2,1)S(1)} %get-tuple-element.61), channel_id=1, source_target_pairs={{0,16},{8,24},{16,0},{24,8},{1,17},{9,25},{17,1},{25,9},{2,18},{10... | collective-permute-start | bytes 393224 | tf_op jit(solution)/shard_map/ppermute | solution.py:318
  65.6 10.3 %collective-permute-start.5 = (bf16[128,512]{1,0:T(8,128)(2,1)S(1)}, bf16[128,512]{1,0:T(8,128)(2,1)S(1)}, u32[]{:S(2)}, u32[]{:S(2)}) collective-permute-start(bf16[128,512]{1,0:T(8,128)(2,1)S(1)} %get-tuple-element.62), channel_id=1, source_target_pairs={{0,24},{8,16},{16,8},{24,0},{1,25},{9,17},{17,9},{25,1},{2,26},{10... | collective-permute-start | bytes 393224 | tf_op jit(solution)/shard_map/ppermute | solution.py:318
  81.7 1.6 collective-permute-start.10
  81.8 1.9 collective-permute-start.11
  82.7 2.1 collective-permute-start.13
  83.2 1.6 collective-permute-start.14
  83.3 1.6 collective-permute-start.15
  85.7 25.5 %collective-permute-start.21 = (bf16[128,2048]{1,0:T(8,128)(2,1)S(1)}, bf16[128,2048]{1,0:T(8,128)(2,1)S(1)}, u32[]{:S(2)}, u32[]{:S(2)}) collective-permute-start(bf16[128,2048]{1,0:T(8,128)(2,1)S(1)} %after.3), channel_id=1, source_target_pairs={{0,8},{8,0},{16,24},{24,16},{1,9},{9,1},{17,25},{25,17},{2,10},{10... | collective-permute-start | bytes 1572872 | tf_op jit(solution)/shard_map/ppermute | solution.py:318
  87.7 26.1 %collective-permute-start.39 = (bf16[128,2048]{1,0:T(8,128)(2,1)S(1)}, bf16[128,2048]{1,0:T(8,128)(2,1)S(1)}, u32[]{:S(2)}, u32[]{:S(2)}) collective-permute-start(bf16[128,2048]{1,0:T(8,128)(2,1)S(1)} %after.3), channel_id=1, source_target_pairs={{0,16},{8,24},{16,0},{24,8},{1,17},{9,25},{17,1},{25,9},{2,18},{10... | collective-permute-start | bytes 1572872 | tf_op jit(solution)/shard_map/ppermute | solution.py:318
  88.7 22.6 %collective-permute-start.18 = (bf16[80,2048]{1,0:T(8,128)(2,1)S(1)}, bf16[80,2048]{1,0:T(8,128)(2,1)S(1)}, u32[]{:S(2)}, u32[]{:S(2)}) collective-permute-start(bf16[80,2048]{1,0:T(8,128)(2,1)S(1)} %get-tuple-element.66), channel_id=1, source_target_pairs={{0,2},{1,3},{2,0},{3,1},{4,6},{5,7},{6,4},{7,5},{8,10},{9,11},{10,... | collective-permute-start | bytes 983048 | tf_op jit(solution)/shard_map/ppermute | solution.py:321
  90.2 21.6 %collective-permute-start.19 = (bf16[80,2048]{1,0:T(8,128)(2,1)S(1)}, bf16[80,2048]{1,0:T(8,128)(2,1)S(1)}, u32[]{:S(2)}, u32[]{:S(2)}) collective-permute-start(bf16[80,2048]{1,0:T(8,128)(2,1)S(1)} %get-tuple-element.67), channel_id=1, source_target_pairs={{0,4},{1,5},{2,6},{3,7},{4,0},{5,1},{6,2},{7,3},{8,12},{9,13},{10,... | collective-permute-start | bytes 983048 | tf_op jit(solution)/shard_map/ppermute | solution.py:321
  91.7 20.2 %collective-permute-start.20 = (bf16[80,2048]{1,0:T(8,128)(2,1)S(1)}, bf16[80,2048]{1,0:T(8,128)(2,1)S(1)}, u32[]{:S(2)}, u32[]{:S(2)}) collective-permute-start(bf16[80,2048]{1,0:T(8,128)(2,1)S(1)} %get-tuple-element.68), channel_id=1, source_target_pairs={{0,6},{1,7},{2,4},{3,5},{4,2},{5,3},{6,0},{7,1},{8,14},{9,15},{10,... | collective-permute-start | bytes 983048 | tf_op jit(solution)/shard_map/ppermute | solution.py:321
  111.2 5.0 %collective-permute-start.22 = (bf16[16,2048]{1,0:T(8,128)(2,1)S(1)}, bf16[16,2048]{1,0:T(8,128)(2,1)S(1)}, u32[]{:S(2)}, u32[]{:S(2)}) collective-permute-start(bf16[16,2048]{1,0:T(8,128)(2,1)S(1)} %get-tuple-element.148), channel_id=1, source_target_pairs={{0,1},{1,0},{2,3},{3,2},{4,5},{5,4},{6,7},{7,6},{8,9},{9,8},{10,11... | collective-permute-start | bytes 196616 | tf_op jit(solution)/shard_map/ppermute | solution.py:324
  111.3 4.9 %collective-permute-start.23 = (bf16[16,2048]{1,0:T(8,128)(2,1)S(1)}, bf16[16,2048]{1,0:T(8,128)(2,1)S(1)}, u32[]{:S(2)}, u32[]{:S(2)}) collective-permute-start(bf16[16,2048]{1,0:T(8,128)(2,1)S(1)} %get-tuple-element.147), channel_id=1, source_target_pairs={{0,1},{1,0},{2,3},{3,2},{4,5},{5,4},{6,7},{7,6},{8,9},{9,8},{10,11... | collective-permute-start | bytes 196616 | tf_op jit(solution)/shard_map/ppermute | solution.py:324
  111.8 4.9 %collective-permute-start.24 = (bf16[16,2048]{1,0:T(8,128)(2,1)S(1)}, bf16[16,2048]{1,0:T(8,128)(2,1)S(1)}, u32[]{:S(2)}, u32[]{:S(2)}) collective-permute-start(bf16[16,2048]{1,0:T(8,128)(2,1)S(1)} %get-tuple-element.146), channel_id=1, source_target_pairs={{0,1},{1,0},{2,3},{3,2},{4,5},{5,4},{6,7},{7,6},{8,9},{9,8},{10,11... | collective-permute-start | bytes 196616 | tf_op jit(solution)/shard_map/ppermute | solution.py:324
  111.9 4.9 %collective-permute-start.25 = (bf16[16,2048]{1,0:T(8,128)(2,1)S(1)}, bf16[16,2048]{1,0:T(8,128)(2,1)S(1)}, u32[]{:S(2)}, u32[]{:S(2)}) collective-permute-start(bf16[16,2048]{1,0:T(8,128)(2,1)S(1)} %get-tuple-element.145), channel_id=1, source_target_pairs={{0,1},{1,0},{2,3},{3,2},{4,5},{5,4},{6,7},{7,6},{8,9},{9,8},{10,11... | collective-permute-start | bytes 196616 | tf_op jit(solution)/shard_map/ppermute | solution.py:324
  113.8 31.0 %collective-permute-start.30 = (bf16[128,2048]{1,0:T(8,128)(2,1)S(1)}, bf16[128,2048]{1,0:T(8,128)(2,1)S(1)}, u32[]{:S(2)}, u32[]{:S(2)}) collective-permute-start(bf16[128,2048]{1,0:T(8,128)(2,1)S(1)} %after.3), channel_id=1, source_target_pairs={{0,24},{8,16},{16,8},{24,0},{1,25},{9,17},{17,9},{25,1},{2,26},{10... | collective-permute-start | bytes 1572872 | tf_op jit(solution)/shard_map/ppermute | solution.py:318
  117.4 2.3 collective-permute-start.40
  117.6 3.6 %collective-permute-start.41 = (bf16[16,2048]{1,0:T(8,128)(2,1)S(1)}, bf16[16,2048]{1,0:T(8,128)(2,1)S(1)}, u32[]{:S(2)}, u32[]{:S(2)}) collective-permute-start(bf16[16,2048]{1,0:T(8,128)(2,1)S(1)} %get-tuple-element.131), channel_id=1, source_target_pairs={{0,1},{1,0},{2,3},{3,2},{4,5},{5,4},{6,7},{7,6},{8,9},{9,8},{10,11... | collective-permute-start | bytes 196616 | tf_op jit(solution)/shard_map/ppermute | solution.py:324
  118.0 4.8 %collective-permute-start.42 = (bf16[16,2048]{1,0:T(8,128)(2,1)S(1)}, bf16[16,2048]{1,0:T(8,128)(2,1)S(1)}, u32[]{:S(2)}, u32[]{:S(2)}) collective-permute-start(bf16[16,2048]{1,0:T(8,128)(2,1)S(1)} %get-tuple-element.130), channel_id=1, source_target_pairs={{0,1},{1,0},{2,3},{3,2},{4,5},{5,4},{6,7},{7,6},{8,9},{9,8},{10,11... | collective-permute-start | bytes 196616 | tf_op jit(solution)/shard_map/ppermute | solution.py:324
  118.1 5.1 %collective-permute-start.43 = (bf16[16,2048]{1,0:T(8,128)(2,1)S(1)}, bf16[16,2048]{1,0:T(8,128)(2,1)S(1)}, u32[]{:S(2)}, u32[]{:S(2)}) collective-permute-start(bf16[16,2048]{1,0:T(8,128)(2,1)S(1)} %get-tuple-element.129), channel_id=1, source_target_pairs={{0,1},{1,0},{2,3},{3,2},{4,5},{5,4},{6,7},{7,6},{8,9},{9,8},{10,11... | collective-permute-start | bytes 196616 | tf_op jit(solution)/shard_map/ppermute | solution.py:324
  119.7 19.0 %collective-permute-start.48 = (bf16[80,2048]{1,0:T(8,128)(2,1)S(1)}, bf16[80,2048]{1,0:T(8,128)(2,1)S(1)}, u32[]{:S(2)}, u32[]{:S(2)}) collective-permute-start(bf16[80,2048]{1,0:T(8,128)(2,1)S(1)} %get-tuple-element.74), channel_id=1, source_target_pairs={{0,2},{1,3},{2,0},{3,1},{4,6},{5,7},{6,4},{7,5},{8,10},{9,11},{10,... | collective-permute-start | bytes 983048 | tf_op jit(solution)/shard_map/ppermute | solution.py:321
  121.2 17.6 %collective-permute-start.49 = (bf16[80,2048]{1,0:T(8,128)(2,1)S(1)}, bf16[80,2048]{1,0:T(8,128)(2,1)S(1)}, u32[]{:S(2)}, u32[]{:S(2)}) collective-permute-start(bf16[80,2048]{1,0:T(8,128)(2,1)S(1)} %get-tuple-element.75), channel_id=1, source_target_pairs={{0,4},{1,5},{2,6},{3,7},{4,0},{5,1},{6,2},{7,3},{8,12},{9,13},{10,... | collective-permute-start | bytes 983048 | tf_op jit(solution)/shard_map/ppermute | solution.py:321
  122.8 16.0 %collective-permute-start.50 = (bf16[80,2048]{1,0:T(8,128)(2,1)S(1)}, bf16[80,2048]{1,0:T(8,128)(2,1)S(1)}, u32[]{:S(2)}, u32[]{:S(2)}) collective-permute-start(bf16[80,2048]{1,0:T(8,128)(2,1)S(1)} %get-tuple-element.76), channel_id=1, source_target_pairs={{0,6},{1,7},{2,4},{3,5},{4,2},{5,3},{6,0},{7,1},{8,14},{9,15},{10,... | collective-permute-start | bytes 983048 | tf_op jit(solution)/shard_map/ppermute | solution.py:321
  127.0 11.7 %collective-permute-start.47 = (bf16[16,2048]{1,0:T(8,128)(2,1)S(1)}, bf16[16,2048]{1,0:T(8,128)(2,1)S(1)}, u32[]{:S(2)}, u32[]{:S(2)}) collective-permute-start(bf16[16,2048]{1,0:T(8,128)(2,1)S(1)} %get-tuple-element.125), channel_id=1, source_target_pairs={{0,1},{1,0},{2,3},{3,2},{4,5},{5,4},{6,7},{7,6},{8,9},{9,8},{10,11... | collective-permute-start | bytes 196616 | tf_op jit(solution)/shard_map/ppermute | solution.py:324
  141.3 19.7 %collective-permute-start.51 = (bf16[80,2048]{1,0:T(8,128)(2,1)S(1)}, bf16[80,2048]{1,0:T(8,128)(2,1)S(1)}, u32[]{:S(2)}, u32[]{:S(2)}) collective-permute-start(bf16[80,2048]{1,0:T(8,128)(2,1)S(1)} %get-tuple-element.78), channel_id=1, source_target_pairs={{0,2},{1,3},{2,0},{3,1},{4,6},{5,7},{6,4},{7,5},{8,10},{9,11},{10,... | collective-permute-start | bytes 983048 | tf_op jit(solution)/shard_map/ppermute | solution.py:321
  142.8 18.2 %collective-permute-start.52 = (bf16[80,2048]{1,0:T(8,128)(2,1)S(1)}, bf16[80,2048]{1,0:T(8,128)(2,1)S(1)}, u32[]{:S(2)}, u32[]{:S(2)}) collective-permute-start(bf16[80,2048]{1,0:T(8,128)(2,1)S(1)} %get-tuple-element.79), channel_id=1, source_target_pairs={{0,4},{1,5},{2,6},{3,7},{4,0},{5,1},{6,2},{7,3},{8,12},{9,13},{10,... | collective-permute-start | bytes 983048 | tf_op jit(solution)/shard_map/ppermute | solution.py:321
  144.3 16.7 %collective-permute-start.53 = (bf16[80,2048]{1,0:T(8,128)(2,1)S(1)}, bf16[80,2048]{1,0:T(8,128)(2,1)S(1)}, u32[]{:S(2)}, u32[]{:S(2)}) collective-permute-start(bf16[80,2048]{1,0:T(8,128)(2,1)S(1)} %get-tuple-element.80), channel_id=1, source_target_pairs={{0,6},{1,7},{2,4},{3,5},{4,2},{5,3},{6,0},{7,1},{8,14},{9,15},{10,... | collective-permute-start | bytes 983048 | tf_op jit(solution)/shard_map/ppermute | solution.py:321
  148.7 12.3 %collective-permute-start.37 = (bf16[16,2048]{1,0:T(8,128)(2,1)S(1)}, bf16[16,2048]{1,0:T(8,128)(2,1)S(1)}, u32[]{:S(2)}, u32[]{:S(2)}) collective-permute-start(bf16[16,2048]{1,0:T(8,128)(2,1)S(1)} %get-tuple-element.134), channel_id=1, source_target_pairs={{0,1},{1,0},{2,3},{3,2},{4,5},{5,4},{6,7},{7,6},{8,9},{9,8},{10,11... | collective-permute-start | bytes 196616 | tf_op jit(solution)/shard_map/ppermute | solution.py:324
  148.8 12.2 %collective-permute-start.38 = (bf16[16,2048]{1,0:T(8,128)(2,1)S(1)}, bf16[16,2048]{1,0:T(8,128)(2,1)S(1)}, u32[]{:S(2)}, u32[]{:S(2)}) collective-permute-start(bf16[16,2048]{1,0:T(8,128)(2,1)S(1)} %get-tuple-element.133), channel_id=1, source_target_pairs={{0,1},{1,0},{2,3},{3,2},{4,5},{5,4},{6,7},{7,6},{8,9},{9,8},{10,11... | collective-permute-start | bytes 196616 | tf_op jit(solution)/shard_map/ppermute | solution.py:324
  163.6 18.1 %collective-permute-start.54 = (bf16[80,2048]{1,0:T(8,128)(2,1)S(1)}, bf16[80,2048]{1,0:T(8,128)(2,1)S(1)}, u32[]{:S(2)}, u32[]{:S(2)}) collective-permute-start(bf16[80,2048]{1,0:T(8,128)(2,1)S(1)} %get-tuple-element.83), channel_id=1, source_target_pairs={{0,2},{1,3},{2,0},{3,1},{4,6},{5,7},{6,4},{7,5},{8,10},{9,11},{10,... | collective-permute-start | bytes 983048 | tf_op jit(solution)/shard_map/ppermute | solution.py:321
  165.0 17.3 %collective-permute-start.55 = (bf16[80,2048]{1,0:T(8,128)(2,1)S(1)}, bf16[80,2048]{1,0:T(8,128)(2,1)}, u32[]{:S(2)}, u32[]{:S(2)}) collective-permute-start(bf16[80,2048]{1,0:T(8,128)(2,1)S(1)} %get-tuple-element.84), channel_id=1, source_target_pairs={{0,4},{1,5},{2,6},{3,7},{4,0},{5,1},{6,2},{7,3},{8,12},{9,13},{10,... | collective-permute-start | bytes 983048 | tf_op jit(solution)/shard_map/ppermute | solution.py:321
  166.6 15.7 %collective-permute-start.56 = (bf16[80,2048]{1,0:T(8,128)(2,1)S(1)}, bf16[80,2048]{1,0:T(8,128)(2,1)}, u32[]{:S(2)}, u32[]{:S(2)}) collective-permute-start(bf16[80,2048]{1,0:T(8,128)(2,1)S(1)} %get-tuple-element.85), channel_id=1, source_target_pairs={{0,6},{1,7},{2,4},{3,5},{4,2},{5,3},{6,0},{7,1},{8,14},{9,15},{10,... | collective-permute-start | bytes 983048 | tf_op jit(solution)/shard_map/ppermute | solution.py:321
  178.6 15.5 %collective-permute-start.60 = (bf16[80,2048]{1,0:T(8,128)(2,1)}, bf16[80,2048]{1,0:T(8,128)(2,1)S(1)}, u32[]{:S(2)}, u32[]{:S(2)}) collective-permute-start(bf16[80,2048]{1,0:T(8,128)(2,1)} %get-tuple-element.91), channel_id=1, source_target_pairs={{0,2},{1,3},{2,0},{3,1},{4,6},{5,7},{6,4},{7,5},{8,10},{9,11},{10,... | collective-permute-start | bytes 983048 | tf_op jit(solution)/shard_map/ppermute | solution.py:321
  180.1 15.9 %collective-permute-start.61 = (bf16[80,2048]{1,0:T(8,128)(2,1)}, bf16[80,2048]{1,0:T(8,128)(2,1)S(1)}, u32[]{:S(2)}, u32[]{:S(2)}) collective-permute-start(bf16[80,2048]{1,0:T(8,128)(2,1)} %get-tuple-element.92), channel_id=1, source_target_pairs={{0,4},{1,5},{2,6},{3,7},{4,0},{5,1},{6,2},{7,3},{8,12},{9,13},{10,... | collective-permute-start | bytes 983048 | tf_op jit(solution)/shard_map/ppermute | solution.py:321
  181.7 14.4 %collective-permute-start.62 = (bf16[80,2048]{1,0:T(8,128)(2,1)}, bf16[80,2048]{1,0:T(8,128)(2,1)S(1)}, u32[]{:S(2)}, u32[]{:S(2)}) collective-permute-start(bf16[80,2048]{1,0:T(8,128)(2,1)} %get-tuple-element.93), channel_id=1, source_target_pairs={{0,6},{1,7},{2,4},{3,5},{4,2},{5,3},{6,0},{7,1},{8,14},{9,15},{10,... | collective-permute-start | bytes 983048 | tf_op jit(solution)/shard_map/ppermute | solution.py:321
  198.8 3.6 %collective-permute-start.63 = (bf16[128,2048]{1,0:T(8,128)(2,1)S(1)}, bf16[128,2048]{1,0:T(8,128)(2,1)S(1)}, u32[]{:S(2)}, u32[]{:S(2)}) collective-permute-start(bf16[128,2048]{1,0:T(8,128)(2,1)S(1)} %get-tuple-element.95), channel_id=1, source_target_pairs={{0,1},{1,0},{2,3},{3,2},{4,5},{5,4},{6,7},{7,6},{8,9},{9,8},{10,11... | collective-permute-start | bytes 1572872 | tf_op jit(solution)/shard_map/ppermute | solution.py:324
  198.9 10.8 %collective-permute-start.57 = (bf16[80,2048]{1,0:T(8,128)(2,1)}, bf16[80,2048]{1,0:T(8,128)(2,1)S(1)}, u32[]{:S(2)}, u32[]{:S(2)}) collective-permute-start(bf16[80,2048]{1,0:T(8,128)(2,1)} %get-tuple-element.88), channel_id=1, source_target_pairs={{0,2},{1,3},{2,0},{3,1},{4,6},{5,7},{6,4},{7,5},{8,10},{9,11},{10,... | collective-permute-start | bytes 983048 | tf_op jit(solution)/shard_map/ppermute | solution.py:321
  200.2 15.5 %collective-permute-start.58 = (bf16[80,2048]{1,0:T(8,128)(2,1)}, bf16[80,2048]{1,0:T(8,128)(2,1)S(1)}, u32[]{:S(2)}, u32[]{:S(2)}) collective-permute-start(bf16[80,2048]{1,0:T(8,128)(2,1)} %get-tuple-element.89), channel_id=1, source_target_pairs={{0,4},{1,5},{2,6},{3,7},{4,0},{5,1},{6,2},{7,3},{8,12},{9,13},{10,... | collective-permute-start | bytes 983048 | tf_op jit(solution)/shard_map/ppermute | solution.py:321
  201.0 16.2 %collective-permute-start.59 = (bf16[80,2048]{1,0:T(8,128)(2,1)}, bf16[80,2048]{1,0:T(8,128)(2,1)S(1)}, u32[]{:S(2)}, u32[]{:S(2)}) collective-permute-start(bf16[80,2048]{1,0:T(8,128)(2,1)} %get-tuple-element.90), channel_id=1, source_target_pairs={{0,6},{1,7},{2,4},{3,5},{4,2},{5,3},{6,0},{7,1},{8,14},{9,15},{10,... | collective-permute-start | bytes 983048 | tf_op jit(solution)/shard_map/ppermute | solution.py:321
  202.6 14.6 %collective-permute-start.64 = (bf16[64,2048]{1,0:T(8,128)(2,1)S(1)}, bf16[64,2048]{1,0:T(8,128)(2,1)S(1)}, u32[]{:S(2)}, u32[]{:S(2)}) collective-permute-start(bf16[64,2048]{1,0:T(8,128)(2,1)S(1)} %get-tuple-element.124), channel_id=1, source_target_pairs={{0,16},{8,24},{16,0},{24,8},{1,17},{9,25},{17,1},{25,9},{2,18},{10... | collective-permute-start | bytes 786440 | tf_op jit(solution)/shard_map/ppermute | solution.py:318
  219.0 3.7 %collective-permute-start.65 = (bf16[128,2048]{1,0:T(8,128)(2,1)S(1)}, bf16[128,2048]{1,0:T(8,128)(2,1)S(1)}, u32[]{:S(2)}, u32[]{:S(2)}) collective-permute-start(bf16[128,2048]{1,0:T(8,128)(2,1)S(1)} %get-tuple-element.97), channel_id=1, source_target_pairs={{0,1},{1,0},{2,3},{3,2},{4,5},{5,4},{6,7},{7,6},{8,9},{9,8},{10,11... | collective-permute-start | bytes 1572872 | tf_op jit(solution)/shard_map/ppermute | solution.py:324
  219.1 22.4 %collective-permute-start.69 = (bf16[80,2048]{1,0:T(8,128)(2,1)S(1)}, bf16[80,2048]{1,0:T(8,128)(2,1)S(1)}, u32[]{:S(2)}, u32[]{:S(2)}) collective-permute-start(bf16[80,2048]{1,0:T(8,128)(2,1)S(1)} %get-tuple-element.106), channel_id=1, source_target_pairs={{0,2},{1,3},{2,0},{3,1},{4,6},{5,7},{6,4},{7,5},{8,10},{9,11},{10,... | collective-permute-start | bytes 983048 | tf_op jit(solution)/shard_map/ppermute | solution.py:321
  219.9 21.6 %collective-permute-start.70 = (bf16[80,2048]{1,0:T(8,128)(2,1)S(1)}, bf16[80,2048]{1,0:T(8,128)(2,1)S(1)}, u32[]{:S(2)}, u32[]{:S(2)}) collective-permute-start(bf16[80,2048]{1,0:T(8,128)(2,1)S(1)} %get-tuple-element.107), channel_id=1, source_target_pairs={{0,4},{1,5},{2,6},{3,7},{4,0},{5,1},{6,2},{7,3},{8,12},{9,13},{10,... | collective-permute-start | bytes 983048 | tf_op jit(solution)/shard_map/ppermute | solution.py:321
  221.5 20.1 %collective-permute-start.71 = (bf16[80,2048]{1,0:T(8,128)(2,1)S(1)}, bf16[80,2048]{1,0:T(8,128)(2,1)S(1)}, u32[]{:S(2)}, u32[]{:S(2)}) collective-permute-start(bf16[80,2048]{1,0:T(8,128)(2,1)S(1)} %get-tuple-element.108), channel_id=1, source_target_pairs={{0,6},{1,7},{2,4},{3,5},{4,2},{5,3},{6,0},{7,1},{8,14},{9,15},{10,... | collective-permute-start | bytes 983048 | tf_op jit(solution)/shard_map/ppermute | solution.py:321
  222.6 18.9 %collective-permute-start.72 = (bf16[64,2048]{1,0:T(8,128)(2,1)S(1)}, bf16[64,2048]{1,0:T(8,128)(2,1)S(1)}, u32[]{:S(2)}, u32[]{:S(2)}) collective-permute-start(bf16[64,2048]{1,0:T(8,128)(2,1)S(1)} %get-tuple-element.123), channel_id=1, source_target_pairs={{0,16},{8,24},{16,0},{24,8},{1,17},{9,25},{17,1},{25,9},{2,18},{10... | collective-permute-start | bytes 786440 | tf_op jit(solution)/shard_map/ppermute | solution.py:318
  222.8 18.7 %collective-permute-start.73 = (bf16[64,2048]{1,0:T(8,128)(2,1)S(1)}, bf16[64,2048]{1,0:T(8,128)(2,1)S(1)}, u32[]{:S(2)}, u32[]{:S(2)}) collective-permute-start(bf16[64,2048]{1,0:T(8,128)(2,1)S(1)} %get-tuple-element.122), channel_id=1, source_target_pairs={{0,24},{8,16},{16,8},{24,0},{1,25},{9,17},{17,9},{25,1},{2,26},{10... | collective-permute-start | bytes 786440 | tf_op jit(solution)/shard_map/ppermute | solution.py:318
  243.3 6.1 %collective-permute-start.74 = (bf16[128,2048]{1,0:T(8,128)(2,1)S(1)}, bf16[128,2048]{1,0:T(8,128)(2,1)S(1)}, u32[]{:S(2)}, u32[]{:S(2)}) collective-permute-start(bf16[128,2048]{1,0:T(8,128)(2,1)S(1)} %get-tuple-element.110), channel_id=1, source_target_pairs={{0,1},{1,0},{2,3},{3,2},{4,5},{5,4},{6,7},{7,6},{8,9},{9,8},{10,11... | collective-permute-start | bytes 1572872 | tf_op jit(solution)/shard_map/ppermute | solution.py:324
  243.5 13.3 %collective-permute-start.66 = (bf16[80,2048]{1,0:T(8,128)(2,1)S(1)}, bf16[80,2048]{1,0:T(8,128)(2,1)S(1)}, u32[]{:S(2)}, u32[]{:S(2)}) collective-permute-start(bf16[80,2048]{1,0:T(8,128)(2,1)S(1)} %get-tuple-element.99), channel_id=1, source_target_pairs={{0,2},{1,3},{2,0},{3,1},{4,6},{5,7},{6,4},{7,5},{8,10},{9,11},{10,... | collective-permute-start | bytes 983048 | tf_op jit(solution)/shard_map/ppermute | solution.py:321
  244.3 15.9 %collective-permute-start.67 = (bf16[80,2048]{1,0:T(8,128)(2,1)S(1)}, bf16[80,2048]{1,0:T(8,128)(2,1)S(1)}, u32[]{:S(2)}, u32[]{:S(2)}) collective-permute-start(bf16[80,2048]{1,0:T(8,128)(2,1)S(1)} %get-tuple-element.100), channel_id=1, source_target_pairs={{0,4},{1,5},{2,6},{3,7},{4,0},{5,1},{6,2},{7,3},{8,12},{9,13},{10,... | collective-permute-start | bytes 983048 | tf_op jit(solution)/shard_map/ppermute | solution.py:321
  245.8 15.3 %collective-permute-start.68 = (bf16[80,2048]{1,0:T(8,128)(2,1)S(1)}, bf16[80,2048]{1,0:T(8,128)(2,1)S(1)}, u32[]{:S(2)}, u32[]{:S(2)}) collective-permute-start(bf16[80,2048]{1,0:T(8,128)(2,1)S(1)} %get-tuple-element.101), channel_id=1, source_target_pairs={{0,6},{1,7},{2,4},{3,5},{4,2},{5,3},{6,0},{7,1},{8,14},{9,15},{10,... | collective-permute-start | bytes 983048 | tf_op jit(solution)/shard_map/ppermute | solution.py:321
  247.0 9.7 %collective-permute-start.75 = (bf16[64,2048]{1,0:T(8,128)(2,1)S(1)}, bf16[64,2048]{1,0:T(8,128)(2,1)S(1)}, u32[]{:S(2)}, u32[]{:S(2)}) collective-permute-start(bf16[64,2048]{1,0:T(8,128)(2,1)S(1)} %get-tuple-element.121), channel_id=1, source_target_pairs={{0,24},{8,16},{16,8},{24,0},{1,25},{9,17},{17,9},{25,1},{2,26},{10... | collective-permute-start | bytes 786440 | tf_op jit(solution)/shard_map/ppermute | solution.py:318
  262.9 18.8 %collective-permute-start.76 = (bf16[128,2048]{1,0:T(8,128)(2,1)S(1)}, bf16[128,2048]{1,0:T(8,128)(2,1)S(1)}, u32[]{:S(2)}, u32[]{:S(2)}) collective-permute-start(bf16[128,2048]{1,0:T(8,128)(2,1)S(1)} %get-tuple-element.112), channel_id=1, source_target_pairs={{0,1},{1,0},{2,3},{3,2},{4,5},{5,4},{6,7},{7,6},{8,9},{9,8},{10,11... | collective-permute-start | bytes 1572872 | tf_op jit(solution)/shard_map/ppermute | solution.py:324
  263.1 13.3 %collective-permute-start.77 = (bf16[64,2048]{1,0:T(8,128)(2,1)S(1)}, bf16[64,2048]{1,0:T(8,128)(2,1)S(1)}, u32[]{:S(2)}, u32[]{:S(2)}) collective-permute-start(bf16[64,2048]{1,0:T(8,128)(2,1)S(1)} %get-tuple-element.119), channel_id=1, source_target_pairs={{0,8},{8,0},{16,24},{24,16},{1,9},{9,1},{17,25},{25,17},{2,10},{10... | collective-permute-start | bytes 786440 | tf_op jit(solution)/shard_map/ppermute | solution.py:318
  269.2 12.6 %collective-permute-start.78 = (bf16[64,2048]{1,0:T(8,128)(2,1)S(1)}, bf16[64,2048]{1,0:T(8,128)(2,1)S(1)}, u32[]{:S(2)}, u32[]{:S(2)}) collective-permute-start(bf16[64,2048]{1,0:T(8,128)(2,1)S(1)} %get-tuple-element.120), channel_id=1, source_target_pairs={{0,8},{8,0},{16,24},{24,16},{1,9},{9,1},{17,25},{25,17},{2,10},{10... | collective-permute-start | bytes 786440 | tf_op jit(solution)/shard_map/ppermute | solution.py:318
  (47 other events, 619.7 us)
Sparse Core Ops, SparseCore 0:
  9.2 57.0 all-gather.1

commit v2 on v1

--- a/solution.py
+++ b/solution.py
@@ -10,8 +10,14 @@
 HEADS = 16
 HEAD_DIM = 128
 TOP = 2
-TRADES = 8
+TRADES = 2
 AHEAD = 2
+COVER = 16
+PAIRS = [(0, 1), (1, 0), (2, 3), (3, 2)]
+CROSS = [(1, 2), (2, 1)]
+OUT = [(1, 0), (2, 3)]
+IN = [(0, 1), (3, 2)]
+FAR = [(1, 3), (2, 0)]
 HID_TILE = 512
 OUT_TILE = 1024
 VMEM_LIMIT = 16 * 1024 * 1024
@@ -32,7 +38,7 @@
 
 def cost(flops, bytes_accessed, transcendentals):
     return pl.CostEstimate(
-        flops=0 * flops, bytes_accessed=0 * bytes_accessed, transcendentals=0 * transcendentals
+        flops=flops, bytes_accessed=bytes_accessed, transcendentals=transcendentals
     )
 
 
@@ -50,6 +56,33 @@
     )(*arrays, *deps)
 
 
+def split_kernel(count, seq_ref, *refs):
+    for i in range(count):
+        refs[count + i][...] = refs[i][...]
+
+
+def split_heads(my_seq, laid, count):
+    tok, width = laid.shape
+    cols = width // (3 * count)
+
+    def source(hop):
+        return pl.BlockSpec((tok, cols), lambda w, seq: (0, w * count + (seq[0] ^ hop)))
+
+    return pl.pallas_call(
+        functools.partial(split_kernel, count),
+        grid_spec=pltpu.PrefetchScalarGridSpec(
+            num_scalar_prefetch=1,
+            grid=(3,),
+            in_specs=[source(hop) for hop in range(count)],
+            out_specs=[pl.BlockSpec((tok, cols), lambda w, seq: (0, w))] * count,
+        ),
+        out_shape=[jax.ShapeDtypeStruct((tok, 3 * cols), laid.dtype)] * count,
+        compiler_params=params(),
+        cost_estimate=cost(0, 4 * tok * width, 0),
+        name="split_heads",
+    )(my_seq.reshape(1), *([laid] * count))
+
+
 def attend_kernel(count, *refs):
     parts, outs = refs[: 3 * count], refs[3 * count :]
     block = outs[0].shape[0]
@@ -62,8 +95,9 @@
     ) * HEAD_DIM ** (-0.5)
     top = jnp.max(scores, axis=-1, keepdims=True)
     grown = jnp.exp(scores - top)
-    probs = (grown / jnp.sum(grown, axis=-1, keepdims=True)).astype(jnp.bfloat16)
-    mixed = jnp.dot(probs, value, preferred_element_type=jnp.float32).astype(jnp.bfloat16)
+    total = jnp.sum(grown, axis=-1, keepdims=True)
+    mixed = jnp.dot(grown.astype(jnp.bfloat16), value, preferred_element_type=jnp.float32)
+    mixed = (mixed / total).astype(jnp.bfloat16)
     for i in range(count):
         outs[i][...] = mixed[i * block : (i + 1) * block]
 
@@ -137,7 +171,13 @@
         compiler_params=params(),
         cost_estimate=cost(2 * tok * count * depth * width, 2 * count * depth * width, 0),
         name="project",
-    )(my_seq.reshape(1), *parts, weight, residual, gain.reshape(1, width))
+    )(
+        my_seq.reshape(1),
+        *parts,
+        pltpu.with_memory_space_constraint(weight, pltpu.HBM),
+        residual,
+        gain.reshape(1, width),
+    )
 
 
 def slot_kernel(hop, chips, place_ref, mine_ref, *rest):
@@ -246,10 +286,14 @@
             pltpu.VMEM((hid, width), jnp.bfloat16),
             pltpu.SemaphoreType.DMA((n_sems,)),
         ],
-        compiler_params=pltpu.CompilerParams(vmem_limit_bytes=56 * 1024 * 1024),
+        compiler_params=pltpu.CompilerParams(vmem_limit_bytes=32 * 1024 * 1024),
         cost_estimate=cost(6 * rows * width * hid, 6 * width * hid, rows * hid),
         name=f"expert{hop}",
-    )(*pieces, gate_mat, up_mat, down_mat, *deps)
+    )(
+        *pieces,
+        *(pltpu.with_memory_space_constraint(w, pltpu.HBM) for w in (gate_mat, up_mat, down_mat)),
+        *deps,
+    )
 
 
 def combine_kernel(hop, chips, n_deps, place_ref, gates_ref, *refs):
@@ -286,7 +330,7 @@
             jax.ShapeDtypeStruct((tok, width), jnp.bfloat16),
         ],
         compiler_params=params(),
-        cost_estimate=cost(8 * tok * chips * piece * width, 2 * width * (chips * piece + 3 * tok), 0),
+        cost_estimate=cost(COVER * 8 * tok * chips * piece * width, COVER * 2 * width * (chips * piece + 3 * tok), 0),
         name=f"combine{hop}",
     )(place, gates, *pieces, *deps)
 
@@ -329,13 +373,8 @@
         part = value.shape[0] // TRADES
         return [over_cores(value[i * part : (i + 1) * part]) for i in range(TRADES)]
 
-    head_cols = head_local * HEAD_DIM
-    laid = attn_inputs.reshape(tok_count, 3, seq_count, head_cols)
-    blocks = []
-    for hop in range(seq_count):
-        part = lax.dynamic_index_in_dim(laid, my_seq ^ hop, 2, keepdims=False)
-        part = part.reshape(tok_count, 3 * head_cols)
-        blocks.append(over_seq(part, hop) if hop else part)
+    blocks = split_heads(my_seq, attn_inputs.reshape(tok_count, 3 * HEADS * HEAD_DIM), seq_count)
+    blocks = [over_seq(part, hop) if hop else part for hop, part in enumerate(blocks)]
     attended = attend(blocks, head_local)
     merged = [over_seq(p, hop) if hop else p for hop, p in enumerate(attended)]
 
@@ -347,7 +386,17 @@
     slot_ids = jnp.sum(before * one_hot, axis=-1)
     target = (route_ids * capacity + slot_ids).reshape(tok_count, TOP)
     route = jnp.concatenate([target.astype(jnp.float32), gate_weights[0]], axis=1).T
-    route = jnp.stack([route] + [over_seq(route, hop) for hop in range(1, seq_count)])
+    (route_out,) = after([route], [blocks[1]])
+    routes = [route] + [over_seq(route_out, hop) for hop in range(1, seq_count)]
+    in_middle = (my_seq == 1) | (my_seq == 2)
+    route = jnp.stack(
+        [
+            routes[0],
+            routes[1],
+            jnp.where(in_middle, routes[3], routes[2]),
+            jnp.where(in_middle, routes[2], routes[3]),
+        ]
+    )
     both = jnp.concatenate([route, over_cores(route)], axis=1)
     goal = jnp.concatenate([both[:, :TOP], both[:, 2 * TOP : 3 * TOP]], axis=1).astype(jnp.int32)
     gates = jnp.concatenate([both[:, TOP : 2 * TOP], both[:, 3 * TOP :]], axis=1)
@@ -380,30 +429,42 @@
         returned = [over_chips(p, s) if s else p for s, p in enumerate(partial)]
         mine, other = combine(hop, returned, place_t, gates_t, deps)
         total = mine + over_cores(other).astype(jnp.float32)
-        if hop == 0:
-            return total, mine
-        total = total.astype(jnp.bfloat16)
-        half = tok_count // 2
-        return [over_seq(total[:half], hop), over_seq(total[half:], hop)], total
+        return total, total.astype(jnp.bfloat16)
+
+    def hop_along(value, pairs):
+        return lax.ppermute(value, "seq", pairs)
 
     arrived = {}
     arrived[0], own0 = dispatch(0, normed, [])
     (normed_out,) = after([normed], [own0])
-    blocks = [normed] + [over_seq(normed_out, hop) for hop in range(1, seq_count)]
-    arrived[1], own1 = dispatch(1, blocks[1], arrived[0])
+    pair_block = hop_along(normed_out, PAIRS)
+    cross_block = hop_along(normed_out, CROSS)
+    cross_pair = hop_along(pair_block, CROSS)
+    arrived[1], own1 = dispatch(1, pair_block, arrived[0])
     done0 = run(0, [own1])
-    arrived[2], own2 = dispatch(2, blocks[2], arrived[1] + [done0[0]])
+    (kept,) = after([cross_block], [done0[0]])
+    second = jnp.where(in_middle, kept, hop_along(cross_block, OUT))
+    arrived[2], own2 = dispatch(2, second, [done0[0]])
     done1 = run(1, [own2])
-    arrived[3], own3 = dispatch(3, blocks[3], arrived[2] + [done1[0]])
+    (kept,) = after([cross_pair], [done1[0]])
+    third = jnp.where(in_middle, kept, hop_along(cross_pair, OUT))
+    arrived[3], own3 = dispatch(3, third, [done1[0]])
     done2 = run(2, [own3])
     done3 = run(3, [done2[0]])
-    back2, mark2 = give_back(2, done2, [], [done3[0]])
-    back3, mark3 = give_back(3, done3, [], [mark2, back2[0]])
-    back1, mark1 = give_back(1, done1, [mark2], [mark3, back2[1], back3[0]])
-    back0, _ = give_back(0, done0, [mark3], [mark1, back3[1]])
-    result = mid_float + back0
+    total2, send2 = give_back(2, done2, [], [done3[0]])
+    in2 = hop_along(send2, IN)
+    total3, send3 = give_back(3, done3, [], [send2])
+    in3 = hop_along(send3, IN)
+    send2 = (total2 + in2.astype(jnp.float32)).astype(jnp.bfloat16)
+    back2 = hop_along(send2, CROSS)
+    total1, send1 = give_back(1, done1, [], [send3, send2])
+    back1 = hop_along(send1, PAIRS)
+    send3 = (total3 + in3.astype(jnp.float32)).astype(jnp.bfloat16)
+    back3 = hop_along(send3, FAR)
+    result, _ = give_back(0, done0, [], [back1, back2, back3])
+    result = mid_float + result
     for back in (back1, back2, back3):
-        result = result + jnp.concatenate(back, axis=0).astype(jnp.float32)
+        result = result + back.astype(jnp.float32)
     return result.astype(jnp.bfloat16).reshape(1, tok_count, model_width)
 
 

time: 290 us -> 253 us (0.87)
  waiting for transfers between devices: 120 us -> 101 us
  local copies, waits for them, and re-layouts: 17.6 us -> 4.91 us
  Pallas kernels: 62.5 us -> 58 us
    ppermute x18 -> x9, waiting for transfers between devices: 92.5 us -> 29.4 us  [over_seq(): return lax.ppermute(value, 'seq', xor_pairs(seq_count, hop))]
    ppermute x24, waiting for transfers between devices: 20.9 us -> 45.3 us  [over_chips(): return lax.ppermute(value, 'exp', xor_pairs(expert_count, 2 * step))]
    ppermute x0 -> x10, waiting for transfers between devices: none -> 19.1 us  [hop_along(): return lax.ppermute(value, 'seq', pairs)]
    ppermute x0 -> x10, starting transfers between devices: none -> 18.8 us  [hop_along(): return lax.ppermute(value, 'seq', pairs)]
    ppermute x18 -> x9, starting transfers between devices: 35.1 us -> 20.2 us  [over_seq(): return lax.ppermute(value, 'seq', xor_pairs(seq_count, hop))]
    unnamed x64 -> x31, local copies, waits for them, and re-layouts: 11.8 us -> 2.54 us
    pallas_call x4, Pallas kernels: 46.5 us -> 38.4 us  [expert(): pl.pallas_call(functools.partial(expert_kernel, chips, len(deps)), in_spe...]
    ppermute x37 -> x13, starting transfers between devices: 8.2 us -> 2.56 us  [over_cores(): return lax.ppermute(value, 'exp', xor_pairs(expert_count, 1))]
  transfers between devices with their start and end apart: 80 -> 57, of which waited for: 25 -> 21; matrix products, arithmetic and copies ran while one was open for 4% -> 2% of each run, Pallas kernels for 18% -> 19%
where the time goes in v2:
time: 253 us; the launch traced here: 252 us
  waiting for transfers between devices  101 us (40%)
  starting transfers between devices  70.9 us (28%)
  Pallas kernels  58 us (23%)
  between operations  14.1 us (6%)
  local copies, waits for them, and re-layouts  4.91 us (2%)
  other arithmetic  3.36 us (1%)
    ppermute x24, waiting for transfers between devices, over_chips(): return lax.ppermute(value, 'exp', xor_pairs(expert_count, 2 * step))  45.3 us
    pallas_call x4, Pallas kernels, expert(): pl.pallas_call(functools.partial(expert_kernel, chips, len(deps)), in_spe...  38.4 us
    ppermute x9, waiting for transfers between devices, over_seq(): return lax.ppermute(value, 'seq', xor_pairs(seq_count, hop))  29.4 us
    ppermute x24, starting transfers between devices, over_chips(): return lax.ppermute(value, 'exp', xor_pairs(expert_count, 2 * step))  29.3 us
    ppermute x9, starting transfers between devices, over_seq(): return lax.ppermute(value, 'seq', xor_pairs(seq_count, hop))  20.2 us
    ppermute x10, waiting for transfers between devices, hop_along(): return lax.ppermute(value, 'seq', pairs)  19.1 us
    ppermute x10, starting transfers between devices, hop_along(): return lax.ppermute(value, 'seq', pairs)  18.8 us
    pallas_call x4, Pallas kernels, combine(): pl.pallas_call(functools.partial(combine_kernel, hop, chips, len(deps)),...  7.07 us
  transfers between devices with their start and end apart: 57, of which 21 were waited for; matrix products, arithmetic and copies ran while one was open for 2% of the time, Pallas kernels for 19%

profile of v2, /device:TPU:0, one launch (start us, length us, event | category | flops | bytes accessed | tf_op | source)
XLA Modules:
  0.0 252.3 jit_solution(9872968990766376509)
XLA Ops:
  6.5 0.7 all-gather.2.cloned.1.call-update
  7.3 1.4 copy-done
  9.2 3.1 %collective-permute-start = (bf16[128,1536]{1,0:T(8,128)(2,1)S(1)}, bf16[128,1536]{1,0:T(8,128)(2,1)S(1)}, u32[]{:S(2)}, u32[]{:S(2)}) collective-permute-start(bf16[128,1536]{1,0:T(8,128)(2,1)S(1)} %get-tuple-element.56), channel_id=1, source_target_pairs={{0,8},{8,0},{16,24},{24,16},{1,9},{9,1},{17,25},{25,17},{2,10},{10... | collective-permute-start | bytes 1179656 | tf_op jit(solution)/shard_map/ppermute | solution.py:362
  12.3 2.6 %collective-permute-start.1 = (bf16[128,1536]{1,0:T(8,128)(2,1)S(1)}, bf16[128,1536]{1,0:T(8,128)(2,1)S(1)}, u32[]{:S(2)}, u32[]{:S(2)}) collective-permute-start(bf16[128,1536]{1,0:T(8,128)(2,1)S(1)} %get-tuple-element.57), channel_id=1, source_target_pairs={{0,16},{8,24},{16,0},{24,8},{1,17},{9,25},{17,1},{25,9},{2,18},{10... | collective-permute-start | bytes 1179656 | tf_op jit(solution)/shard_map/ppermute | solution.py:362
  16.5 12.5 %collective-permute-done.refs_1_.refs_5_.refs_9_.__1_ = bf16[128,1536]{1,0:T(8,128)(2,1)S(1)} collective-permute-done((bf16[128,1536]{1,0:T(8,128)(2,1)S(1)}, bf16[128,1536]{1,0:T(8,128)(2,1)S(1)}, u32[]{:S(2)}, u32[]{:S(2)}) %collective-permute-start) | collective-permute-done | bytes 393248 | tf_op jit(solution)/shard_map/ppermute | solution.py:362
  29.1 3.2 %collective-permute-start.7 = (f32[4,128]{1,0:T(4,128)S(1)}, f32[4,128]{1,0:T(4,128)S(1)}, u32[]{:S(2)}, u32[]{:S(2)}) collective-permute-start(f32[4,128]{1,0:T(4,128)S(1)} %after.4), channel_id=1, source_target_pairs={{0,24},{8,16},{16,8},{24,0},{1,25},{9,17},{17,9},{25,1},{2,26},{10... | collective-permute-start | bytes 6152 | tf_op jit(solution)/shard_map/ppermute | solution.py:362
  32.3 1.2 collective-permute-start.6
  33.5 8.7 %collective-permute-done.1.refs_2_.refs_6_.refs_10_ = bf16[128,1536]{1,0:T(8,128)(2,1)S(1)} collective-permute-done((bf16[128,1536]{1,0:T(8,128)(2,1)S(1)}, bf16[128,1536]{1,0:T(8,128)(2,1)S(1)}, u32[]{:S(2)}, u32[]{:S(2)}) %collective-permute-start.1) | collective-permute-done | bytes 393248 | tf_op jit(solution)/shard_map/ppermute | solution.py:362
  42.2 3.9 %attend.1 = (bf16[128,512]{1,0:T(8,128)(2,1)S(1)}, bf16[128,512]{1,0:T(8,128)(2,1)S(1)}, bf16[128,512]{1,0:T(8,128)(2,1)S(1)}, bf16[128,512]{1,0:T(8,128)(2,1)S(1)}) custom-call(bf16[128,1536]{1,0:T(8,128)(2,1)S(1)} %get-tuple-element.55.refs_0_.refs_4_.refs_8_, bf16[128,1536]{1,0:T(8,128)(2,1)S(1)} %collective-permute-done.refs_1_.refs_5_.refs_9_.__1_, ...), custom_call_target="tpu_custom_call" | custom-call | flops 536870912 | bytes 2097152 | tf_op jit(solution)/shard_map/attend/pallas_call | solution.py:113
  46.1 7.7 %collective-permute-start.3 = (bf16[128,512]{1,0:T(8,128)(2,1)S(1)}, bf16[128,512]{1,0:T(8,128)(2,1)S(1)}, u32[]{:S(2)}, u32[]{:S(2)}) collective-permute-start(bf16[128,512]{1,0:T(8,128)(2,1)S(1)} %get-tuple-element.60), channel_id=1, source_target_pairs={{0,8},{8,0},{16,24},{24,16},{1,9},{9,1},{17,25},{25,17},{2,10},{10... | collective-permute-start | bytes 393224 | tf_op jit(solution)/shard_map/ppermute | solution.py:362
  53.8 1.1 collective-permute-start.4
  54.9 1.4 collective-permute-start.5
  56.4 1.1 collective-permute-done.9
  58.0 7.6 %collective-permute-done.4.refs_2_ = bf16[128,512]{1,0:T(8,128)(2,1)S(1)} collective-permute-done((bf16[128,512]{1,0:T(8,128)(2,1)S(1)}, bf16[128,512]{1,0:T(8,128)(2,1)S(1)}, u32[]{:S(2)}, u32[]{:S(2)}) %collective-permute-start.4) | collective-permute-done | bytes 131104 | tf_op jit(solution)/shard_map/ppermute | solution.py:362
  65.6 0.8 all-gather.2.cloned.1.call-done.refs_4_
  66.4 5.1 %project.1 = (bf16[128,2048]{1,0:T(8,128)(2,1)S(1)}, bf16[128,2048]{1,0:T(8,128)(2,1)S(1)}) custom-call(s32[1]{0:T(128)} %bitcast.seq_ref, bf16[128,512]{1,0:T(8,128)(2,1)S(1)} %get-tuple-element.59.refs_0_, bf16[128,512]{1,0:T(8,128)(2,1)S(1)} %collective-permute-done.3.refs_1_, bf16[128,512]{1,0:T(8,128)(2,1)S(1)} %collective-permute-done.4.refs_2_, ...), custom_call_target="tpu_custom_call" | custom-call | flops 1073741824 | bytes 8388608 | tf_op jit(solution)/shard_map/project/pallas_call | solution.py:156
  74.1 1.6 collective-permute-start.15
  76.3 1.5 collective-permute-start.12
  77.9 1.3 collective-permute-start.13
  79.1 0.7 collective-permute-start.14
  79.9 8.4 %collective-permute-done.15.mine_ref = bf16[128,2048]{1,0:T(8,128)(2,1)S(1)} collective-permute-done((bf16[128,2048]{1,0:T(8,128)(2,1)S(1)}, bf16[128,2048]{1,0:T(8,128)(2,1)S(1)}, u32[]{:S(2)}, u32[]{:S(2)}) %collective-permute-start.15) | collective-permute-done | bytes 524320 | tf_op jit(solution)/shard_map/ppermute | solution.py:435
  88.9 5.3 %collective-permute-done.13.rest_4_.refs_2_ = bf16[80,2048]{1,0:T(8,128)(2,1)S(1)} collective-permute-done((bf16[80,2048]{1,0:T(8,128)(2,1)S(1)}, bf16[80,2048]{1,0:T(8,128)(2,1)S(1)}, u32[]{:S(2)}, u32[]{:S(2)}) %collective-permute-start.13) | collective-permute-done | bytes 327712 | tf_op jit(solution)/shard_map/ppermute | solution.py:365
  94.9 1.3 collective-permute-start.25
  96.8 1.2 collective-permute-start.22
  98.0 2.3 collective-permute-start.23
  100.3 9.2 %expert0.1 = (bf16[80,2048]{1,0:T(8,128)(2,1)S(1)}, bf16[80,2048]{1,0:T(8,128)(2,1)S(1)}, bf16[80,2048]{1,0:T(8,128)(2,1)S(1)}, bf16[80,2048]{1,0:T(8,128)(2,1)S(1)}) custom-call(bf16[80,2048]{1,0:T(8,128)(2,1)S(1)} %get-tuple-element.65.__1_.rest_2_.refs_0_, bf16[80,2048]{1,0:T(8,128)(2,1)S(1)} %collective-permute-done.12.rest_3_.refs_1_, ...), custom_call_target="tpu_custom_call" | custom-call | flops 5536481280 | bytes 17301504 | tf_op jit(solution)/shard_map/expert0/pallas_call | solution.py:276
  110.3 1.0 collective-permute-done.26.rest_0_
  111.3 1.5 collective-permute-start.32
  112.8 1.4 slots2.1
  114.3 1.2 collective-permute-start.39
  115.5 2.3 collective-permute-start.40
  117.7 9.2 %expert1.1 = (bf16[80,2048]{1,0:T(8,128)(2,1)S(1)}, bf16[80,2048]{1,0:T(8,128)(2,1)S(1)}, bf16[80,2048]{1,0:T(8,128)(2,1)S(1)}, bf16[80,2048]{1,0:T(8,128)(2,1)S(1)}) custom-call(bf16[80,2048]{1,0:T(8,128)(2,1)S(1)} %get-tuple-element.69.refs_7_.refs_0_, bf16[80,2048]{1,0:T(8,128)(2,1)S(1)} %collective-permute-done.21.refs_1_, ...), custom_call_target="tpu_custom_call" | custom-call | flops 5536481280 | bytes 17301504 | tf_op jit(solution)/shard_map/expert1/pallas_call | solution.py:276
  127.0 3.2 %collective-permute-done.32 = bf16[128,2048]{1,0:T(8,128)(2,1)S(1)} collective-permute-done((bf16[128,2048]{1,0:T(8,128)(2,1)S(1)}, bf16[128,2048]{1,0:T(8,128)(2,1)S(1)}, u32[]{:S(2)}, u32[]{:S(2)}) %collective-permute-start.32) | collective-permute-done | bytes 524320 | tf_op jit(solution)/shard_map/ppermute | solution.py:435
  130.3 0.9 fusion.20
  131.8 1.1 collective-permute-done.33.rest_0_
  134.5 2.9 %collective-permute-start.37 = (bf16[80,2048]{1,0:T(8,128)(2,1)S(1)}, bf16[80,2048]{1,0:T(8,128)(2,1)S(1)}, u32[]{:S(2)}, u32[]{:S(2)}) collective-permute-start(bf16[80,2048]{1,0:T(8,128)(2,1)S(1)} %get-tuple-element.85), channel_id=1, source_target_pairs={{0,6},{1,7},{2,4},{3,5},{4,2},{5,3},{6,0},{7,1},{8,14},{9,15},{10,... | collective-permute-start | bytes 983048 | tf_op jit(solution)/shard_map/ppermute | solution.py:365
  137.4 1.0 copy-done.12
  138.3 10.4 %expert2.1 = (bf16[80,2048]{1,0:T(8,128)(2,1)S(1)}, bf16[80,2048]{1,0:T(8,128)(2,1)S(1)}, bf16[80,2048]{1,0:T(8,128)(2,1)S(1)}, bf16[80,2048]{1,0:T(8,128)(2,1)S(1)}) custom-call(bf16[80,2048]{1,0:T(8,128)(2,1)S(1)} %copy-done.12, bf16[80,2048]{1,0:T(8,128)(2,1)} %collective-permute-done.38.refs_1_, bf16[80,2048]{1,0:T(8,128)(2,1)} %collective-permute-done.39.refs_2_, ...), custom_call_target="tpu_custom_call" | custom-call | flops 5536481280 | bytes 17301504 | tf_op jit(solution)/shard_map/expert2/pallas_call | solution.py:276
  149.4 2.9 %collective-permute-start.46 = (bf16[80,2048]{1,0:T(8,128)(2,1)S(1)}, bf16[80,2048]{1,0:T(8,128)(2,1)S(1)}, u32[]{:S(2)}, u32[]{:S(2)}) collective-permute-start(bf16[80,2048]{1,0:T(8,128)(2,1)S(1)} %get-tuple-element.96), channel_id=1, source_target_pairs={{0,6},{1,7},{2,4},{3,5},{4,2},{5,3},{6,0},{7,1},{8,14},{9,15},{10,... | collective-permute-start | bytes 983048 | tf_op jit(solution)/shard_map/ppermute | solution.py:365
  152.3 9.5 %expert3.1 = (bf16[80,2048]{1,0:T(8,128)(2,1)S(1)}, bf16[80,2048]{1,0:T(8,128)(2,1)S(1)}, bf16[80,2048]{1,0:T(8,128)(2,1)S(1)}, bf16[80,2048]{1,0:T(8,128)(2,1)S(1)}) custom-call(bf16[80,2048]{1,0:T(8,128)(2,1)S(1)} %get-tuple-element.82.refs_7_.refs_0_, bf16[80,2048]{1,0:T(8,128)(2,1)S(1)} %collective-permute-done.35.refs_1_, ...), custom_call_target="tpu_custom_call" | custom-call | flops 5536481280 | bytes 17301504 | tf_op jit(solution)/shard_map/expert3/pallas_call | solution.py:276
  161.8 3.2 %collective-permute-done.45.refs_2_ = bf16[80,2048]{1,0:T(8,128)(2,1)S(1)} collective-permute-done((bf16[80,2048]{1,0:T(8,128)(2,1)S(1)}, bf16[80,2048]{1,0:T(8,128)(2,1)S(1)}, u32[]{:S(2)}, u32[]{:S(2)}) %collective-permute-start.45) | collective-permute-done | bytes 327712 | tf_op jit(solution)/shard_map/ppermute | solution.py:365
  165.0 1.8 combine2.1
  166.9 1.5 collective-permute-start.41
  169.0 1.5 collective-permute-start.43
  170.6 4.5 %collective-permute-start.49 = (bf16[128,2048]{1,0:T(8,128)(2,1)S(1)}, bf16[128,2048]{1,0:T(8,128)(2,1)S(1)}, u32[]{:S(2)}, u32[]{:S(2)}) collective-permute-start(bf16[128,2048]{1,0:T(8,128)(2,1)S(1)} %fusion.refs_4_), channel_id=1, source_target_pairs={{0,8},{24,16},{1,9},{25,17},{2,10},{26,18},{3,11},{27,19},{4,12},{... | collective-permute-start | bytes 1572872 | tf_op jit(solution)/shard_map/ppermute | solution.py:435
  175.0 2.4 collective-permute-done.41.refs_1_
  177.4 7.8 %collective-permute-done.42.refs_2_ = bf16[80,2048]{1,0:T(8,128)(2,1)S(1)} collective-permute-done((bf16[80,2048]{1,0:T(8,128)(2,1)S(1)}, bf16[80,2048]{1,0:T(8,128)(2,1)S(1)}, u32[]{:S(2)}, u32[]{:S(2)}) %collective-permute-start.42) | collective-permute-done | bytes 327712 | tf_op jit(solution)/shard_map/ppermute | solution.py:365
  185.2 1.8 combine3.1
  187.7 1.2 collective-permute-start.29
  188.9 1.7 collective-permute-start.30
  191.0 6.7 %collective-permute-done.28.refs_1_ = bf16[80,2048]{1,0:T(8,128)(2,1)S(1)} collective-permute-done((bf16[80,2048]{1,0:T(8,128)(2,1)S(1)}, bf16[80,2048]{1,0:T(8,128)(2,1)S(1)}, u32[]{:S(2)}, u32[]{:S(2)}) %collective-permute-start.28) | collective-permute-done | bytes 327712 | tf_op jit(solution)/shard_map/ppermute | solution.py:365
  197.7 6.8 %collective-permute-done.29.refs_2_ = bf16[80,2048]{1,0:T(8,128)(2,1)S(1)} collective-permute-done((bf16[80,2048]{1,0:T(8,128)(2,1)S(1)}, bf16[80,2048]{1,0:T(8,128)(2,1)S(1)}, u32[]{:S(2)}, u32[]{:S(2)}) %collective-permute-start.29) | collective-permute-done | bytes 327712 | tf_op jit(solution)/shard_map/ppermute | solution.py:365
  204.5 1.8 combine1.1
  206.4 4.3 %collective-permute-start.53 = (bf16[128,2048]{1,0:T(8,128)(2,1)S(1)}, bf16[128,2048]{1,0:T(8,128)(2,1)S(1)}, u32[]{:S(2)}, u32[]{:S(2)}) collective-permute-start(bf16[128,2048]{1,0:T(8,128)(2,1)S(1)} %fusion.1.refs_4_), channel_id=1, source_target_pairs={{0,8},{24,16},{1,9},{25,17},{2,10},{26,18},{3,11},{27,19},{4,12},{... | collective-permute-start | bytes 1572872 | tf_op jit(solution)/shard_map/ppermute | solution.py:435
  210.7 1.5 collective-permute-start.18
  213.1 2.4 collective-permute-start.51
  215.4 7.5 %collective-permute-done.53 = bf16[128,2048]{1,0:T(8,128)(2,1)S(1)} collective-permute-done((bf16[128,2048]{1,0:T(8,128)(2,1)S(1)}, bf16[128,2048]{1,0:T(8,128)(2,1)S(1)}, u32[]{:S(2)}, u32[]{:S(2)}) %collective-permute-start.53) | collective-permute-done | bytes 524320 | tf_op jit(solution)/shard_map/ppermute | solution.py:435
  223.1 1.3 collective-permute-start.54
  224.4 1.2 collective-permute-start.19
  225.6 1.8 collective-permute-start.20
  227.4 13.0 %collective-permute-done.19.refs_2_ = bf16[80,2048]{1,0:T(8,128)(2,1)S(1)} collective-permute-done((bf16[80,2048]{1,0:T(8,128)(2,1)S(1)}, bf16[80,2048]{1,0:T(8,128)(2,1)S(1)}, u32[]{:S(2)}, u32[]{:S(2)}) %collective-permute-start.19) | collective-permute-done | bytes 327712 | tf_op jit(solution)/shard_map/ppermute | solution.py:365
  240.4 1.8 combine0.1
  242.3 1.9 collective-permute-done.55
  244.2 1.3 fusion.2
  (138 shorter events, 14.4 us)
Async XLA Ops:
  6.5 59.8 %all-gather.2.cloned.1.call-start = ((), (), s32[]{:S(2)}) async-start(), calls=%async_computation | async-start | bytes 9437184 | tf_op jit(solution)/shard_map/all_gather | solution.py:413
  8.7 57.7 %copy-start.1 = (bf16[1,128,2048]{2,1,0:T(8,128)(2,1)S(1)}, bf16[1,128,2048]{2,1,0:T(8,128)(2,1)}, u32[]{:S(2)}) copy-start(bf16[1,128,2048]{2,1,0:T(8,128)(2,1)} %param.10) | copy-start | bytes 1572868
  8.7 57.7 %copy-start.2 = (f32[2048]{0:T(1024)S(1)}, f32[2048]{0:T(1024)}, u32[]{:S(2)}) copy-start(f32[2048]{0:T(1024)} %param.12) | copy-start | bytes 24580
  9.2 19.9 %collective-permute-start = (bf16[128,1536]{1,0:T(8,128)(2,1)S(1)}, bf16[128,1536]{1,0:T(8,128)(2,1)S(1)}, u32[]{:S(2)}, u32[]{:S(2)}) collective-permute-start(bf16[128,1536]{1,0:T(8,128)(2,1)S(1)} %get-tuple-element.56), channel_id=1, source_target_pairs={{0,8},{8,0},{16,24},{24,16},{1,9},{9,1},{17,25},{25,17},{2,10},{10... | collective-permute-start | bytes 1179656 | tf_op jit(solution)/shard_map/ppermute | solution.py:362
  12.3 29.9 %collective-permute-start.1 = (bf16[128,1536]{1,0:T(8,128)(2,1)S(1)}, bf16[128,1536]{1,0:T(8,128)(2,1)S(1)}, u32[]{:S(2)}, u32[]{:S(2)}) collective-permute-start(bf16[128,1536]{1,0:T(8,128)(2,1)S(1)} %get-tuple-element.57), channel_id=1, source_target_pairs={{0,16},{8,24},{16,0},{24,8},{1,17},{9,25},{17,1},{25,9},{2,18},{10... | collective-permute-start | bytes 1179656 | tf_op jit(solution)/shard_map/ppermute | solution.py:362
  14.9 27.3 %collective-permute-start.2 = (bf16[128,1536]{1,0:T(8,128)(2,1)S(1)}, bf16[128,1536]{1,0:T(8,128)(2,1)S(1)}, u32[]{:S(2)}, u32[]{:S(2)}) collective-permute-start(bf16[128,1536]{1,0:T(8,128)(2,1)S(1)} %get-tuple-element.58), channel_id=1, source_target_pairs={{0,24},{8,16},{16,8},{24,0},{1,25},{9,17},{17,9},{25,1},{2,26},{10... | collective-permute-start | bytes 1179656 | tf_op jit(solution)/shard_map/ppermute | solution.py:362
  29.1 25.8 %collective-permute-start.7 = (f32[4,128]{1,0:T(4,128)S(1)}, f32[4,128]{1,0:T(4,128)S(1)}, u32[]{:S(2)}, u32[]{:S(2)}) collective-permute-start(f32[4,128]{1,0:T(4,128)S(1)} %after.4), channel_id=1, source_target_pairs={{0,24},{8,16},{16,8},{24,0},{1,25},{9,17},{17,9},{25,1},{2,26},{10... | collective-permute-start | bytes 6152 | tf_op jit(solution)/shard_map/ppermute | solution.py:362
  32.3 24.0 %collective-permute-start.8 = (f32[4,128]{1,0:T(4,128)S(1)}, f32[4,128]{1,0:T(4,128)S(1)}, u32[]{:S(2)}, u32[]{:S(2)}) collective-permute-start(f32[4,128]{1,0:T(4,128)S(1)} %after.4), channel_id=1, source_target_pairs={{0,16},{8,24},{16,0},{24,8},{1,17},{9,25},{17,1},{25,9},{2,18},{10... | collective-permute-start | bytes 6152 | tf_op jit(solution)/shard_map/ppermute | solution.py:362
  32.3 24.0 %collective-permute-start.6 = (f32[4,128]{1,0:T(4,128)S(1)}, f32[4,128]{1,0:T(4,128)S(1)}, u32[]{:S(2)}, u32[]{:S(2)}) collective-permute-start(f32[4,128]{1,0:T(4,128)S(1)} %after.4), channel_id=1, source_target_pairs={{0,8},{8,0},{16,24},{24,16},{1,9},{9,1},{17,25},{25,17},{2,10},{10... | collective-permute-start | bytes 6152 | tf_op jit(solution)/shard_map/ppermute | solution.py:362
  46.1 11.9 %collective-permute-start.3 = (bf16[128,512]{1,0:T(8,128)(2,1)S(1)}, bf16[128,512]{1,0:T(8,128)(2,1)S(1)}, u32[]{:S(2)}, u32[]{:S(2)}) collective-permute-start(bf16[128,512]{1,0:T(8,128)(2,1)S(1)} %get-tuple-element.60), channel_id=1, source_target_pairs={{0,8},{8,0},{16,24},{24,16},{1,9},{9,1},{17,25},{25,17},{2,10},{10... | collective-permute-start | bytes 393224 | tf_op jit(solution)/shard_map/ppermute | solution.py:362
  53.8 11.8 %collective-permute-start.4 = (bf16[128,512]{1,0:T(8,128)(2,1)S(1)}, bf16[128,512]{1,0:T(8,128)(2,1)S(1)}, u32[]{:S(2)}, u32[]{:S(2)}) collective-permute-start(bf16[128,512]{1,0:T(8,128)(2,1)S(1)} %get-tuple-element.61), channel_id=1, source_target_pairs={{0,16},{8,24},{16,0},{24,8},{1,17},{9,25},{17,1},{25,9},{2,18},{10... | collective-permute-start | bytes 393224 | tf_op jit(solution)/shard_map/ppermute | solution.py:362
  54.9 10.8 %collective-permute-start.5 = (bf16[128,512]{1,0:T(8,128)(2,1)S(1)}, bf16[128,512]{1,0:T(8,128)(2,1)S(1)}, u32[]{:S(2)}, u32[]{:S(2)}) collective-permute-start(bf16[128,512]{1,0:T(8,128)(2,1)S(1)} %get-tuple-element.62), channel_id=1, source_target_pairs={{0,24},{8,16},{16,8},{24,0},{1,25},{9,17},{17,9},{25,1},{2,26},{10... | collective-permute-start | bytes 393224 | tf_op jit(solution)/shard_map/ppermute | solution.py:362
  56.3 1.2 collective-permute-start.9
  71.6 1.7 collective-permute-start.10
  71.9 1.6 collective-permute-start.11
  74.1 14.2 %collective-permute-start.15 = (bf16[128,2048]{1,0:T(8,128)(2,1)S(1)}, bf16[128,2048]{1,0:T(8,128)(2,1)S(1)}, u32[]{:S(2)}, u32[]{:S(2)}) collective-permute-start(bf16[128,2048]{1,0:T(8,128)(2,1)S(1)} %after.5), channel_id=1, source_target_pairs={{0,8},{8,0},{16,24},{24,16},{1,9},{9,1},{17,25},{25,17},{2,10},{10... | collective-permute-start | bytes 1572872 | tf_op jit(solution)/shard_map/ppermute | solution.py:435
  75.6 19.3 %collective-permute-start.24 = (bf16[128,2048]{1,0:T(8,128)(2,1)S(1)}, bf16[128,2048]{1,0:T(8,128)(2,1)S(1)}, u32[]{:S(2)}, u32[]{:S(2)}) collective-permute-start(bf16[128,2048]{1,0:T(8,128)(2,1)S(1)} %after.5), channel_id=1, source_target_pairs={{8,16},{16,8},{9,17},{17,9},{10,18},{18,10},{11,19},{19,11},{12,20... | collective-permute-start | bytes 1572872 | tf_op jit(solution)/shard_map/ppermute | solution.py:435
  76.3 12.1 %collective-permute-start.12 = (bf16[80,2048]{1,0:T(8,128)(2,1)S(1)}, bf16[80,2048]{1,0:T(8,128)(2,1)S(1)}, u32[]{:S(2)}, u32[]{:S(2)}) collective-permute-start(bf16[80,2048]{1,0:T(8,128)(2,1)S(1)} %get-tuple-element.66), channel_id=1, source_target_pairs={{0,2},{1,3},{2,0},{3,1},{4,6},{5,7},{6,4},{7,5},{8,10},{9,11},{10,... | collective-permute-start | bytes 983048 | tf_op jit(solution)/shard_map/ppermute | solution.py:365
  77.9 16.3 %collective-permute-start.13 = (bf16[80,2048]{1,0:T(8,128)(2,1)S(1)}, bf16[80,2048]{1,0:T(8,128)(2,1)S(1)}, u32[]{:S(2)}, u32[]{:S(2)}) collective-permute-start(bf16[80,2048]{1,0:T(8,128)(2,1)S(1)} %get-tuple-element.67), channel_id=1, source_target_pairs={{0,4},{1,5},{2,6},{3,7},{4,0},{5,1},{6,2},{7,3},{8,12},{9,13},{10,... | collective-permute-start | bytes 983048 | tf_op jit(solution)/shard_map/ppermute | solution.py:365
  79.1 17.1 %collective-permute-start.14 = (bf16[80,2048]{1,0:T(8,128)(2,1)S(1)}, bf16[80,2048]{1,0:T(8,128)(2,1)S(1)}, u32[]{:S(2)}, u32[]{:S(2)}) collective-permute-start(bf16[80,2048]{1,0:T(8,128)(2,1)S(1)} %get-tuple-element.68), channel_id=1, source_target_pairs={{0,6},{1,7},{2,4},{3,5},{4,2},{5,3},{6,0},{7,1},{8,14},{9,15},{10,... | collective-permute-start | bytes 983048 | tf_op jit(solution)/shard_map/ppermute | solution.py:365
  88.3 7.9 %collective-permute-start.16 = (bf16[64,2048]{1,0:T(8,128)(2,1)S(1)}, bf16[64,2048]{1,0:T(8,128)(2,1)S(1)}, u32[]{:S(2)}, u32[]{:S(2)}) collective-permute-start(bf16[64,2048]{1,0:T(8,128)(2,1)S(1)} %get-tuple-element.112), channel_id=1, source_target_pairs={{0,1},{1,0},{2,3},{3,2},{4,5},{5,4},{6,7},{7,6},{8,9},{9,8},{10,11... | collective-permute-start | bytes 786440 | tf_op jit(solution)/shard_map/ppermute | solution.py:368
  88.4 7.8 %collective-permute-start.17 = (bf16[64,2048]{1,0:T(8,128)(2,1)S(1)}, bf16[64,2048]{1,0:T(8,128)(2,1)S(1)}, u32[]{:S(2)}, u32[]{:S(2)}) collective-permute-start(bf16[64,2048]{1,0:T(8,128)(2,1)S(1)} %get-tuple-element.111), channel_id=1, source_target_pairs={{0,1},{1,0},{2,3},{3,2},{4,5},{5,4},{6,7},{7,6},{8,9},{9,8},{10,11... | collective-permute-start | bytes 786440 | tf_op jit(solution)/shard_map/ppermute | solution.py:368
  94.2 15.6 %collective-permute-start.31 = (bf16[128,2048]{1,0:T(8,128)(2,1)S(1)}, bf16[128,2048]{1,0:T(8,128)(2,1)S(1)}, u32[]{:S(2)}, u32[]{:S(2)}) collective-permute-start(bf16[128,2048]{1,0:T(8,128)(2,1)S(1)} %collective-permute-done.15.mine_ref), channel_id=1, source_target_pairs={{8,16},{16,8},{9,17},{17,9},{10,18},{18,10},{11,19},{19,11},{12,20... | collective-permute-start | bytes 1572872 | tf_op jit(solution)/shard_map/ppermute | solution.py:435
  94.9 14.7 %collective-permute-start.25 = (bf16[128,2048]{1,0:T(8,128)(2,1)S(1)}, bf16[128,2048]{1,0:T(8,128)(2,1)S(1)}, u32[]{:S(2)}, u32[]{:S(2)}) collective-permute-start(bf16[128,2048]{1,0:T(8,128)(2,1)S(1)} %collective-permute-done.24.__0_), channel_id=1, source_target_pairs={{8,0},{16,24},{9,1},{17,25},{10,2},{18,26},{11,3},{19,27},{12,4},{... | collective-permute-start | bytes 1572872 | tf_op jit(solution)/shard_map/ppermute | solution.py:435
  96.7 17.5 %collective-permute-start.21 = (bf16[80,2048]{1,0:T(8,128)(2,1)S(1)}, bf16[80,2048]{1,0:T(8,128)(2,1)S(1)}, u32[]{:S(2)}, u32[]{:S(2)}) collective-permute-start(bf16[80,2048]{1,0:T(8,128)(2,1)S(1)} %get-tuple-element.74), channel_id=1, source_target_pairs={{0,2},{1,3},{2,0},{3,1},{4,6},{5,7},{6,4},{7,5},{8,10},{9,11},{10,... | collective-permute-start | bytes 983048 | tf_op jit(solution)/shard_map/ppermute | solution.py:365
  96.8 18.6 %collective-permute-start.22 = (bf16[80,2048]{1,0:T(8,128)(2,1)S(1)}, bf16[80,2048]{1,0:T(8,128)(2,1)S(1)}, u32[]{:S(2)}, u32[]{:S(2)}) collective-permute-start(bf16[80,2048]{1,0:T(8,128)(2,1)S(1)} %get-tuple-element.75), channel_id=1, source_target_pairs={{0,4},{1,5},{2,6},{3,7},{4,0},{5,1},{6,2},{7,3},{8,12},{9,13},{10,... | collective-permute-start | bytes 983048 | tf_op jit(solution)/shard_map/ppermute | solution.py:365
  98.0 19.7 %collective-permute-start.23 = (bf16[80,2048]{1,0:T(8,128)(2,1)S(1)}, bf16[80,2048]{1,0:T(8,128)(2,1)S(1)}, u32[]{:S(2)}, u32[]{:S(2)}) collective-permute-start(bf16[80,2048]{1,0:T(8,128)(2,1)S(1)} %get-tuple-element.76), channel_id=1, source_target_pairs={{0,6},{1,7},{2,4},{3,5},{4,2},{5,3},{6,0},{7,1},{8,14},{9,15},{10,... | collective-permute-start | bytes 983048 | tf_op jit(solution)/shard_map/ppermute | solution.py:365
  109.7 1.6 collective-permute-start.26
  109.8 3.0 %collective-permute-start.27 = (bf16[64,2048]{1,0:T(8,128)(2,1)S(1)}, bf16[64,2048]{1,0:T(8,128)(2,1)S(1)}, u32[]{:S(2)}, u32[]{:S(2)}) collective-permute-start(bf16[64,2048]{1,0:T(8,128)(2,1)S(1)} %get-tuple-element.109), channel_id=1, source_target_pairs={{0,1},{1,0},{2,3},{3,2},{4,5},{5,4},{6,7},{7,6},{8,9},{9,8},{10,11... | collective-permute-start | bytes 786440 | tf_op jit(solution)/shard_map/ppermute | solution.py:368
  111.3 18.9 %collective-permute-start.32 = (bf16[128,2048]{1,0:T(8,128)(2,1)S(1)}, bf16[128,2048]{1,0:T(8,128)(2,1)S(1)}, u32[]{:S(2)}, u32[]{:S(2)}) collective-permute-start(bf16[128,2048]{1,0:T(8,128)(2,1)S(1)} %collective-permute-done.31.__0_), channel_id=1, source_target_pairs={{8,0},{16,24},{9,1},{17,25},{10,2},{18,26},{11,3},{19,27},{12,4},{... | collective-permute-start | bytes 1572872 | tf_op jit(solution)/shard_map/ppermute | solution.py:435
  114.2 12.8 %copy-start.11 = (bf16[80,2048]{1,0:T(8,128)(2,1)}, bf16[80,2048]{1,0:T(8,128)(2,1)S(1)}, u32[]{:S(2)}) copy-start(bf16[80,2048]{1,0:T(8,128)(2,1)S(1)} %get-tuple-element.77.refs_7_.refs_0_) | copy-start | bytes 983044
  114.2 20.3 %collective-permute-start.38 = (bf16[80,2048]{1,0:T(8,128)(2,1)}, bf16[80,2048]{1,0:T(8,128)(2,1)}, u32[]{:S(2)}, u32[]{:S(2)}) collective-permute-start(bf16[80,2048]{1,0:T(8,128)(2,1)} %get-tuple-element.86), channel_id=1, source_target_pairs={{0,2},{1,3},{2,0},{3,1},{4,6},{5,7},{6,4},{7,5},{8,10},{9,11},{10,... | collective-permute-start | bytes 983048 | tf_op jit(solution)/shard_map/ppermute | solution.py:365
  114.3 23.1 %collective-permute-start.39 = (bf16[80,2048]{1,0:T(8,128)(2,1)}, bf16[80,2048]{1,0:T(8,128)(2,1)}, u32[]{:S(2)}, u32[]{:S(2)}) collective-permute-start(bf16[80,2048]{1,0:T(8,128)(2,1)} %get-tuple-element.87), channel_id=1, source_target_pairs={{0,4},{1,5},{2,6},{3,7},{4,0},{5,1},{6,2},{7,3},{8,12},{9,13},{10,... | collective-permute-start | bytes 983048 | tf_op jit(solution)/shard_map/ppermute | solution.py:365
  115.5 21.9 %collective-permute-start.40 = (bf16[80,2048]{1,0:T(8,128)(2,1)}, bf16[80,2048]{1,0:T(8,128)(2,1)}, u32[]{:S(2)}, u32[]{:S(2)}) collective-permute-start(bf16[80,2048]{1,0:T(8,128)(2,1)} %get-tuple-element.88), channel_id=1, source_target_pairs={{0,6},{1,7},{2,4},{3,5},{4,2},{5,3},{6,0},{7,1},{8,14},{9,15},{10,... | collective-permute-start | bytes 983048 | tf_op jit(solution)/shard_map/ppermute | solution.py:365
  131.1 1.7 collective-permute-start.33
  131.2 2.1 collective-permute-start.34
  133.8 15.7 %collective-permute-start.35 = (bf16[80,2048]{1,0:T(8,128)(2,1)S(1)}, bf16[80,2048]{1,0:T(8,128)(2,1)S(1)}, u32[]{:S(2)}, u32[]{:S(2)}) collective-permute-start(bf16[80,2048]{1,0:T(8,128)(2,1)S(1)} %get-tuple-element.83), channel_id=1, source_target_pairs={{0,2},{1,3},{2,0},{3,1},{4,6},{5,7},{6,4},{7,5},{8,10},{9,11},{10,... | collective-permute-start | bytes 983048 | tf_op jit(solution)/shard_map/ppermute | solution.py:365
  134.4 17.9 %collective-permute-start.36 = (bf16[80,2048]{1,0:T(8,128)(2,1)S(1)}, bf16[80,2048]{1,0:T(8,128)(2,1)S(1)}, u32[]{:S(2)}, u32[]{:S(2)}) collective-permute-start(bf16[80,2048]{1,0:T(8,128)(2,1)S(1)} %get-tuple-element.84), channel_id=1, source_target_pairs={{0,4},{1,5},{2,6},{3,7},{4,0},{5,1},{6,2},{7,3},{8,12},{9,13},{10,... | collective-permute-start | bytes 983048 | tf_op jit(solution)/shard_map/ppermute | solution.py:365
  134.5 17.8 %collective-permute-start.37 = (bf16[80,2048]{1,0:T(8,128)(2,1)S(1)}, bf16[80,2048]{1,0:T(8,128)(2,1)S(1)}, u32[]{:S(2)}, u32[]{:S(2)}) collective-permute-start(bf16[80,2048]{1,0:T(8,128)(2,1)S(1)} %get-tuple-element.85), channel_id=1, source_target_pairs={{0,6},{1,7},{2,4},{3,5},{4,2},{5,3},{6,0},{7,1},{8,14},{9,15},{10,... | collective-permute-start | bytes 983048 | tf_op jit(solution)/shard_map/ppermute | solution.py:365
  148.7 13.0 %collective-permute-start.44 = (bf16[80,2048]{1,0:T(8,128)(2,1)S(1)}, bf16[80,2048]{1,0:T(8,128)(2,1)S(1)}, u32[]{:S(2)}, u32[]{:S(2)}) collective-permute-start(bf16[80,2048]{1,0:T(8,128)(2,1)S(1)} %get-tuple-element.94), channel_id=1, source_target_pairs={{0,2},{1,3},{2,0},{3,1},{4,6},{5,7},{6,4},{7,5},{8,10},{9,11},{10,... | collective-permute-start | bytes 983048 | tf_op jit(solution)/shard_map/ppermute | solution.py:365
  149.4 15.7 %collective-permute-start.45 = (bf16[80,2048]{1,0:T(8,128)(2,1)S(1)}, bf16[80,2048]{1,0:T(8,128)(2,1)S(1)}, u32[]{:S(2)}, u32[]{:S(2)}) collective-permute-start(bf16[80,2048]{1,0:T(8,128)(2,1)S(1)} %get-tuple-element.95), channel_id=1, source_target_pairs={{0,4},{1,5},{2,6},{3,7},{4,0},{5,1},{6,2},{7,3},{8,12},{9,13},{10,... | collective-permute-start | bytes 983048 | tf_op jit(solution)/shard_map/ppermute | solution.py:365
  149.4 15.6 %collective-permute-start.46 = (bf16[80,2048]{1,0:T(8,128)(2,1)S(1)}, bf16[80,2048]{1,0:T(8,128)(2,1)S(1)}, u32[]{:S(2)}, u32[]{:S(2)}) collective-permute-start(bf16[80,2048]{1,0:T(8,128)(2,1)S(1)} %get-tuple-element.96), channel_id=1, source_target_pairs={{0,6},{1,7},{2,4},{3,5},{4,2},{5,3},{6,0},{7,1},{8,14},{9,15},{10,... | collective-permute-start | bytes 983048 | tf_op jit(solution)/shard_map/ppermute | solution.py:365
  166.8 3.6 %collective-permute-start.47 = (bf16[128,2048]{1,0:T(8,128)(2,1)S(1)}, bf16[128,2048]{1,0:T(8,128)(2,1)S(1)}, u32[]{:S(2)}, u32[]{:S(2)}) collective-permute-start(bf16[128,2048]{1,0:T(8,128)(2,1)S(1)} %get-tuple-element.98), channel_id=1, source_target_pairs={{0,1},{1,0},{2,3},{3,2},{4,5},{5,4},{6,7},{7,6},{8,9},{9,8},{10,11... | collective-permute-start | bytes 1572872 | tf_op jit(solution)/shard_map/ppermute | solution.py:368
  166.9 10.6 %collective-permute-start.41 = (bf16[80,2048]{1,0:T(8,128)(2,1)S(1)}, bf16[80,2048]{1,0:T(8,128)(2,1)S(1)}, u32[]{:S(2)}, u32[]{:S(2)}) collective-permute-start(bf16[80,2048]{1,0:T(8,128)(2,1)S(1)} %get-tuple-element.91), channel_id=1, source_target_pairs={{0,2},{1,3},{2,0},{3,1},{4,6},{5,7},{6,4},{7,5},{8,10},{9,11},{10,... | collective-permute-start | bytes 983048 | tf_op jit(solution)/shard_map/ppermute | solution.py:365
  168.4 16.8 %collective-permute-start.42 = (bf16[80,2048]{1,0:T(8,128)(2,1)S(1)}, bf16[80,2048]{1,0:T(8,128)(2,1)S(1)}, u32[]{:S(2)}, u32[]{:S(2)}) collective-permute-start(bf16[80,2048]{1,0:T(8,128)(2,1)S(1)} %get-tuple-element.92), channel_id=1, source_target_pairs={{0,4},{1,5},{2,6},{3,7},{4,0},{5,1},{6,2},{7,3},{8,12},{9,13},{10,... | collective-permute-start | bytes 983048 | tf_op jit(solution)/shard_map/ppermute | solution.py:365
  169.0 16.3 %collective-permute-start.43 = (bf16[80,2048]{1,0:T(8,128)(2,1)S(1)}, bf16[80,2048]{1,0:T(8,128)(2,1)S(1)}, u32[]{:S(2)}, u32[]{:S(2)}) collective-permute-start(bf16[80,2048]{1,0:T(8,128)(2,1)S(1)} %get-tuple-element.93), channel_id=1, source_target_pairs={{0,6},{1,7},{2,4},{3,5},{4,2},{5,3},{6,0},{7,1},{8,14},{9,15},{10,... | collective-permute-start | bytes 983048 | tf_op jit(solution)/shard_map/ppermute | solution.py:365
  170.5 16.5 %copy-start.10 = (bf16[80,2048]{1,0:T(8,128)(2,1)S(1)}, bf16[80,2048]{1,0:T(8,128)(2,1)}, u32[]{:S(2)}) copy-start(bf16[80,2048]{1,0:T(8,128)(2,1)} %copy-done.9) | copy-start | bytes 983044
  170.6 17.1 %copy-start.8 = (bf16[80,2048]{1,0:T(8,128)(2,1)S(1)}, bf16[80,2048]{1,0:T(8,128)(2,1)}, u32[]{:S(2)}) copy-start(bf16[80,2048]{1,0:T(8,128)(2,1)} %copy-done.7) | copy-start | bytes 983044
  170.6 18.3 %copy-start.6 = (bf16[80,2048]{1,0:T(8,128)(2,1)S(1)}, bf16[80,2048]{1,0:T(8,128)(2,1)}, u32[]{:S(2)}) copy-start(bf16[80,2048]{1,0:T(8,128)(2,1)} %copy-done.5) | copy-start | bytes 983044
  170.6 20.1 %collective-permute-start.49 = (bf16[128,2048]{1,0:T(8,128)(2,1)S(1)}, bf16[128,2048]{1,0:T(8,128)(2,1)S(1)}, u32[]{:S(2)}, u32[]{:S(2)}) collective-permute-start(bf16[128,2048]{1,0:T(8,128)(2,1)S(1)} %fusion.refs_4_), channel_id=1, source_target_pairs={{0,8},{24,16},{1,9},{25,17},{2,10},{26,18},{3,11},{27,19},{4,12},{... | collective-permute-start | bytes 1572872 | tf_op jit(solution)/shard_map/ppermute | solution.py:435
  187.0 3.8 %collective-permute-start.48 = (bf16[128,2048]{1,0:T(8,128)(2,1)S(1)}, bf16[128,2048]{1,0:T(8,128)(2,1)S(1)}, u32[]{:S(2)}, u32[]{:S(2)}) collective-permute-start(bf16[128,2048]{1,0:T(8,128)(2,1)S(1)} %get-tuple-element.100), channel_id=1, source_target_pairs={{0,1},{1,0},{2,3},{3,2},{4,5},{5,4},{6,7},{7,6},{8,9},{9,8},{10,11... | collective-permute-start | bytes 1572872 | tf_op jit(solution)/shard_map/ppermute | solution.py:368
  187.1 10.6 %collective-permute-start.28 = (bf16[80,2048]{1,0:T(8,128)(2,1)S(1)}, bf16[80,2048]{1,0:T(8,128)(2,1)S(1)}, u32[]{:S(2)}, u32[]{:S(2)}) collective-permute-start(bf16[80,2048]{1,0:T(8,128)(2,1)S(1)} %copy-done.10), channel_id=1, source_target_pairs={{0,2},{1,3},{2,0},{3,1},{4,6},{5,7},{6,4},{7,5},{8,10},{9,11},{10,... | collective-permute-start | bytes 983048 | tf_op jit(solution)/shard_map/ppermute | solution.py:365
  187.7 16.8 %collective-permute-start.29 = (bf16[80,2048]{1,0:T(8,128)(2,1)S(1)}, bf16[80,2048]{1,0:T(8,128)(2,1)S(1)}, u32[]{:S(2)}, u32[]{:S(2)}) collective-permute-start(bf16[80,2048]{1,0:T(8,128)(2,1)S(1)} %copy-done.8), channel_id=1, source_target_pairs={{0,4},{1,5},{2,6},{3,7},{4,0},{5,1},{6,2},{7,3},{8,12},{9,13},{10,... | collective-permute-start | bytes 983048 | tf_op jit(solution)/shard_map/ppermute | solution.py:365
  188.9 15.6 %collective-permute-start.30 = (bf16[80,2048]{1,0:T(8,128)(2,1)S(1)}, bf16[80,2048]{1,0:T(8,128)(2,1)S(1)}, u32[]{:S(2)}, u32[]{:S(2)}) collective-permute-start(bf16[80,2048]{1,0:T(8,128)(2,1)S(1)} %copy-done.6), channel_id=1, source_target_pairs={{0,6},{1,7},{2,4},{3,5},{4,2},{5,3},{6,0},{7,1},{8,14},{9,15},{10,... | collective-permute-start | bytes 983048 | tf_op jit(solution)/shard_map/ppermute | solution.py:365
  191.0 19.7 %copy-start.4 = (bf16[80,2048]{1,0:T(8,128)(2,1)S(1)}, bf16[80,2048]{1,0:T(8,128)(2,1)}, u32[]{:S(2)}) copy-start(bf16[80,2048]{1,0:T(8,128)(2,1)} %copy-done.3) | copy-start | bytes 983044
  206.3 6.7 %collective-permute-start.50 = (bf16[128,2048]{1,0:T(8,128)(2,1)S(1)}, bf16[128,2048]{1,0:T(8,128)(2,1)S(1)}, u32[]{:S(2)}, u32[]{:S(2)}) collective-permute-start(bf16[128,2048]{1,0:T(8,128)(2,1)S(1)} %get-tuple-element.102), channel_id=1, source_target_pairs={{0,1},{1,0},{2,3},{3,2},{4,5},{5,4},{6,7},{7,6},{8,9},{9,8},{10,11... | collective-permute-start | bytes 1572872 | tf_op jit(solution)/shard_map/ppermute | solution.py:368
  206.4 16.5 %collective-permute-start.53 = (bf16[128,2048]{1,0:T(8,128)(2,1)S(1)}, bf16[128,2048]{1,0:T(8,128)(2,1)S(1)}, u32[]{:S(2)}, u32[]{:S(2)}) collective-permute-start(bf16[128,2048]{1,0:T(8,128)(2,1)S(1)} %fusion.1.refs_4_), channel_id=1, source_target_pairs={{0,8},{24,16},{1,9},{25,17},{2,10},{26,18},{3,11},{27,19},{4,12},{... | collective-permute-start | bytes 1572872 | tf_op jit(solution)/shard_map/ppermute | solution.py:435
  210.7 14.9 %collective-permute-start.18 = (bf16[80,2048]{1,0:T(8,128)(2,1)S(1)}, bf16[80,2048]{1,0:T(8,128)(2,1)S(1)}, u32[]{:S(2)}, u32[]{:S(2)}) collective-permute-start(bf16[80,2048]{1,0:T(8,128)(2,1)S(1)} %copy-done.4), channel_id=1, source_target_pairs={{0,2},{1,3},{2,0},{3,1},{4,6},{5,7},{6,4},{7,5},{8,10},{9,11},{10,... | collective-permute-start | bytes 983048 | tf_op jit(solution)/shard_map/ppermute | solution.py:365
  212.2 28.1 %collective-permute-start.52 = (bf16[128,2048]{1,0:T(8,128)(2,1)S(1)}, bf16[128,2048]{1,0:T(8,128)(2,1)S(1)}, u32[]{:S(2)}, u32[]{:S(2)}) collective-permute-start(bf16[128,2048]{1,0:T(8,128)(2,1)S(1)} %add_convert_fusion.3.refs_5_), channel_id=1, source_target_pairs={{8,16},{16,8},{9,17},{17,9},{10,18},{18,10},{11,19},{19,11},{12,20... | collective-permute-start | bytes 1572872 | tf_op jit(solution)/shard_map/ppermute | solution.py:435
  213.1 27.3 %collective-permute-start.51 = (bf16[128,2048]{1,0:T(8,128)(2,1)S(1)}, bf16[128,2048]{1,0:T(8,128)(2,1)S(1)}, u32[]{:S(2)}, u32[]{:S(2)}) collective-permute-start(bf16[128,2048]{1,0:T(8,128)(2,1)S(1)} %add_convert_fusion.2), channel_id=1, source_target_pairs={{0,8},{8,0},{16,24},{24,16},{1,9},{9,1},{17,25},{25,17},{2,10},{10... | collective-permute-start | bytes 1572872 | tf_op jit(solution)/shard_map/ppermute | solution.py:435
  223.1 17.3 %collective-permute-start.54 = (bf16[128,2048]{1,0:T(8,128)(2,1)S(1)}, bf16[128,2048]{1,0:T(8,128)(2,1)S(1)}, u32[]{:S(2)}, u32[]{:S(2)}) collective-permute-start(bf16[128,2048]{1,0:T(8,128)(2,1)S(1)} %add_convert_fusion.1), channel_id=1, source_target_pairs={{8,24},{16,0},{9,25},{17,1},{10,26},{18,2},{11,27},{19,3},{12,28},... | collective-permute-start | bytes 1572872 | tf_op jit(solution)/shard_map/ppermute | solution.py:435
  224.4 16.0 %collective-permute-start.19 = (bf16[80,2048]{1,0:T(8,128)(2,1)S(1)}, bf16[80,2048]{1,0:T(8,128)(2,1)S(1)}, u32[]{:S(2)}, u32[]{:S(2)}) collective-permute-start(bf16[80,2048]{1,0:T(8,128)(2,1)S(1)} %get-tuple-element.72), channel_id=1, source_target_pairs={{0,4},{1,5},{2,6},{3,7},{4,0},{5,1},{6,2},{7,3},{8,12},{9,13},{10,... | collective-permute-start | bytes 983048 | tf_op jit(solution)/shard_map/ppermute | solution.py:365
  225.6 14.8 %collective-permute-start.20 = (bf16[80,2048]{1,0:T(8,128)(2,1)S(1)}, bf16[80,2048]{1,0:T(8,128)(2,1)S(1)}, u32[]{:S(2)}, u32[]{:S(2)}) collective-permute-start(bf16[80,2048]{1,0:T(8,128)(2,1)S(1)} %get-tuple-element.73), channel_id=1, source_target_pairs={{0,6},{1,7},{2,4},{3,5},{4,2},{5,3},{6,0},{7,1},{8,14},{9,15},{10,... | collective-permute-start | bytes 983048 | tf_op jit(solution)/shard_map/ppermute | solution.py:365
  242.2 2.0 collective-permute-start.55
  (8 other events, 42.4 us)
Sparse Core Ops, SparseCore 0:
  9.2 57.0 all-gather.1

commit v3 on v2

--- a/solution.py
+++ b/solution.py
@@ -431,6 +431,9 @@
         total = mine + over_cores(other).astype(jnp.float32)
         return total, total.astype(jnp.bfloat16)
 
+    def joined(total, received):
+        return (total + received.astype(jnp.float32)).astype(jnp.bfloat16)
+
     def hop_along(value, pairs):
         return lax.ppermute(value, "seq", pairs)
 
@@ -440,7 +443,7 @@
     pair_block = hop_along(normed_out, PAIRS)
     cross_block = hop_along(normed_out, CROSS)
     cross_pair = hop_along(pair_block, CROSS)
-    arrived[1], own1 = dispatch(1, pair_block, arrived[0])
+    arrived[1], own1 = dispatch(1, pair_block, arrived[0][1:2])
     done0 = run(0, [own1])
     (kept,) = after([cross_block], [done0[0]])
     second = jnp.where(in_middle, kept, hop_along(cross_block, OUT))
@@ -453,15 +456,15 @@
     done3 = run(3, [done2[0]])
     total2, send2 = give_back(2, done2, [], [done3[0]])
     in2 = hop_along(send2, IN)
+    next2 = joined(total2, in2)
+    back2 = hop_along(next2, CROSS)
     total3, send3 = give_back(3, done3, [], [send2])
     in3 = hop_along(send3, IN)
-    send2 = (total2 + in2.astype(jnp.float32)).astype(jnp.bfloat16)
-    back2 = hop_along(send2, CROSS)
-    total1, send1 = give_back(1, done1, [], [send3, send2])
+    next3 = joined(total3, in3)
+    back3 = hop_along(next3, FAR)
+    total1, send1 = give_back(1, done1, [], [send3, next2])
     back1 = hop_along(send1, PAIRS)
-    send3 = (total3 + in3.astype(jnp.float32)).astype(jnp.bfloat16)
-    back3 = hop_along(send3, FAR)
-    result, _ = give_back(0, done0, [], [back1, back2, back3])
+    result, _ = give_back(0, done0, [], [send1])
     result = mid_float + result
     for back in (back1, back2, back3):
         result = result + back.astype(jnp.float32)

time: 253 us -> 248 us (0.980)
  waiting for transfers between devices: 101 us -> 96.3 us
    ppermute x24, waiting for transfers between devices: 45.3 us -> 33 us  [over_chips(): return lax.ppermute(value, 'exp', xor_pairs(expert_count, 2 * step))]
    ppermute x10, waiting for transfers between devices: 19.1 us -> 28.2 us  [hop_along(): return lax.ppermute(value, 'seq', pairs)]
  transfers between devices with their start and end apart: 57 -> 57, of which waited for: 21 -> 24; matrix products, arithmetic and copies ran while one was open for 2% -> 2% of each run, Pallas kernels for 19% -> 20%
where the time goes in v3:
time: 248 us
  waiting for transfers between devices  96.3 us (39%)
  starting transfers between devices  71.3 us (29%)
  Pallas kernels  58 us (23%)
  between operations  14.1 us (6%)
  local copies, waits for them, and re-layouts  4.91 us (2%)
  other arithmetic  3.36 us (1%)
    pallas_call x4, Pallas kernels, expert(): pl.pallas_call(functools.partial(expert_kernel, chips, len(deps)), in_spe...  38.4 us
    ppermute x24, waiting for transfers between devices, over_chips(): return lax.ppermute(value, 'exp', xor_pairs(expert_count, 2 * step))  33 us
    ppermute x9, waiting for transfers between devices, over_seq(): return lax.ppermute(value, 'seq', xor_pairs(seq_count, hop))  29.4 us
    ppermute x10, waiting for transfers between devices, hop_along(): return lax.ppermute(value, 'seq', pairs)  28.2 us
    ppermute x24, starting transfers between devices, over_chips(): return lax.ppermute(value, 'exp', xor_pairs(expert_count, 2 * step))  27.5 us
    ppermute x10, starting transfers between devices, hop_along(): return lax.ppermute(value, 'seq', pairs)  21 us
    ppermute x9, starting transfers between devices, over_seq(): return lax.ppermute(value, 'seq', xor_pairs(seq_count, hop))  20.2 us
    pallas_call x4, Pallas kernels, combine(): pl.pallas_call(functools.partial(combine_kernel, hop, chips, len(deps)),...  7.06 us
  transfers between devices with their start and end apart: 57, of which 24 were waited for; matrix products, arithmetic and copies ran while one was open for 2% of the time, Pallas kernels for 20%

profile of v3, /device:TPU:0, one launch (start us, length us, event | category | flops | bytes accessed | tf_op | source)
XLA Modules:
  0.0 247.8 jit_solution(13298234752273644040)
XLA Ops:
  7.3 1.4 copy-done
  9.2 3.1 %collective-permute-start = (bf16[128,1536]{1,0:T(8,128)(2,1)S(1)}, bf16[128,1536]{1,0:T(8,128)(2,1)S(1)}, u32[]{:S(2)}, u32[]{:S(2)}) collective-permute-start(bf16[128,1536]{1,0:T(8,128)(2,1)S(1)} %get-tuple-element.56), channel_id=1, source_target_pairs={{0,8},{8,0},{16,24},{24,16},{1,9},{9,1},{17,25},{25,17},{2,10},{10... | collective-permute-start | bytes 1179656 | tf_op jit(solution)/shard_map/ppermute | solution.py:362
  12.3 2.6 %collective-permute-start.1 = (bf16[128,1536]{1,0:T(8,128)(2,1)S(1)}, bf16[128,1536]{1,0:T(8,128)(2,1)S(1)}, u32[]{:S(2)}, u32[]{:S(2)}) collective-permute-start(bf16[128,1536]{1,0:T(8,128)(2,1)S(1)} %get-tuple-element.57), channel_id=1, source_target_pairs={{0,16},{8,24},{16,0},{24,8},{1,17},{9,25},{17,1},{25,9},{2,18},{10... | collective-permute-start | bytes 1179656 | tf_op jit(solution)/shard_map/ppermute | solution.py:362
  16.5 12.5 %collective-permute-done.refs_1_.refs_5_.refs_9_.__1_ = bf16[128,1536]{1,0:T(8,128)(2,1)S(1)} collective-permute-done((bf16[128,1536]{1,0:T(8,128)(2,1)S(1)}, bf16[128,1536]{1,0:T(8,128)(2,1)S(1)}, u32[]{:S(2)}, u32[]{:S(2)}) %collective-permute-start) | collective-permute-done | bytes 393248 | tf_op jit(solution)/shard_map/ppermute | solution.py:362
  29.1 3.2 %collective-permute-start.7 = (f32[4,128]{1,0:T(4,128)S(1)}, f32[4,128]{1,0:T(4,128)S(1)}, u32[]{:S(2)}, u32[]{:S(2)}) collective-permute-start(f32[4,128]{1,0:T(4,128)S(1)} %after.4), channel_id=1, source_target_pairs={{0,24},{8,16},{16,8},{24,0},{1,25},{9,17},{17,9},{25,1},{2,26},{10... | collective-permute-start | bytes 6152 | tf_op jit(solution)/shard_map/ppermute | solution.py:362
  32.3 1.2 collective-permute-start.6
  33.5 8.7 %collective-permute-done.1.refs_2_.refs_6_.refs_10_ = bf16[128,1536]{1,0:T(8,128)(2,1)S(1)} collective-permute-done((bf16[128,1536]{1,0:T(8,128)(2,1)S(1)}, bf16[128,1536]{1,0:T(8,128)(2,1)S(1)}, u32[]{:S(2)}, u32[]{:S(2)}) %collective-permute-start.1) | collective-permute-done | bytes 393248 | tf_op jit(solution)/shard_map/ppermute | solution.py:362
  42.2 3.9 %attend.1 = (bf16[128,512]{1,0:T(8,128)(2,1)S(1)}, bf16[128,512]{1,0:T(8,128)(2,1)S(1)}, bf16[128,512]{1,0:T(8,128)(2,1)S(1)}, bf16[128,512]{1,0:T(8,128)(2,1)S(1)}) custom-call(bf16[128,1536]{1,0:T(8,128)(2,1)S(1)} %get-tuple-element.55.refs_0_.refs_4_.refs_8_, bf16[128,1536]{1,0:T(8,128)(2,1)S(1)} %collective-permute-done.refs_1_.refs_5_.refs_9_.__1_, ...), custom_call_target="tpu_custom_call" | custom-call | flops 536870912 | bytes 2097152 | tf_op jit(solution)/shard_map/attend/pallas_call | solution.py:113
  46.1 7.7 %collective-permute-start.3 = (bf16[128,512]{1,0:T(8,128)(2,1)S(1)}, bf16[128,512]{1,0:T(8,128)(2,1)S(1)}, u32[]{:S(2)}, u32[]{:S(2)}) collective-permute-start(bf16[128,512]{1,0:T(8,128)(2,1)S(1)} %get-tuple-element.60), channel_id=1, source_target_pairs={{0,8},{8,0},{16,24},{24,16},{1,9},{9,1},{17,25},{25,17},{2,10},{10... | collective-permute-start | bytes 393224 | tf_op jit(solution)/shard_map/ppermute | solution.py:362
  53.8 1.1 collective-permute-start.4
  54.9 1.4 collective-permute-start.5
  56.4 1.1 collective-permute-done.9
  58.0 7.6 %collective-permute-done.4.refs_2_ = bf16[128,512]{1,0:T(8,128)(2,1)S(1)} collective-permute-done((bf16[128,512]{1,0:T(8,128)(2,1)S(1)}, bf16[128,512]{1,0:T(8,128)(2,1)S(1)}, u32[]{:S(2)}, u32[]{:S(2)}) %collective-permute-start.4) | collective-permute-done | bytes 131104 | tf_op jit(solution)/shard_map/ppermute | solution.py:362
  65.6 0.8 all-gather.2.cloned.1.call-done.refs_4_
  66.4 5.1 %project.1 = (bf16[128,2048]{1,0:T(8,128)(2,1)S(1)}, bf16[128,2048]{1,0:T(8,128)(2,1)S(1)}) custom-call(s32[1]{0:T(128)} %bitcast.seq_ref, bf16[128,512]{1,0:T(8,128)(2,1)S(1)} %get-tuple-element.59.refs_0_, bf16[128,512]{1,0:T(8,128)(2,1)S(1)} %collective-permute-done.3.refs_1_, bf16[128,512]{1,0:T(8,128)(2,1)S(1)} %collective-permute-done.4.refs_2_, ...), custom_call_target="tpu_custom_call" | custom-call | flops 1073741824 | bytes 8388608 | tf_op jit(solution)/shard_map/project/pallas_call | solution.py:156
  74.1 1.6 collective-permute-start.15
  76.3 1.5 collective-permute-start.12
  77.9 1.3 collective-permute-start.13
  79.9 8.4 %collective-permute-done.15.mine_ref = bf16[128,2048]{1,0:T(8,128)(2,1)S(1)} collective-permute-done((bf16[128,2048]{1,0:T(8,128)(2,1)S(1)}, bf16[128,2048]{1,0:T(8,128)(2,1)S(1)}, u32[]{:S(2)}, u32[]{:S(2)}) %collective-permute-start.15) | collective-permute-done | bytes 524320 | tf_op jit(solution)/shard_map/ppermute | solution.py:438
  89.9 1.3 collective-permute-start.25
  91.7 1.5 collective-permute-start.21
  93.2 0.9 collective-permute-done.13.refs_2_
  94.2 1.2 collective-permute-start.22
  95.4 9.2 %expert0.1 = (bf16[80,2048]{1,0:T(8,128)(2,1)S(1)}, bf16[80,2048]{1,0:T(8,128)(2,1)S(1)}, bf16[80,2048]{1,0:T(8,128)(2,1)S(1)}, bf16[80,2048]{1,0:T(8,128)(2,1)S(1)}) custom-call(bf16[80,2048]{1,0:T(8,128)(2,1)S(1)} %get-tuple-element.65.__1_.refs_0_, bf16[80,2048]{1,0:T(8,128)(2,1)S(1)} %collective-permute-done.12.rest_2_.refs_1_, ...), custom_call_target="tpu_custom_call" | custom-call | flops 5536481280 | bytes 17301504 | tf_op jit(solution)/shard_map/expert0/pallas_call | solution.py:276
  104.6 3.8 %collective-permute-done.25 = bf16[128,2048]{1,0:T(8,128)(2,1)S(1)} collective-permute-done((bf16[128,2048]{1,0:T(8,128)(2,1)S(1)}, bf16[128,2048]{1,0:T(8,128)(2,1)S(1)}, u32[]{:S(2)}, u32[]{:S(2)}) %collective-permute-start.25) | collective-permute-done | bytes 524320 | tf_op jit(solution)/shard_map/ppermute | solution.py:438
  109.1 1.0 collective-permute-done.26.rest_0_
  110.1 1.5 collective-permute-start.32
  111.6 1.4 slots2.1
  113.0 1.5 collective-permute-start.38
  115.1 1.5 collective-permute-start.40
  116.6 9.2 %expert1.1 = (bf16[80,2048]{1,0:T(8,128)(2,1)S(1)}, bf16[80,2048]{1,0:T(8,128)(2,1)S(1)}, bf16[80,2048]{1,0:T(8,128)(2,1)S(1)}, bf16[80,2048]{1,0:T(8,128)(2,1)S(1)}) custom-call(bf16[80,2048]{1,0:T(8,128)(2,1)S(1)} %get-tuple-element.69.refs_7_.refs_0_, bf16[80,2048]{1,0:T(8,128)(2,1)S(1)} %collective-permute-done.21.refs_1_, ...), custom_call_target="tpu_custom_call" | custom-call | flops 5536481280 | bytes 17301504 | tf_op jit(solution)/shard_map/expert1/pallas_call | solution.py:276
  126.2 0.9 fusion.20
  127.7 1.1 collective-permute-done.33.rest_0_
  129.7 1.5 collective-permute-start.35
  131.8 1.5 collective-permute-start.37
  133.2 1.0 copy-done.12
  134.2 10.4 %expert2.1 = (bf16[80,2048]{1,0:T(8,128)(2,1)S(1)}, bf16[80,2048]{1,0:T(8,128)(2,1)S(1)}, bf16[80,2048]{1,0:T(8,128)(2,1)S(1)}, bf16[80,2048]{1,0:T(8,128)(2,1)S(1)}) custom-call(bf16[80,2048]{1,0:T(8,128)(2,1)S(1)} %copy-done.12, bf16[80,2048]{1,0:T(8,128)(2,1)} %collective-permute-done.38.refs_1_, bf16[80,2048]{1,0:T(8,128)(2,1)} %collective-permute-done.39.refs_2_, ...), custom_call_target="tpu_custom_call" | custom-call | flops 5536481280 | bytes 17301504 | tf_op jit(solution)/shard_map/expert2/pallas_call | solution.py:276
  144.6 1.5 collective-permute-start.44
  146.7 1.5 collective-permute-start.46
  148.2 9.5 %expert3.1 = (bf16[80,2048]{1,0:T(8,128)(2,1)S(1)}, bf16[80,2048]{1,0:T(8,128)(2,1)S(1)}, bf16[80,2048]{1,0:T(8,128)(2,1)S(1)}, bf16[80,2048]{1,0:T(8,128)(2,1)S(1)}) custom-call(bf16[80,2048]{1,0:T(8,128)(2,1)S(1)} %get-tuple-element.82.refs_7_.refs_0_, bf16[80,2048]{1,0:T(8,128)(2,1)S(1)} %collective-permute-done.35.refs_1_, ...), custom_call_target="tpu_custom_call" | custom-call | flops 5536481280 | bytes 17301504 | tf_op jit(solution)/shard_map/expert3/pallas_call | solution.py:276
  157.7 4.1 %collective-permute-done.45.refs_2_ = bf16[80,2048]{1,0:T(8,128)(2,1)S(1)} collective-permute-done((bf16[80,2048]{1,0:T(8,128)(2,1)S(1)}, bf16[80,2048]{1,0:T(8,128)(2,1)S(1)}, u32[]{:S(2)}, u32[]{:S(2)}) %collective-permute-start.45) | collective-permute-done | bytes 327712 | tf_op jit(solution)/shard_map/ppermute | solution.py:365
  161.8 1.8 combine2.1
  164.3 1.2 collective-permute-start.42
  165.5 1.8 collective-permute-start.43
  167.4 4.6 %collective-permute-start.49 = (bf16[128,2048]{1,0:T(8,128)(2,1)S(1)}, bf16[128,2048]{1,0:T(8,128)(2,1)S(1)}, u32[]{:S(2)}, u32[]{:S(2)}) collective-permute-start(bf16[128,2048]{1,0:T(8,128)(2,1)S(1)} %fusion.refs_4_), channel_id=1, source_target_pairs={{0,8},{24,16},{1,9},{25,17},{2,10},{26,18},{3,11},{27,19},{4,12},{... | collective-permute-start | bytes 1572872 | tf_op jit(solution)/shard_map/ppermute | solution.py:438
  172.0 2.3 collective-permute-done.41.refs_1_
  174.3 6.8 %collective-permute-done.42.refs_2_ = bf16[80,2048]{1,0:T(8,128)(2,1)S(1)} collective-permute-done((bf16[80,2048]{1,0:T(8,128)(2,1)S(1)}, bf16[80,2048]{1,0:T(8,128)(2,1)S(1)}, u32[]{:S(2)}, u32[]{:S(2)}) %collective-permute-start.42) | collective-permute-done | bytes 327712 | tf_op jit(solution)/shard_map/ppermute | solution.py:365
  181.1 1.8 combine3.1
  183.0 1.5 collective-permute-start.28
  185.1 1.5 collective-permute-start.30
  186.8 6.7 %collective-permute-done.28.refs_1_ = bf16[80,2048]{1,0:T(8,128)(2,1)S(1)} collective-permute-done((bf16[80,2048]{1,0:T(8,128)(2,1)S(1)}, bf16[80,2048]{1,0:T(8,128)(2,1)S(1)}, u32[]{:S(2)}, u32[]{:S(2)}) %collective-permute-start.28) | collective-permute-done | bytes 327712 | tf_op jit(solution)/shard_map/ppermute | solution.py:365
  193.5 7.8 %collective-permute-done.29.refs_2_ = bf16[80,2048]{1,0:T(8,128)(2,1)S(1)} collective-permute-done((bf16[80,2048]{1,0:T(8,128)(2,1)S(1)}, bf16[80,2048]{1,0:T(8,128)(2,1)S(1)}, u32[]{:S(2)}, u32[]{:S(2)}) %collective-permute-start.29) | collective-permute-done | bytes 327712 | tf_op jit(solution)/shard_map/ppermute | solution.py:365
  201.3 1.8 combine1.1
  203.8 1.2 collective-permute-start.19
  205.0 1.8 collective-permute-start.20
  207.4 6.3 %collective-permute-start.54 = (bf16[128,2048]{1,0:T(8,128)(2,1)S(1)}, bf16[128,2048]{1,0:T(8,128)(2,1)S(1)}, u32[]{:S(2)}, u32[]{:S(2)}) collective-permute-start(bf16[128,2048]{1,0:T(8,128)(2,1)S(1)} %fusion.1.refs_4_), channel_id=1, source_target_pairs={{0,8},{24,16},{1,9},{25,17},{2,10},{26,18},{3,11},{27,19},{4,12},{... | collective-permute-start | bytes 1572872 | tf_op jit(solution)/shard_map/ppermute | solution.py:438
  213.9 2.4 collective-permute-start.52
  216.3 4.3 %collective-permute-done.19.refs_2_ = bf16[80,2048]{1,0:T(8,128)(2,1)S(1)} collective-permute-done((bf16[80,2048]{1,0:T(8,128)(2,1)S(1)}, bf16[80,2048]{1,0:T(8,128)(2,1)S(1)}, u32[]{:S(2)}, u32[]{:S(2)}) %collective-permute-start.19) | collective-permute-done | bytes 327712 | tf_op jit(solution)/shard_map/ppermute | solution.py:365
  220.6 1.8 combine0.1
  222.4 3.6 %collective-permute-done.54 = bf16[128,2048]{1,0:T(8,128)(2,1)S(1)} collective-permute-done((bf16[128,2048]{1,0:T(8,128)(2,1)S(1)}, bf16[128,2048]{1,0:T(8,128)(2,1)S(1)}, u32[]{:S(2)}, u32[]{:S(2)}) %collective-permute-start.54) | collective-permute-done | bytes 524320 | tf_op jit(solution)/shard_map/ppermute | solution.py:438
  226.3 1.3 collective-permute-start.55
  227.6 8.0 %collective-permute-done.52 = bf16[128,2048]{1,0:T(8,128)(2,1)S(1)} collective-permute-done((bf16[128,2048]{1,0:T(8,128)(2,1)S(1)}, bf16[128,2048]{1,0:T(8,128)(2,1)S(1)}, u32[]{:S(2)}, u32[]{:S(2)}) %collective-permute-start.52) | collective-permute-done | bytes 524320 | tf_op jit(solution)/shard_map/ppermute | solution.py:438
  235.6 4.2 %collective-permute-done.55 = bf16[128,2048]{1,0:T(8,128)(2,1)S(1)} collective-permute-done((bf16[128,2048]{1,0:T(8,128)(2,1)S(1)}, bf16[128,2048]{1,0:T(8,128)(2,1)S(1)}, u32[]{:S(2)}, u32[]{:S(2)}) %collective-permute-start.55) | collective-permute-done | bytes 524320 | tf_op jit(solution)/shard_map/ppermute | solution.py:438
  239.8 1.3 fusion.2
  (138 shorter events, 17.2 us)
Async XLA Ops:
  6.5 59.8 %all-gather.2.cloned.1.call-start = ((), (), s32[]{:S(2)}) async-start(), calls=%async_computation | async-start | bytes 9437184 | tf_op jit(solution)/shard_map/all_gather | solution.py:413
  8.7 57.7 %copy-start.1 = (bf16[1,128,2048]{2,1,0:T(8,128)(2,1)S(1)}, bf16[1,128,2048]{2,1,0:T(8,128)(2,1)}, u32[]{:S(2)}) copy-start(bf16[1,128,2048]{2,1,0:T(8,128)(2,1)} %param.10) | copy-start | bytes 1572868
  8.7 57.7 %copy-start.2 = (f32[2048]{0:T(1024)S(1)}, f32[2048]{0:T(1024)}, u32[]{:S(2)}) copy-start(f32[2048]{0:T(1024)} %param.12) | copy-start | bytes 24580
  9.2 19.9 %collective-permute-start = (bf16[128,1536]{1,0:T(8,128)(2,1)S(1)}, bf16[128,1536]{1,0:T(8,128)(2,1)S(1)}, u32[]{:S(2)}, u32[]{:S(2)}) collective-permute-start(bf16[128,1536]{1,0:T(8,128)(2,1)S(1)} %get-tuple-element.56), channel_id=1, source_target_pairs={{0,8},{8,0},{16,24},{24,16},{1,9},{9,1},{17,25},{25,17},{2,10},{10... | collective-permute-start | bytes 1179656 | tf_op jit(solution)/shard_map/ppermute | solution.py:362
  12.3 29.9 %collective-permute-start.1 = (bf16[128,1536]{1,0:T(8,128)(2,1)S(1)}, bf16[128,1536]{1,0:T(8,128)(2,1)S(1)}, u32[]{:S(2)}, u32[]{:S(2)}) collective-permute-start(bf16[128,1536]{1,0:T(8,128)(2,1)S(1)} %get-tuple-element.57), channel_id=1, source_target_pairs={{0,16},{8,24},{16,0},{24,8},{1,17},{9,25},{17,1},{25,9},{2,18},{10... | collective-permute-start | bytes 1179656 | tf_op jit(solution)/shard_map/ppermute | solution.py:362
  14.9 27.3 %collective-permute-start.2 = (bf16[128,1536]{1,0:T(8,128)(2,1)S(1)}, bf16[128,1536]{1,0:T(8,128)(2,1)S(1)}, u32[]{:S(2)}, u32[]{:S(2)}) collective-permute-start(bf16[128,1536]{1,0:T(8,128)(2,1)S(1)} %get-tuple-element.58), channel_id=1, source_target_pairs={{0,24},{8,16},{16,8},{24,0},{1,25},{9,17},{17,9},{25,1},{2,26},{10... | collective-permute-start | bytes 1179656 | tf_op jit(solution)/shard_map/ppermute | solution.py:362
  29.1 25.8 %collective-permute-start.7 = (f32[4,128]{1,0:T(4,128)S(1)}, f32[4,128]{1,0:T(4,128)S(1)}, u32[]{:S(2)}, u32[]{:S(2)}) collective-permute-start(f32[4,128]{1,0:T(4,128)S(1)} %after.4), channel_id=1, source_target_pairs={{0,24},{8,16},{16,8},{24,0},{1,25},{9,17},{17,9},{25,1},{2,26},{10... | collective-permute-start | bytes 6152 | tf_op jit(solution)/shard_map/ppermute | solution.py:362
  32.3 24.0 %collective-permute-start.8 = (f32[4,128]{1,0:T(4,128)S(1)}, f32[4,128]{1,0:T(4,128)S(1)}, u32[]{:S(2)}, u32[]{:S(2)}) collective-permute-start(f32[4,128]{1,0:T(4,128)S(1)} %after.4), channel_id=1, source_target_pairs={{0,16},{8,24},{16,0},{24,8},{1,17},{9,25},{17,1},{25,9},{2,18},{10... | collective-permute-start | bytes 6152 | tf_op jit(solution)/shard_map/ppermute | solution.py:362
  32.3 24.0 %collective-permute-start.6 = (f32[4,128]{1,0:T(4,128)S(1)}, f32[4,128]{1,0:T(4,128)S(1)}, u32[]{:S(2)}, u32[]{:S(2)}) collective-permute-start(f32[4,128]{1,0:T(4,128)S(1)} %after.4), channel_id=1, source_target_pairs={{0,8},{8,0},{16,24},{24,16},{1,9},{9,1},{17,25},{25,17},{2,10},{10... | collective-permute-start | bytes 6152 | tf_op jit(solution)/shard_map/ppermute | solution.py:362
  46.1 11.9 %collective-permute-start.3 = (bf16[128,512]{1,0:T(8,128)(2,1)S(1)}, bf16[128,512]{1,0:T(8,128)(2,1)S(1)}, u32[]{:S(2)}, u32[]{:S(2)}) collective-permute-start(bf16[128,512]{1,0:T(8,128)(2,1)S(1)} %get-tuple-element.60), channel_id=1, source_target_pairs={{0,8},{8,0},{16,24},{24,16},{1,9},{9,1},{17,25},{25,17},{2,10},{10... | collective-permute-start | bytes 393224 | tf_op jit(solution)/shard_map/ppermute | solution.py:362
  53.8 11.8 %collective-permute-start.4 = (bf16[128,512]{1,0:T(8,128)(2,1)S(1)}, bf16[128,512]{1,0:T(8,128)(2,1)S(1)}, u32[]{:S(2)}, u32[]{:S(2)}) collective-permute-start(bf16[128,512]{1,0:T(8,128)(2,1)S(1)} %get-tuple-element.61), channel_id=1, source_target_pairs={{0,16},{8,24},{16,0},{24,8},{1,17},{9,25},{17,1},{25,9},{2,18},{10... | collective-permute-start | bytes 393224 | tf_op jit(solution)/shard_map/ppermute | solution.py:362
  54.9 10.8 %collective-permute-start.5 = (bf16[128,512]{1,0:T(8,128)(2,1)S(1)}, bf16[128,512]{1,0:T(8,128)(2,1)S(1)}, u32[]{:S(2)}, u32[]{:S(2)}) collective-permute-start(bf16[128,512]{1,0:T(8,128)(2,1)S(1)} %get-tuple-element.62), channel_id=1, source_target_pairs={{0,24},{8,16},{16,8},{24,0},{1,25},{9,17},{17,9},{25,1},{2,26},{10... | collective-permute-start | bytes 393224 | tf_op jit(solution)/shard_map/ppermute | solution.py:362
  56.3 1.2 collective-permute-start.9
  71.6 1.7 collective-permute-start.10
  71.9 1.6 collective-permute-start.11
  74.1 14.2 %collective-permute-start.15 = (bf16[128,2048]{1,0:T(8,128)(2,1)S(1)}, bf16[128,2048]{1,0:T(8,128)(2,1)S(1)}, u32[]{:S(2)}, u32[]{:S(2)}) collective-permute-start(bf16[128,2048]{1,0:T(8,128)(2,1)S(1)} %after.5), channel_id=1, source_target_pairs={{0,8},{8,0},{16,24},{24,16},{1,9},{9,1},{17,25},{25,17},{2,10},{10... | collective-permute-start | bytes 1572872 | tf_op jit(solution)/shard_map/ppermute | solution.py:438
  75.6 13.2 %collective-permute-start.24 = (bf16[128,2048]{1,0:T(8,128)(2,1)S(1)}, bf16[128,2048]{1,0:T(8,128)(2,1)S(1)}, u32[]{:S(2)}, u32[]{:S(2)}) collective-permute-start(bf16[128,2048]{1,0:T(8,128)(2,1)S(1)} %after.5), channel_id=1, source_target_pairs={{8,16},{16,8},{9,17},{17,9},{10,18},{18,10},{11,19},{19,11},{12,20... | collective-permute-start | bytes 1572872 | tf_op jit(solution)/shard_map/ppermute | solution.py:438
  76.3 12.1 %collective-permute-start.12 = (bf16[80,2048]{1,0:T(8,128)(2,1)S(1)}, bf16[80,2048]{1,0:T(8,128)(2,1)S(1)}, u32[]{:S(2)}, u32[]{:S(2)}) collective-permute-start(bf16[80,2048]{1,0:T(8,128)(2,1)S(1)} %get-tuple-element.66), channel_id=1, source_target_pairs={{0,2},{1,3},{2,0},{3,1},{4,6},{5,7},{6,4},{7,5},{8,10},{9,11},{10,... | collective-permute-start | bytes 983048 | tf_op jit(solution)/shard_map/ppermute | solution.py:365
  77.9 16.3 %collective-permute-start.13 = (bf16[80,2048]{1,0:T(8,128)(2,1)S(1)}, bf16[80,2048]{1,0:T(8,128)(2,1)S(1)}, u32[]{:S(2)}, u32[]{:S(2)}) collective-permute-start(bf16[80,2048]{1,0:T(8,128)(2,1)S(1)} %get-tuple-element.67), channel_id=1, source_target_pairs={{0,4},{1,5},{2,6},{3,7},{4,0},{5,1},{6,2},{7,3},{8,12},{9,13},{10,... | collective-permute-start | bytes 983048 | tf_op jit(solution)/shard_map/ppermute | solution.py:365
  79.1 16.2 %collective-permute-start.14 = (bf16[80,2048]{1,0:T(8,128)(2,1)S(1)}, bf16[80,2048]{1,0:T(8,128)(2,1)S(1)}, u32[]{:S(2)}, u32[]{:S(2)}) collective-permute-start(bf16[80,2048]{1,0:T(8,128)(2,1)S(1)} %get-tuple-element.68), channel_id=1, source_target_pairs={{0,6},{1,7},{2,4},{3,5},{4,2},{5,3},{6,0},{7,1},{8,14},{9,15},{10,... | collective-permute-start | bytes 983048 | tf_op jit(solution)/shard_map/ppermute | solution.py:365
  88.3 1.6 collective-permute-start.16
  88.4 2.8 %collective-permute-start.17 = (bf16[64,2048]{1,0:T(8,128)(2,1)S(1)}, bf16[64,2048]{1,0:T(8,128)(2,1)S(1)}, u32[]{:S(2)}, u32[]{:S(2)}) collective-permute-start(bf16[64,2048]{1,0:T(8,128)(2,1)S(1)} %get-tuple-element.111), channel_id=1, source_target_pairs={{0,1},{1,0},{2,3},{3,2},{4,5},{5,4},{6,7},{7,6},{8,9},{9,8},{10,11... | collective-permute-start | bytes 786440 | tf_op jit(solution)/shard_map/ppermute | solution.py:368
  88.9 19.7 %collective-permute-start.31 = (bf16[128,2048]{1,0:T(8,128)(2,1)S(1)}, bf16[128,2048]{1,0:T(8,128)(2,1)S(1)}, u32[]{:S(2)}, u32[]{:S(2)}) collective-permute-start(bf16[128,2048]{1,0:T(8,128)(2,1)S(1)} %collective-permute-done.15.mine_ref), channel_id=1, source_target_pairs={{8,16},{16,8},{9,17},{17,9},{10,18},{18,10},{11,19},{19,11},{12,20... | collective-permute-start | bytes 1572872 | tf_op jit(solution)/shard_map/ppermute | solution.py:438
  89.9 18.5 %collective-permute-start.25 = (bf16[128,2048]{1,0:T(8,128)(2,1)S(1)}, bf16[128,2048]{1,0:T(8,128)(2,1)S(1)}, u32[]{:S(2)}, u32[]{:S(2)}) collective-permute-start(bf16[128,2048]{1,0:T(8,128)(2,1)S(1)} %collective-permute-done.24.__0_), channel_id=1, source_target_pairs={{8,0},{16,24},{9,1},{17,25},{10,2},{18,26},{11,3},{19,27},{12,4},{... | collective-permute-start | bytes 1572872 | tf_op jit(solution)/shard_map/ppermute | solution.py:438
  91.7 22.8 %collective-permute-start.21 = (bf16[80,2048]{1,0:T(8,128)(2,1)S(1)}, bf16[80,2048]{1,0:T(8,128)(2,1)S(1)}, u32[]{:S(2)}, u32[]{:S(2)}) collective-permute-start(bf16[80,2048]{1,0:T(8,128)(2,1)S(1)} %get-tuple-element.74), channel_id=1, source_target_pairs={{0,2},{1,3},{2,0},{3,1},{4,6},{5,7},{6,4},{7,5},{8,10},{9,11},{10,... | collective-permute-start | bytes 983048 | tf_op jit(solution)/shard_map/ppermute | solution.py:365
  94.2 20.9 %collective-permute-start.22 = (bf16[80,2048]{1,0:T(8,128)(2,1)S(1)}, bf16[80,2048]{1,0:T(8,128)(2,1)S(1)}, u32[]{:S(2)}, u32[]{:S(2)}) collective-permute-start(bf16[80,2048]{1,0:T(8,128)(2,1)S(1)} %get-tuple-element.75), channel_id=1, source_target_pairs={{0,4},{1,5},{2,6},{3,7},{4,0},{5,1},{6,2},{7,3},{8,12},{9,13},{10,... | collective-permute-start | bytes 983048 | tf_op jit(solution)/shard_map/ppermute | solution.py:365
  95.4 21.2 %collective-permute-start.23 = (bf16[80,2048]{1,0:T(8,128)(2,1)S(1)}, bf16[80,2048]{1,0:T(8,128)(2,1)S(1)}, u32[]{:S(2)}, u32[]{:S(2)}) collective-permute-start(bf16[80,2048]{1,0:T(8,128)(2,1)S(1)} %get-tuple-element.76), channel_id=1, source_target_pairs={{0,6},{1,7},{2,4},{3,5},{4,2},{5,3},{6,0},{7,1},{8,14},{9,15},{10,... | collective-permute-start | bytes 983048 | tf_op jit(solution)/shard_map/ppermute | solution.py:365
  108.5 1.6 collective-permute-start.26
  108.6 3.0 %collective-permute-start.27 = (bf16[64,2048]{1,0:T(8,128)(2,1)S(1)}, bf16[64,2048]{1,0:T(8,128)(2,1)S(1)}, u32[]{:S(2)}, u32[]{:S(2)}) collective-permute-start(bf16[64,2048]{1,0:T(8,128)(2,1)S(1)} %get-tuple-element.109), channel_id=1, source_target_pairs={{0,1},{1,0},{2,3},{3,2},{4,5},{5,4},{6,7},{7,6},{8,9},{9,8},{10,11... | collective-permute-start | bytes 786440 | tf_op jit(solution)/shard_map/ppermute | solution.py:368
  110.1 16.0 %collective-permute-start.32 = (bf16[128,2048]{1,0:T(8,128)(2,1)S(1)}, bf16[128,2048]{1,0:T(8,128)(2,1)S(1)}, u32[]{:S(2)}, u32[]{:S(2)}) collective-permute-start(bf16[128,2048]{1,0:T(8,128)(2,1)S(1)} %collective-permute-done.31.__0_), channel_id=1, source_target_pairs={{8,0},{16,24},{9,1},{17,25},{10,2},{18,26},{11,3},{19,27},{12,4},{... | collective-permute-start | bytes 1572872 | tf_op jit(solution)/shard_map/ppermute | solution.py:438
  113.0 12.8 %copy-start.11 = (bf16[80,2048]{1,0:T(8,128)(2,1)}, bf16[80,2048]{1,0:T(8,128)(2,1)S(1)}, u32[]{:S(2)}) copy-start(bf16[80,2048]{1,0:T(8,128)(2,1)S(1)} %get-tuple-element.77.refs_7_.refs_0_) | copy-start | bytes 983044
  113.0 18.7 %collective-permute-start.38 = (bf16[80,2048]{1,0:T(8,128)(2,1)}, bf16[80,2048]{1,0:T(8,128)(2,1)}, u32[]{:S(2)}, u32[]{:S(2)}) collective-permute-start(bf16[80,2048]{1,0:T(8,128)(2,1)} %get-tuple-element.86), channel_id=1, source_target_pairs={{0,2},{1,3},{2,0},{3,1},{4,6},{5,7},{6,4},{7,5},{8,10},{9,11},{10,... | collective-permute-start | bytes 983048 | tf_op jit(solution)/shard_map/ppermute | solution.py:365
  114.5 18.7 %collective-permute-start.39 = (bf16[80,2048]{1,0:T(8,128)(2,1)}, bf16[80,2048]{1,0:T(8,128)(2,1)}, u32[]{:S(2)}, u32[]{:S(2)}) collective-permute-start(bf16[80,2048]{1,0:T(8,128)(2,1)} %get-tuple-element.87), channel_id=1, source_target_pairs={{0,4},{1,5},{2,6},{3,7},{4,0},{5,1},{6,2},{7,3},{8,12},{9,13},{10,... | collective-permute-start | bytes 983048 | tf_op jit(solution)/shard_map/ppermute | solution.py:365
  115.1 18.2 %collective-permute-start.40 = (bf16[80,2048]{1,0:T(8,128)(2,1)}, bf16[80,2048]{1,0:T(8,128)(2,1)}, u32[]{:S(2)}, u32[]{:S(2)}) collective-permute-start(bf16[80,2048]{1,0:T(8,128)(2,1)} %get-tuple-element.88), channel_id=1, source_target_pairs={{0,6},{1,7},{2,4},{3,5},{4,2},{5,3},{6,0},{7,1},{8,14},{9,15},{10,... | collective-permute-start | bytes 983048 | tf_op jit(solution)/shard_map/ppermute | solution.py:365
  127.0 1.7 collective-permute-start.33
  127.0 2.1 collective-permute-start.34
  129.7 17.0 %collective-permute-start.35 = (bf16[80,2048]{1,0:T(8,128)(2,1)S(1)}, bf16[80,2048]{1,0:T(8,128)(2,1)S(1)}, u32[]{:S(2)}, u32[]{:S(2)}) collective-permute-start(bf16[80,2048]{1,0:T(8,128)(2,1)S(1)} %get-tuple-element.83), channel_id=1, source_target_pairs={{0,2},{1,3},{2,0},{3,1},{4,6},{5,7},{6,4},{7,5},{8,10},{9,11},{10,... | collective-permute-start | bytes 983048 | tf_op jit(solution)/shard_map/ppermute | solution.py:365
  131.2 17.0 %collective-permute-start.36 = (bf16[80,2048]{1,0:T(8,128)(2,1)S(1)}, bf16[80,2048]{1,0:T(8,128)(2,1)S(1)}, u32[]{:S(2)}, u32[]{:S(2)}) collective-permute-start(bf16[80,2048]{1,0:T(8,128)(2,1)S(1)} %get-tuple-element.84), channel_id=1, source_target_pairs={{0,4},{1,5},{2,6},{3,7},{4,0},{5,1},{6,2},{7,3},{8,12},{9,13},{10,... | collective-permute-start | bytes 983048 | tf_op jit(solution)/shard_map/ppermute | solution.py:365
  131.8 16.4 %collective-permute-start.37 = (bf16[80,2048]{1,0:T(8,128)(2,1)S(1)}, bf16[80,2048]{1,0:T(8,128)(2,1)S(1)}, u32[]{:S(2)}, u32[]{:S(2)}) collective-permute-start(bf16[80,2048]{1,0:T(8,128)(2,1)S(1)} %get-tuple-element.85), channel_id=1, source_target_pairs={{0,6},{1,7},{2,4},{3,5},{4,2},{5,3},{6,0},{7,1},{8,14},{9,15},{10,... | collective-permute-start | bytes 983048 | tf_op jit(solution)/shard_map/ppermute | solution.py:365
  144.6 13.0 %collective-permute-start.44 = (bf16[80,2048]{1,0:T(8,128)(2,1)S(1)}, bf16[80,2048]{1,0:T(8,128)(2,1)S(1)}, u32[]{:S(2)}, u32[]{:S(2)}) collective-permute-start(bf16[80,2048]{1,0:T(8,128)(2,1)S(1)} %get-tuple-element.94), channel_id=1, source_target_pairs={{0,2},{1,3},{2,0},{3,1},{4,6},{5,7},{6,4},{7,5},{8,10},{9,11},{10,... | collective-permute-start | bytes 983048 | tf_op jit(solution)/shard_map/ppermute | solution.py:365
  146.2 15.7 %collective-permute-start.45 = (bf16[80,2048]{1,0:T(8,128)(2,1)S(1)}, bf16[80,2048]{1,0:T(8,128)(2,1)S(1)}, u32[]{:S(2)}, u32[]{:S(2)}) collective-permute-start(bf16[80,2048]{1,0:T(8,128)(2,1)S(1)} %get-tuple-element.95), channel_id=1, source_target_pairs={{0,4},{1,5},{2,6},{3,7},{4,0},{5,1},{6,2},{7,3},{8,12},{9,13},{10,... | collective-permute-start | bytes 983048 | tf_op jit(solution)/shard_map/ppermute | solution.py:365
  146.7 15.1 %collective-permute-start.46 = (bf16[80,2048]{1,0:T(8,128)(2,1)S(1)}, bf16[80,2048]{1,0:T(8,128)(2,1)S(1)}, u32[]{:S(2)}, u32[]{:S(2)}) collective-permute-start(bf16[80,2048]{1,0:T(8,128)(2,1)S(1)} %get-tuple-element.96), channel_id=1, source_target_pairs={{0,6},{1,7},{2,4},{3,5},{4,2},{5,3},{6,0},{7,1},{8,14},{9,15},{10,... | collective-permute-start | bytes 983048 | tf_op jit(solution)/shard_map/ppermute | solution.py:365
  163.6 3.6 %collective-permute-start.47 = (bf16[128,2048]{1,0:T(8,128)(2,1)S(1)}, bf16[128,2048]{1,0:T(8,128)(2,1)S(1)}, u32[]{:S(2)}, u32[]{:S(2)}) collective-permute-start(bf16[128,2048]{1,0:T(8,128)(2,1)S(1)} %get-tuple-element.98), channel_id=1, source_target_pairs={{0,1},{1,0},{2,3},{3,2},{4,5},{5,4},{6,7},{7,6},{8,9},{9,8},{10,11... | collective-permute-start | bytes 1572872 | tf_op jit(solution)/shard_map/ppermute | solution.py:368
  163.7 10.6 %collective-permute-start.41 = (bf16[80,2048]{1,0:T(8,128)(2,1)S(1)}, bf16[80,2048]{1,0:T(8,128)(2,1)S(1)}, u32[]{:S(2)}, u32[]{:S(2)}) collective-permute-start(bf16[80,2048]{1,0:T(8,128)(2,1)S(1)} %get-tuple-element.91), channel_id=1, source_target_pairs={{0,2},{1,3},{2,0},{3,1},{4,6},{5,7},{6,4},{7,5},{8,10},{9,11},{10,... | collective-permute-start | bytes 983048 | tf_op jit(solution)/shard_map/ppermute | solution.py:365
  164.3 16.8 %collective-permute-start.42 = (bf16[80,2048]{1,0:T(8,128)(2,1)S(1)}, bf16[80,2048]{1,0:T(8,128)(2,1)S(1)}, u32[]{:S(2)}, u32[]{:S(2)}) collective-permute-start(bf16[80,2048]{1,0:T(8,128)(2,1)S(1)} %get-tuple-element.92), channel_id=1, source_target_pairs={{0,4},{1,5},{2,6},{3,7},{4,0},{5,1},{6,2},{7,3},{8,12},{9,13},{10,... | collective-permute-start | bytes 983048 | tf_op jit(solution)/shard_map/ppermute | solution.py:365
  165.5 15.6 %collective-permute-start.43 = (bf16[80,2048]{1,0:T(8,128)(2,1)S(1)}, bf16[80,2048]{1,0:T(8,128)(2,1)S(1)}, u32[]{:S(2)}, u32[]{:S(2)}) collective-permute-start(bf16[80,2048]{1,0:T(8,128)(2,1)S(1)} %get-tuple-element.93), channel_id=1, source_target_pairs={{0,6},{1,7},{2,4},{3,5},{4,2},{5,3},{6,0},{7,1},{8,14},{9,15},{10,... | collective-permute-start | bytes 983048 | tf_op jit(solution)/shard_map/ppermute | solution.py:365
  167.4 15.6 %copy-start.10 = (bf16[80,2048]{1,0:T(8,128)(2,1)S(1)}, bf16[80,2048]{1,0:T(8,128)(2,1)}, u32[]{:S(2)}) copy-start(bf16[80,2048]{1,0:T(8,128)(2,1)} %copy-done.9) | copy-start | bytes 983044
  167.4 17.1 %copy-start.8 = (bf16[80,2048]{1,0:T(8,128)(2,1)S(1)}, bf16[80,2048]{1,0:T(8,128)(2,1)}, u32[]{:S(2)}) copy-start(bf16[80,2048]{1,0:T(8,128)(2,1)} %copy-done.7) | copy-start | bytes 983044
  167.4 17.7 %copy-start.6 = (bf16[80,2048]{1,0:T(8,128)(2,1)S(1)}, bf16[80,2048]{1,0:T(8,128)(2,1)}, u32[]{:S(2)}) copy-start(bf16[80,2048]{1,0:T(8,128)(2,1)} %copy-done.5) | copy-start | bytes 983044
  167.4 19.1 %collective-permute-start.49 = (bf16[128,2048]{1,0:T(8,128)(2,1)S(1)}, bf16[128,2048]{1,0:T(8,128)(2,1)S(1)}, u32[]{:S(2)}, u32[]{:S(2)}) collective-permute-start(bf16[128,2048]{1,0:T(8,128)(2,1)S(1)} %fusion.refs_4_), channel_id=1, source_target_pairs={{0,8},{24,16},{1,9},{25,17},{2,10},{26,18},{3,11},{27,19},{4,12},{... | collective-permute-start | bytes 1572872 | tf_op jit(solution)/shard_map/ppermute | solution.py:438
  182.9 3.8 %collective-permute-start.48 = (bf16[128,2048]{1,0:T(8,128)(2,1)S(1)}, bf16[128,2048]{1,0:T(8,128)(2,1)S(1)}, u32[]{:S(2)}, u32[]{:S(2)}) collective-permute-start(bf16[128,2048]{1,0:T(8,128)(2,1)S(1)} %get-tuple-element.100), channel_id=1, source_target_pairs={{0,1},{1,0},{2,3},{3,2},{4,5},{5,4},{6,7},{7,6},{8,9},{9,8},{10,11... | collective-permute-start | bytes 1572872 | tf_op jit(solution)/shard_map/ppermute | solution.py:368
  183.0 10.6 %collective-permute-start.28 = (bf16[80,2048]{1,0:T(8,128)(2,1)S(1)}, bf16[80,2048]{1,0:T(8,128)(2,1)S(1)}, u32[]{:S(2)}, u32[]{:S(2)}) collective-permute-start(bf16[80,2048]{1,0:T(8,128)(2,1)S(1)} %copy-done.10), channel_id=1, source_target_pairs={{0,2},{1,3},{2,0},{3,1},{4,6},{5,7},{6,4},{7,5},{8,10},{9,11},{10,... | collective-permute-start | bytes 983048 | tf_op jit(solution)/shard_map/ppermute | solution.py:365
  184.5 16.8 %collective-permute-start.29 = (bf16[80,2048]{1,0:T(8,128)(2,1)S(1)}, bf16[80,2048]{1,0:T(8,128)(2,1)S(1)}, u32[]{:S(2)}, u32[]{:S(2)}) collective-permute-start(bf16[80,2048]{1,0:T(8,128)(2,1)S(1)} %copy-done.8), channel_id=1, source_target_pairs={{0,4},{1,5},{2,6},{3,7},{4,0},{5,1},{6,2},{7,3},{8,12},{9,13},{10,... | collective-permute-start | bytes 983048 | tf_op jit(solution)/shard_map/ppermute | solution.py:365
  185.1 16.2 %collective-permute-start.30 = (bf16[80,2048]{1,0:T(8,128)(2,1)S(1)}, bf16[80,2048]{1,0:T(8,128)(2,1)S(1)}, u32[]{:S(2)}, u32[]{:S(2)}) collective-permute-start(bf16[80,2048]{1,0:T(8,128)(2,1)S(1)} %copy-done.6), channel_id=1, source_target_pairs={{0,6},{1,7},{2,4},{3,5},{4,2},{5,3},{6,0},{7,1},{8,14},{9,15},{10,... | collective-permute-start | bytes 983048 | tf_op jit(solution)/shard_map/ppermute | solution.py:365
  186.8 16.3 %copy-start.4 = (bf16[80,2048]{1,0:T(8,128)(2,1)S(1)}, bf16[80,2048]{1,0:T(8,128)(2,1)}, u32[]{:S(2)}) copy-start(bf16[80,2048]{1,0:T(8,128)(2,1)} %copy-done.3) | copy-start | bytes 983044
  203.1 4.3 %collective-permute-start.50 = (bf16[128,2048]{1,0:T(8,128)(2,1)S(1)}, bf16[128,2048]{1,0:T(8,128)(2,1)S(1)}, u32[]{:S(2)}, u32[]{:S(2)}) collective-permute-start(bf16[128,2048]{1,0:T(8,128)(2,1)S(1)} %get-tuple-element.102), channel_id=1, source_target_pairs={{0,1},{1,0},{2,3},{3,2},{4,5},{5,4},{6,7},{7,6},{8,9},{9,8},{10,11... | collective-permute-start | bytes 1572872 | tf_op jit(solution)/shard_map/ppermute | solution.py:368
  203.2 10.7 %collective-permute-start.18 = (bf16[80,2048]{1,0:T(8,128)(2,1)S(1)}, bf16[80,2048]{1,0:T(8,128)(2,1)S(1)}, u32[]{:S(2)}, u32[]{:S(2)}) collective-permute-start(bf16[80,2048]{1,0:T(8,128)(2,1)S(1)} %copy-done.4), channel_id=1, source_target_pairs={{0,2},{1,3},{2,0},{3,1},{4,6},{5,7},{6,4},{7,5},{8,10},{9,11},{10,... | collective-permute-start | bytes 983048 | tf_op jit(solution)/shard_map/ppermute | solution.py:365
  203.8 16.8 %collective-permute-start.19 = (bf16[80,2048]{1,0:T(8,128)(2,1)S(1)}, bf16[80,2048]{1,0:T(8,128)(2,1)S(1)}, u32[]{:S(2)}, u32[]{:S(2)}) collective-permute-start(bf16[80,2048]{1,0:T(8,128)(2,1)S(1)} %get-tuple-element.72), channel_id=1, source_target_pairs={{0,4},{1,5},{2,6},{3,7},{4,0},{5,1},{6,2},{7,3},{8,12},{9,13},{10,... | collective-permute-start | bytes 983048 | tf_op jit(solution)/shard_map/ppermute | solution.py:365
  205.0 15.6 %collective-permute-start.20 = (bf16[80,2048]{1,0:T(8,128)(2,1)S(1)}, bf16[80,2048]{1,0:T(8,128)(2,1)S(1)}, u32[]{:S(2)}, u32[]{:S(2)}) collective-permute-start(bf16[80,2048]{1,0:T(8,128)(2,1)S(1)} %get-tuple-element.73), channel_id=1, source_target_pairs={{0,6},{1,7},{2,4},{3,5},{4,2},{5,3},{6,0},{7,1},{8,14},{9,15},{10,... | collective-permute-start | bytes 983048 | tf_op jit(solution)/shard_map/ppermute | solution.py:365
  206.7 20.8 %collective-permute-start.53 = (bf16[128,2048]{1,0:T(8,128)(2,1)S(1)}, bf16[128,2048]{1,0:T(8,128)(2,1)S(1)}, u32[]{:S(2)}, u32[]{:S(2)}) collective-permute-start(bf16[128,2048]{1,0:T(8,128)(2,1)S(1)} %add_convert_fusion.3.refs_5_), channel_id=1, source_target_pairs={{8,16},{16,8},{9,17},{17,9},{10,18},{18,10},{11,19},{19,11},{12,20... | collective-permute-start | bytes 1572872 | tf_op jit(solution)/shard_map/ppermute | solution.py:438
  207.4 18.6 %collective-permute-start.54 = (bf16[128,2048]{1,0:T(8,128)(2,1)S(1)}, bf16[128,2048]{1,0:T(8,128)(2,1)S(1)}, u32[]{:S(2)}, u32[]{:S(2)}) collective-permute-start(bf16[128,2048]{1,0:T(8,128)(2,1)S(1)} %fusion.1.refs_4_), channel_id=1, source_target_pairs={{0,8},{24,16},{1,9},{25,17},{2,10},{26,18},{3,11},{27,19},{4,12},{... | collective-permute-start | bytes 1572872 | tf_op jit(solution)/shard_map/ppermute | solution.py:438
  213.9 21.7 %collective-permute-start.52 = (bf16[128,2048]{1,0:T(8,128)(2,1)S(1)}, bf16[128,2048]{1,0:T(8,128)(2,1)S(1)}, u32[]{:S(2)}, u32[]{:S(2)}) collective-permute-start(bf16[128,2048]{1,0:T(8,128)(2,1)S(1)} %add_convert_fusion.2.refs_4_), channel_id=1, source_target_pairs={{0,8},{8,0},{16,24},{24,16},{1,9},{9,1},{17,25},{25,17},{2,10},{10... | collective-permute-start | bytes 1572872 | tf_op jit(solution)/shard_map/ppermute | solution.py:438
  222.4 5.2 %collective-permute-start.51 = (bf16[128,2048]{1,0:T(8,128)(2,1)S(1)}, bf16[128,2048]{1,0:T(8,128)(2,1)S(1)}, u32[]{:S(2)}, u32[]{:S(2)}) collective-permute-start(bf16[128,2048]{1,0:T(8,128)(2,1)S(1)} %get-tuple-element.104), channel_id=1, source_target_pairs={{0,1},{1,0},{2,3},{3,2},{4,5},{5,4},{6,7},{7,6},{8,9},{9,8},{10,11... | collective-permute-start | bytes 1572872 | tf_op jit(solution)/shard_map/ppermute | solution.py:368
  226.3 13.5 %collective-permute-start.55 = (bf16[128,2048]{1,0:T(8,128)(2,1)S(1)}, bf16[128,2048]{1,0:T(8,128)(2,1)S(1)}, u32[]{:S(2)}, u32[]{:S(2)}) collective-permute-start(bf16[128,2048]{1,0:T(8,128)(2,1)S(1)} %add_convert_fusion.1), channel_id=1, source_target_pairs={{8,24},{16,0},{9,25},{17,1},{10,26},{18,2},{11,27},{19,3},{12,28},... | collective-permute-start | bytes 1572872 | tf_op jit(solution)/shard_map/ppermute | solution.py:438
  (8 other events, 37.3 us)
Sparse Core Ops, SparseCore 0:
  9.2 57.0 all-gather.1

commit v4 on v3

--- a/solution.py
+++ b/solution.py
@@ -447,7 +447,7 @@
     done0 = run(0, [own1])
     (kept,) = after([cross_block], [done0[0]])
     second = jnp.where(in_middle, kept, hop_along(cross_block, OUT))
-    arrived[2], own2 = dispatch(2, second, [done0[0]])
+    arrived[2], own2 = dispatch(2, second, [done0[0]] + arrived[1][1:2])
     done1 = run(1, [own2])
     (kept,) = after([cross_pair], [done1[0]])
     third = jnp.where(in_middle, kept, hop_along(cross_pair, OUT))

time: 248 us -> 247 us (level)
  transfers between devices with their start and end apart: 57 -> 57, of which waited for: 24 -> 23; matrix products, arithmetic and copies ran while one was open for 2% -> 2% of each run, Pallas kernels for 20% -> 20%
where the time goes in v4:
time: 247 us
  waiting for transfers between devices  95.1 us (39%)
  starting transfers between devices  71.4 us (29%)
  Pallas kernels  57.9 us (23%)
  between operations  14.1 us (6%)
  local copies, waits for them, and re-layouts  4.91 us (2%)
  other arithmetic  3.36 us (1%)
    pallas_call x4, Pallas kernels, expert(): pl.pallas_call(functools.partial(expert_kernel, chips, len(deps)), in_spe...  38.4 us
    ppermute x24, waiting for transfers between devices, over_chips(): return lax.ppermute(value, 'exp', xor_pairs(expert_count, 2 * step))  32.9 us
    ppermute x9, waiting for transfers between devices, over_seq(): return lax.ppermute(value, 'seq', xor_pairs(seq_count, hop))  29.4 us
    ppermute x10, waiting for transfers between devices, hop_along(): return lax.ppermute(value, 'seq', pairs)  28.2 us
    ppermute x24, starting transfers between devices, over_chips(): return lax.ppermute(value, 'exp', xor_pairs(expert_count, 2 * step))  27.5 us
    ppermute x10, starting transfers between devices, hop_along(): return lax.ppermute(value, 'seq', pairs)  21.1 us
    ppermute x9, starting transfers between devices, over_seq(): return lax.ppermute(value, 'seq', xor_pairs(seq_count, hop))  20.2 us
    pallas_call x4, Pallas kernels, combine(): pl.pallas_call(functools.partial(combine_kernel, hop, chips, len(deps)),...  7.05 us
  transfers between devices with their start and end apart: 57, of which 23 were waited for; matrix products, arithmetic and copies ran while one was open for 2% of the time, Pallas kernels for 20%

profile of v4, /device:TPU:0, one launch (start us, length us, event | category | flops | bytes accessed | tf_op | source)
XLA Modules:
  0.0 246.8 jit_solution(3233745461002833533)
XLA Ops:
  7.3 1.4 copy-done
  9.2 3.1 %collective-permute-start = (bf16[128,1536]{1,0:T(8,128)(2,1)S(1)}, bf16[128,1536]{1,0:T(8,128)(2,1)S(1)}, u32[]{:S(2)}, u32[]{:S(2)}) collective-permute-start(bf16[128,1536]{1,0:T(8,128)(2,1)S(1)} %get-tuple-element.56), channel_id=1, source_target_pairs={{0,8},{8,0},{16,24},{24,16},{1,9},{9,1},{17,25},{25,17},{2,10},{10... | collective-permute-start | bytes 1179656 | tf_op jit(solution)/shard_map/ppermute | solution.py:362
  12.3 2.6 %collective-permute-start.1 = (bf16[128,1536]{1,0:T(8,128)(2,1)S(1)}, bf16[128,1536]{1,0:T(8,128)(2,1)S(1)}, u32[]{:S(2)}, u32[]{:S(2)}) collective-permute-start(bf16[128,1536]{1,0:T(8,128)(2,1)S(1)} %get-tuple-element.57), channel_id=1, source_target_pairs={{0,16},{8,24},{16,0},{24,8},{1,17},{9,25},{17,1},{25,9},{2,18},{10... | collective-permute-start | bytes 1179656 | tf_op jit(solution)/shard_map/ppermute | solution.py:362
  16.5 12.5 %collective-permute-done.refs_1_.refs_5_.refs_9_.__1_ = bf16[128,1536]{1,0:T(8,128)(2,1)S(1)} collective-permute-done((bf16[128,1536]{1,0:T(8,128)(2,1)S(1)}, bf16[128,1536]{1,0:T(8,128)(2,1)S(1)}, u32[]{:S(2)}, u32[]{:S(2)}) %collective-permute-start) | collective-permute-done | bytes 393248 | tf_op jit(solution)/shard_map/ppermute | solution.py:362
  29.1 3.2 %collective-permute-start.7 = (f32[4,128]{1,0:T(4,128)S(1)}, f32[4,128]{1,0:T(4,128)S(1)}, u32[]{:S(2)}, u32[]{:S(2)}) collective-permute-start(f32[4,128]{1,0:T(4,128)S(1)} %after.4), channel_id=1, source_target_pairs={{0,24},{8,16},{16,8},{24,0},{1,25},{9,17},{17,9},{25,1},{2,26},{10... | collective-permute-start | bytes 6152 | tf_op jit(solution)/shard_map/ppermute | solution.py:362
  32.3 1.2 collective-permute-start.6
  33.5 8.7 %collective-permute-done.1.refs_2_.refs_6_.refs_10_ = bf16[128,1536]{1,0:T(8,128)(2,1)S(1)} collective-permute-done((bf16[128,1536]{1,0:T(8,128)(2,1)S(1)}, bf16[128,1536]{1,0:T(8,128)(2,1)S(1)}, u32[]{:S(2)}, u32[]{:S(2)}) %collective-permute-start.1) | collective-permute-done | bytes 393248 | tf_op jit(solution)/shard_map/ppermute | solution.py:362
  42.2 3.9 %attend.1 = (bf16[128,512]{1,0:T(8,128)(2,1)S(1)}, bf16[128,512]{1,0:T(8,128)(2,1)S(1)}, bf16[128,512]{1,0:T(8,128)(2,1)S(1)}, bf16[128,512]{1,0:T(8,128)(2,1)S(1)}) custom-call(bf16[128,1536]{1,0:T(8,128)(2,1)S(1)} %get-tuple-element.55.refs_0_.refs_4_.refs_8_, bf16[128,1536]{1,0:T(8,128)(2,1)S(1)} %collective-permute-done.refs_1_.refs_5_.refs_9_.__1_, ...), custom_call_target="tpu_custom_call" | custom-call | flops 536870912 | bytes 2097152 | tf_op jit(solution)/shard_map/attend/pallas_call | solution.py:113
  46.1 7.7 %collective-permute-start.3 = (bf16[128,512]{1,0:T(8,128)(2,1)S(1)}, bf16[128,512]{1,0:T(8,128)(2,1)S(1)}, u32[]{:S(2)}, u32[]{:S(2)}) collective-permute-start(bf16[128,512]{1,0:T(8,128)(2,1)S(1)} %get-tuple-element.60), channel_id=1, source_target_pairs={{0,8},{8,0},{16,24},{24,16},{1,9},{9,1},{17,25},{25,17},{2,10},{10... | collective-permute-start | bytes 393224 | tf_op jit(solution)/shard_map/ppermute | solution.py:362
  53.8 1.1 collective-permute-start.4
  54.9 1.4 collective-permute-start.5
  56.4 1.1 collective-permute-done.9
  58.0 7.6 %collective-permute-done.4.refs_2_ = bf16[128,512]{1,0:T(8,128)(2,1)S(1)} collective-permute-done((bf16[128,512]{1,0:T(8,128)(2,1)S(1)}, bf16[128,512]{1,0:T(8,128)(2,1)S(1)}, u32[]{:S(2)}, u32[]{:S(2)}) %collective-permute-start.4) | collective-permute-done | bytes 131104 | tf_op jit(solution)/shard_map/ppermute | solution.py:362
  65.6 0.8 all-gather.2.cloned.1.call-done.refs_4_
  66.4 5.1 %project.1 = (bf16[128,2048]{1,0:T(8,128)(2,1)S(1)}, bf16[128,2048]{1,0:T(8,128)(2,1)S(1)}) custom-call(s32[1]{0:T(128)} %bitcast.seq_ref, bf16[128,512]{1,0:T(8,128)(2,1)S(1)} %get-tuple-element.59.refs_0_, bf16[128,512]{1,0:T(8,128)(2,1)S(1)} %collective-permute-done.3.refs_1_, bf16[128,512]{1,0:T(8,128)(2,1)S(1)} %collective-permute-done.4.refs_2_, ...), custom_call_target="tpu_custom_call" | custom-call | flops 1073741824 | bytes 8388608 | tf_op jit(solution)/shard_map/project/pallas_call | solution.py:156
  74.1 1.6 collective-permute-start.15
  76.3 1.5 collective-permute-start.12
  77.9 1.3 collective-permute-start.13
  79.1 0.7 collective-permute-start.14
  79.9 8.4 %collective-permute-done.15.mine_ref = bf16[128,2048]{1,0:T(8,128)(2,1)S(1)} collective-permute-done((bf16[128,2048]{1,0:T(8,128)(2,1)S(1)}, bf16[128,2048]{1,0:T(8,128)(2,1)S(1)}, u32[]{:S(2)}, u32[]{:S(2)}) %collective-permute-start.15) | collective-permute-done | bytes 524320 | tf_op jit(solution)/shard_map/ppermute | solution.py:438
  89.9 1.3 collective-permute-start.25
  91.7 1.5 collective-permute-start.21
  93.2 1.0 collective-permute-done.13.refs_2_
  94.2 1.2 collective-permute-start.22
  95.4 9.2 %expert0.1 = (bf16[80,2048]{1,0:T(8,128)(2,1)S(1)}, bf16[80,2048]{1,0:T(8,128)(2,1)S(1)}, bf16[80,2048]{1,0:T(8,128)(2,1)S(1)}, bf16[80,2048]{1,0:T(8,128)(2,1)S(1)}) custom-call(bf16[80,2048]{1,0:T(8,128)(2,1)S(1)} %get-tuple-element.65.__1_.refs_0_, bf16[80,2048]{1,0:T(8,128)(2,1)S(1)} %collective-permute-done.12.rest_2_.refs_1_, ...), custom_call_target="tpu_custom_call" | custom-call | flops 5536481280 | bytes 17301504 | tf_op jit(solution)/shard_map/expert0/pallas_call | solution.py:276
  104.6 3.8 %collective-permute-done.25 = bf16[128,2048]{1,0:T(8,128)(2,1)S(1)} collective-permute-done((bf16[128,2048]{1,0:T(8,128)(2,1)S(1)}, bf16[128,2048]{1,0:T(8,128)(2,1)S(1)}, u32[]{:S(2)}, u32[]{:S(2)}) %collective-permute-start.25) | collective-permute-done | bytes 524320 | tf_op jit(solution)/shard_map/ppermute | solution.py:438
  109.1 1.5 collective-permute-start.32
  110.6 1.4 slots2.1
  112.0 1.5 collective-permute-start.38
  114.0 1.5 collective-permute-start.40
  115.5 9.2 %expert1.1 = (bf16[80,2048]{1,0:T(8,128)(2,1)S(1)}, bf16[80,2048]{1,0:T(8,128)(2,1)S(1)}, bf16[80,2048]{1,0:T(8,128)(2,1)S(1)}, bf16[80,2048]{1,0:T(8,128)(2,1)S(1)}) custom-call(bf16[80,2048]{1,0:T(8,128)(2,1)S(1)} %get-tuple-element.69.refs_7_.refs_0_, bf16[80,2048]{1,0:T(8,128)(2,1)S(1)} %collective-permute-done.21.rest_3_.refs_1_, ...), custom_call_target="tpu_custom_call" | custom-call | flops 5536481280 | bytes 17301504 | tf_op jit(solution)/shard_map/expert1/pallas_call | solution.py:276
  125.1 0.9 fusion.20
  126.6 1.1 collective-permute-done.33.rest_0_
  128.6 1.5 collective-permute-start.35
  130.7 1.5 collective-permute-start.37
  132.2 1.0 copy-done.12
  133.1 10.4 %expert2.1 = (bf16[80,2048]{1,0:T(8,128)(2,1)S(1)}, bf16[80,2048]{1,0:T(8,128)(2,1)S(1)}, bf16[80,2048]{1,0:T(8,128)(2,1)S(1)}, bf16[80,2048]{1,0:T(8,128)(2,1)S(1)}) custom-call(bf16[80,2048]{1,0:T(8,128)(2,1)S(1)} %copy-done.12, bf16[80,2048]{1,0:T(8,128)(2,1)} %collective-permute-done.38.refs_1_, bf16[80,2048]{1,0:T(8,128)(2,1)} %collective-permute-done.39.refs_2_, ...), custom_call_target="tpu_custom_call" | custom-call | flops 5536481280 | bytes 17301504 | tf_op jit(solution)/shard_map/expert2/pallas_call | solution.py:276
  143.6 1.5 collective-permute-start.44
  145.7 1.5 collective-permute-start.46
  147.1 9.5 %expert3.1 = (bf16[80,2048]{1,0:T(8,128)(2,1)S(1)}, bf16[80,2048]{1,0:T(8,128)(2,1)S(1)}, bf16[80,2048]{1,0:T(8,128)(2,1)S(1)}, bf16[80,2048]{1,0:T(8,128)(2,1)S(1)}) custom-call(bf16[80,2048]{1,0:T(8,128)(2,1)S(1)} %get-tuple-element.82.refs_7_.refs_0_, bf16[80,2048]{1,0:T(8,128)(2,1)S(1)} %collective-permute-done.35.refs_1_, ...), custom_call_target="tpu_custom_call" | custom-call | flops 5536481280 | bytes 17301504 | tf_op jit(solution)/shard_map/expert3/pallas_call | solution.py:276
  156.6 4.1 %collective-permute-done.45.refs_2_ = bf16[80,2048]{1,0:T(8,128)(2,1)S(1)} collective-permute-done((bf16[80,2048]{1,0:T(8,128)(2,1)S(1)}, bf16[80,2048]{1,0:T(8,128)(2,1)S(1)}, u32[]{:S(2)}, u32[]{:S(2)}) %collective-permute-start.45) | collective-permute-done | bytes 327712 | tf_op jit(solution)/shard_map/ppermute | solution.py:365
  160.8 1.8 combine2.1
  163.2 1.2 collective-permute-start.42
  164.4 1.7 collective-permute-start.43
  166.3 4.7 %collective-permute-start.49 = (bf16[128,2048]{1,0:T(8,128)(2,1)S(1)}, bf16[128,2048]{1,0:T(8,128)(2,1)S(1)}, u32[]{:S(2)}, u32[]{:S(2)}) collective-permute-start(bf16[128,2048]{1,0:T(8,128)(2,1)S(1)} %fusion.refs_4_), channel_id=1, source_target_pairs={{0,8},{24,16},{1,9},{25,17},{2,10},{26,18},{3,11},{27,19},{4,12},{... | collective-permute-start | bytes 1572872 | tf_op jit(solution)/shard_map/ppermute | solution.py:438
  171.0 2.2 collective-permute-done.41.refs_1_
  173.2 6.9 %collective-permute-done.42.refs_2_ = bf16[80,2048]{1,0:T(8,128)(2,1)S(1)} collective-permute-done((bf16[80,2048]{1,0:T(8,128)(2,1)S(1)}, bf16[80,2048]{1,0:T(8,128)(2,1)S(1)}, u32[]{:S(2)}, u32[]{:S(2)}) %collective-permute-start.42) | collective-permute-done | bytes 327712 | tf_op jit(solution)/shard_map/ppermute | solution.py:365
  180.0 1.8 combine3.1
  181.9 1.5 collective-permute-start.28
  184.0 1.5 collective-permute-start.30
  185.8 6.7 %collective-permute-done.28.refs_1_ = bf16[80,2048]{1,0:T(8,128)(2,1)S(1)} collective-permute-done((bf16[80,2048]{1,0:T(8,128)(2,1)S(1)}, bf16[80,2048]{1,0:T(8,128)(2,1)S(1)}, u32[]{:S(2)}, u32[]{:S(2)}) %collective-permute-start.28) | collective-permute-done | bytes 327712 | tf_op jit(solution)/shard_map/ppermute | solution.py:365
  192.5 7.7 %collective-permute-done.29.refs_2_ = bf16[80,2048]{1,0:T(8,128)(2,1)S(1)} collective-permute-done((bf16[80,2048]{1,0:T(8,128)(2,1)S(1)}, bf16[80,2048]{1,0:T(8,128)(2,1)S(1)}, u32[]{:S(2)}, u32[]{:S(2)}) %collective-permute-start.29) | collective-permute-done | bytes 327712 | tf_op jit(solution)/shard_map/ppermute | solution.py:365
  200.2 1.8 combine1.1
  202.7 1.2 collective-permute-start.19
  203.9 1.8 collective-permute-start.20
  206.3 6.4 %collective-permute-start.54 = (bf16[128,2048]{1,0:T(8,128)(2,1)S(1)}, bf16[128,2048]{1,0:T(8,128)(2,1)S(1)}, u32[]{:S(2)}, u32[]{:S(2)}) collective-permute-start(bf16[128,2048]{1,0:T(8,128)(2,1)S(1)} %fusion.1.refs_4_), channel_id=1, source_target_pairs={{0,8},{24,16},{1,9},{25,17},{2,10},{26,18},{3,11},{27,19},{4,12},{... | collective-permute-start | bytes 1572872 | tf_op jit(solution)/shard_map/ppermute | solution.py:438
  212.9 2.4 collective-permute-start.52
  215.3 4.2 %collective-permute-done.19.refs_2_ = bf16[80,2048]{1,0:T(8,128)(2,1)S(1)} collective-permute-done((bf16[80,2048]{1,0:T(8,128)(2,1)S(1)}, bf16[80,2048]{1,0:T(8,128)(2,1)S(1)}, u32[]{:S(2)}, u32[]{:S(2)}) %collective-permute-start.19) | collective-permute-done | bytes 327712 | tf_op jit(solution)/shard_map/ppermute | solution.py:365
  219.5 1.8 combine0.1
  221.4 3.7 %collective-permute-done.54 = bf16[128,2048]{1,0:T(8,128)(2,1)S(1)} collective-permute-done((bf16[128,2048]{1,0:T(8,128)(2,1)S(1)}, bf16[128,2048]{1,0:T(8,128)(2,1)S(1)}, u32[]{:S(2)}, u32[]{:S(2)}) %collective-permute-start.54) | collective-permute-done | bytes 524320 | tf_op jit(solution)/shard_map/ppermute | solution.py:438
  225.3 1.3 collective-permute-start.55
  226.6 8.0 %collective-permute-done.52 = bf16[128,2048]{1,0:T(8,128)(2,1)S(1)} collective-permute-done((bf16[128,2048]{1,0:T(8,128)(2,1)S(1)}, bf16[128,2048]{1,0:T(8,128)(2,1)S(1)}, u32[]{:S(2)}, u32[]{:S(2)}) %collective-permute-start.52) | collective-permute-done | bytes 524320 | tf_op jit(solution)/shard_map/ppermute | solution.py:438
  234.6 4.1 %collective-permute-done.55 = bf16[128,2048]{1,0:T(8,128)(2,1)S(1)} collective-permute-done((bf16[128,2048]{1,0:T(8,128)(2,1)S(1)}, bf16[128,2048]{1,0:T(8,128)(2,1)S(1)}, u32[]{:S(2)}, u32[]{:S(2)}) %collective-permute-start.55) | collective-permute-done | bytes 524320 | tf_op jit(solution)/shard_map/ppermute | solution.py:438
  238.7 1.3 fusion.2
  (138 shorter events, 16.5 us)
Async XLA Ops:
  6.5 59.8 %all-gather.2.cloned.1.call-start = ((), (), s32[]{:S(2)}) async-start(), calls=%async_computation | async-start | bytes 9437184 | tf_op jit(solution)/shard_map/all_gather | solution.py:413
  8.7 57.7 %copy-start.1 = (bf16[1,128,2048]{2,1,0:T(8,128)(2,1)S(1)}, bf16[1,128,2048]{2,1,0:T(8,128)(2,1)}, u32[]{:S(2)}) copy-start(bf16[1,128,2048]{2,1,0:T(8,128)(2,1)} %param.10) | copy-start | bytes 1572868
  8.7 57.7 %copy-start.2 = (f32[2048]{0:T(1024)S(1)}, f32[2048]{0:T(1024)}, u32[]{:S(2)}) copy-start(f32[2048]{0:T(1024)} %param.12) | copy-start | bytes 24580
  9.2 19.9 %collective-permute-start = (bf16[128,1536]{1,0:T(8,128)(2,1)S(1)}, bf16[128,1536]{1,0:T(8,128)(2,1)S(1)}, u32[]{:S(2)}, u32[]{:S(2)}) collective-permute-start(bf16[128,1536]{1,0:T(8,128)(2,1)S(1)} %get-tuple-element.56), channel_id=1, source_target_pairs={{0,8},{8,0},{16,24},{24,16},{1,9},{9,1},{17,25},{25,17},{2,10},{10... | collective-permute-start | bytes 1179656 | tf_op jit(solution)/shard_map/ppermute | solution.py:362
  12.3 29.9 %collective-permute-start.1 = (bf16[128,1536]{1,0:T(8,128)(2,1)S(1)}, bf16[128,1536]{1,0:T(8,128)(2,1)S(1)}, u32[]{:S(2)}, u32[]{:S(2)}) collective-permute-start(bf16[128,1536]{1,0:T(8,128)(2,1)S(1)} %get-tuple-element.57), channel_id=1, source_target_pairs={{0,16},{8,24},{16,0},{24,8},{1,17},{9,25},{17,1},{25,9},{2,18},{10... | collective-permute-start | bytes 1179656 | tf_op jit(solution)/shard_map/ppermute | solution.py:362
  14.9 27.3 %collective-permute-start.2 = (bf16[128,1536]{1,0:T(8,128)(2,1)S(1)}, bf16[128,1536]{1,0:T(8,128)(2,1)S(1)}, u32[]{:S(2)}, u32[]{:S(2)}) collective-permute-start(bf16[128,1536]{1,0:T(8,128)(2,1)S(1)} %get-tuple-element.58), channel_id=1, source_target_pairs={{0,24},{8,16},{16,8},{24,0},{1,25},{9,17},{17,9},{25,1},{2,26},{10... | collective-permute-start | bytes 1179656 | tf_op jit(solution)/shard_map/ppermute | solution.py:362
  29.1 25.8 %collective-permute-start.7 = (f32[4,128]{1,0:T(4,128)S(1)}, f32[4,128]{1,0:T(4,128)S(1)}, u32[]{:S(2)}, u32[]{:S(2)}) collective-permute-start(f32[4,128]{1,0:T(4,128)S(1)} %after.4), channel_id=1, source_target_pairs={{0,24},{8,16},{16,8},{24,0},{1,25},{9,17},{17,9},{25,1},{2,26},{10... | collective-permute-start | bytes 6152 | tf_op jit(solution)/shard_map/ppermute | solution.py:362
  32.3 24.0 %collective-permute-start.8 = (f32[4,128]{1,0:T(4,128)S(1)}, f32[4,128]{1,0:T(4,128)S(1)}, u32[]{:S(2)}, u32[]{:S(2)}) collective-permute-start(f32[4,128]{1,0:T(4,128)S(1)} %after.4), channel_id=1, source_target_pairs={{0,16},{8,24},{16,0},{24,8},{1,17},{9,25},{17,1},{25,9},{2,18},{10... | collective-permute-start | bytes 6152 | tf_op jit(solution)/shard_map/ppermute | solution.py:362
  32.3 24.0 %collective-permute-start.6 = (f32[4,128]{1,0:T(4,128)S(1)}, f32[4,128]{1,0:T(4,128)S(1)}, u32[]{:S(2)}, u32[]{:S(2)}) collective-permute-start(f32[4,128]{1,0:T(4,128)S(1)} %after.4), channel_id=1, source_target_pairs={{0,8},{8,0},{16,24},{24,16},{1,9},{9,1},{17,25},{25,17},{2,10},{10... | collective-permute-start | bytes 6152 | tf_op jit(solution)/shard_map/ppermute | solution.py:362
  46.1 11.9 %collective-permute-start.3 = (bf16[128,512]{1,0:T(8,128)(2,1)S(1)}, bf16[128,512]{1,0:T(8,128)(2,1)S(1)}, u32[]{:S(2)}, u32[]{:S(2)}) collective-permute-start(bf16[128,512]{1,0:T(8,128)(2,1)S(1)} %get-tuple-element.60), channel_id=1, source_target_pairs={{0,8},{8,0},{16,24},{24,16},{1,9},{9,1},{17,25},{25,17},{2,10},{10... | collective-permute-start | bytes 393224 | tf_op jit(solution)/shard_map/ppermute | solution.py:362
  53.8 11.8 %collective-permute-start.4 = (bf16[128,512]{1,0:T(8,128)(2,1)S(1)}, bf16[128,512]{1,0:T(8,128)(2,1)S(1)}, u32[]{:S(2)}, u32[]{:S(2)}) collective-permute-start(bf16[128,512]{1,0:T(8,128)(2,1)S(1)} %get-tuple-element.61), channel_id=1, source_target_pairs={{0,16},{8,24},{16,0},{24,8},{1,17},{9,25},{17,1},{25,9},{2,18},{10... | collective-permute-start | bytes 393224 | tf_op jit(solution)/shard_map/ppermute | solution.py:362
  54.9 10.8 %collective-permute-start.5 = (bf16[128,512]{1,0:T(8,128)(2,1)S(1)}, bf16[128,512]{1,0:T(8,128)(2,1)S(1)}, u32[]{:S(2)}, u32[]{:S(2)}) collective-permute-start(bf16[128,512]{1,0:T(8,128)(2,1)S(1)} %get-tuple-element.62), channel_id=1, source_target_pairs={{0,24},{8,16},{16,8},{24,0},{1,25},{9,17},{17,9},{25,1},{2,26},{10... | collective-permute-start | bytes 393224 | tf_op jit(solution)/shard_map/ppermute | solution.py:362
  56.3 1.2 collective-permute-start.9
  71.6 1.7 collective-permute-start.10
  71.9 1.6 collective-permute-start.11
  74.1 14.2 %collective-permute-start.15 = (bf16[128,2048]{1,0:T(8,128)(2,1)S(1)}, bf16[128,2048]{1,0:T(8,128)(2,1)S(1)}, u32[]{:S(2)}, u32[]{:S(2)}) collective-permute-start(bf16[128,2048]{1,0:T(8,128)(2,1)S(1)} %after.5), channel_id=1, source_target_pairs={{0,8},{8,0},{16,24},{24,16},{1,9},{9,1},{17,25},{25,17},{2,10},{10... | collective-permute-start | bytes 1572872 | tf_op jit(solution)/shard_map/ppermute | solution.py:438
  75.6 13.2 %collective-permute-start.24 = (bf16[128,2048]{1,0:T(8,128)(2,1)S(1)}, bf16[128,2048]{1,0:T(8,128)(2,1)S(1)}, u32[]{:S(2)}, u32[]{:S(2)}) collective-permute-start(bf16[128,2048]{1,0:T(8,128)(2,1)S(1)} %after.5), channel_id=1, source_target_pairs={{8,16},{16,8},{9,17},{17,9},{10,18},{18,10},{11,19},{19,11},{12,20... | collective-permute-start | bytes 1572872 | tf_op jit(solution)/shard_map/ppermute | solution.py:438
  76.3 12.0 %collective-permute-start.12 = (bf16[80,2048]{1,0:T(8,128)(2,1)S(1)}, bf16[80,2048]{1,0:T(8,128)(2,1)S(1)}, u32[]{:S(2)}, u32[]{:S(2)}) collective-permute-start(bf16[80,2048]{1,0:T(8,128)(2,1)S(1)} %get-tuple-element.66), channel_id=1, source_target_pairs={{0,2},{1,3},{2,0},{3,1},{4,6},{5,7},{6,4},{7,5},{8,10},{9,11},{10,... | collective-permute-start | bytes 983048 | tf_op jit(solution)/shard_map/ppermute | solution.py:365
  77.9 16.3 %collective-permute-start.13 = (bf16[80,2048]{1,0:T(8,128)(2,1)S(1)}, bf16[80,2048]{1,0:T(8,128)(2,1)S(1)}, u32[]{:S(2)}, u32[]{:S(2)}) collective-permute-start(bf16[80,2048]{1,0:T(8,128)(2,1)S(1)} %get-tuple-element.67), channel_id=1, source_target_pairs={{0,4},{1,5},{2,6},{3,7},{4,0},{5,1},{6,2},{7,3},{8,12},{9,13},{10,... | collective-permute-start | bytes 983048 | tf_op jit(solution)/shard_map/ppermute | solution.py:365
  79.1 16.2 %collective-permute-start.14 = (bf16[80,2048]{1,0:T(8,128)(2,1)S(1)}, bf16[80,2048]{1,0:T(8,128)(2,1)S(1)}, u32[]{:S(2)}, u32[]{:S(2)}) collective-permute-start(bf16[80,2048]{1,0:T(8,128)(2,1)S(1)} %get-tuple-element.68), channel_id=1, source_target_pairs={{0,6},{1,7},{2,4},{3,5},{4,2},{5,3},{6,0},{7,1},{8,14},{9,15},{10,... | collective-permute-start | bytes 983048 | tf_op jit(solution)/shard_map/ppermute | solution.py:365
  88.3 1.6 collective-permute-start.16
  88.4 2.8 %collective-permute-start.17 = (bf16[64,2048]{1,0:T(8,128)(2,1)S(1)}, bf16[64,2048]{1,0:T(8,128)(2,1)S(1)}, u32[]{:S(2)}, u32[]{:S(2)}) collective-permute-start(bf16[64,2048]{1,0:T(8,128)(2,1)S(1)} %get-tuple-element.111), channel_id=1, source_target_pairs={{0,1},{1,0},{2,3},{3,2},{4,5},{5,4},{6,7},{7,6},{8,9},{9,8},{10,11... | collective-permute-start | bytes 786440 | tf_op jit(solution)/shard_map/ppermute | solution.py:368
  88.9 19.7 %collective-permute-start.31 = (bf16[128,2048]{1,0:T(8,128)(2,1)S(1)}, bf16[128,2048]{1,0:T(8,128)(2,1)S(1)}, u32[]{:S(2)}, u32[]{:S(2)}) collective-permute-start(bf16[128,2048]{1,0:T(8,128)(2,1)S(1)} %collective-permute-done.15.mine_ref), channel_id=1, source_target_pairs={{8,16},{16,8},{9,17},{17,9},{10,18},{18,10},{11,19},{19,11},{12,20... | collective-permute-start | bytes 1572872 | tf_op jit(solution)/shard_map/ppermute | solution.py:438
  89.9 18.5 %collective-permute-start.25 = (bf16[128,2048]{1,0:T(8,128)(2,1)S(1)}, bf16[128,2048]{1,0:T(8,128)(2,1)S(1)}, u32[]{:S(2)}, u32[]{:S(2)}) collective-permute-start(bf16[128,2048]{1,0:T(8,128)(2,1)S(1)} %collective-permute-done.24.__0_), channel_id=1, source_target_pairs={{8,0},{16,24},{9,1},{17,25},{10,2},{18,26},{11,3},{19,27},{12,4},{... | collective-permute-start | bytes 1572872 | tf_op jit(solution)/shard_map/ppermute | solution.py:438
  91.7 17.4 %collective-permute-start.21 = (bf16[80,2048]{1,0:T(8,128)(2,1)S(1)}, bf16[80,2048]{1,0:T(8,128)(2,1)S(1)}, u32[]{:S(2)}, u32[]{:S(2)}) collective-permute-start(bf16[80,2048]{1,0:T(8,128)(2,1)S(1)} %get-tuple-element.74), channel_id=1, source_target_pairs={{0,2},{1,3},{2,0},{3,1},{4,6},{5,7},{6,4},{7,5},{8,10},{9,11},{10,... | collective-permute-start | bytes 983048 | tf_op jit(solution)/shard_map/ppermute | solution.py:365
  94.2 19.9 %collective-permute-start.22 = (bf16[80,2048]{1,0:T(8,128)(2,1)S(1)}, bf16[80,2048]{1,0:T(8,128)(2,1)S(1)}, u32[]{:S(2)}, u32[]{:S(2)}) collective-permute-start(bf16[80,2048]{1,0:T(8,128)(2,1)S(1)} %get-tuple-element.75), channel_id=1, source_target_pairs={{0,4},{1,5},{2,6},{3,7},{4,0},{5,1},{6,2},{7,3},{8,12},{9,13},{10,... | collective-permute-start | bytes 983048 | tf_op jit(solution)/shard_map/ppermute | solution.py:365
  95.4 20.2 %collective-permute-start.23 = (bf16[80,2048]{1,0:T(8,128)(2,1)S(1)}, bf16[80,2048]{1,0:T(8,128)(2,1)S(1)}, u32[]{:S(2)}, u32[]{:S(2)}) collective-permute-start(bf16[80,2048]{1,0:T(8,128)(2,1)S(1)} %get-tuple-element.76), channel_id=1, source_target_pairs={{0,6},{1,7},{2,4},{3,5},{4,2},{5,3},{6,0},{7,1},{8,14},{9,15},{10,... | collective-permute-start | bytes 983048 | tf_op jit(solution)/shard_map/ppermute | solution.py:365
  104.6 20.2 %copy-start.3 = (bf16[80,2048]{1,0:T(8,128)(2,1)}, bf16[80,2048]{1,0:T(8,128)(2,1)S(1)}, u32[]{:S(2)}) copy-start(bf16[80,2048]{1,0:T(8,128)(2,1)S(1)} %get-tuple-element.71) | copy-start | bytes 983044
  108.5 2.1 collective-permute-start.26
  108.6 2.0 collective-permute-start.27
  109.1 15.9 %collective-permute-start.32 = (bf16[128,2048]{1,0:T(8,128)(2,1)S(1)}, bf16[128,2048]{1,0:T(8,128)(2,1)S(1)}, u32[]{:S(2)}, u32[]{:S(2)}) collective-permute-start(bf16[128,2048]{1,0:T(8,128)(2,1)S(1)} %collective-permute-done.31.__0_), channel_id=1, source_target_pairs={{8,0},{16,24},{9,1},{17,25},{10,2},{18,26},{11,3},{19,27},{12,4},{... | collective-permute-start | bytes 1572872 | tf_op jit(solution)/shard_map/ppermute | solution.py:438
  112.0 18.7 %collective-permute-start.38 = (bf16[80,2048]{1,0:T(8,128)(2,1)}, bf16[80,2048]{1,0:T(8,128)(2,1)}, u32[]{:S(2)}, u32[]{:S(2)}) collective-permute-start(bf16[80,2048]{1,0:T(8,128)(2,1)} %get-tuple-element.86), channel_id=1, source_target_pairs={{0,2},{1,3},{2,0},{3,1},{4,6},{5,7},{6,4},{7,5},{8,10},{9,11},{10,... | collective-permute-start | bytes 983048 | tf_op jit(solution)/shard_map/ppermute | solution.py:365
  113.5 18.7 %collective-permute-start.39 = (bf16[80,2048]{1,0:T(8,128)(2,1)}, bf16[80,2048]{1,0:T(8,128)(2,1)}, u32[]{:S(2)}, u32[]{:S(2)}) collective-permute-start(bf16[80,2048]{1,0:T(8,128)(2,1)} %get-tuple-element.87), channel_id=1, source_target_pairs={{0,4},{1,5},{2,6},{3,7},{4,0},{5,1},{6,2},{7,3},{8,12},{9,13},{10,... | collective-permute-start | bytes 983048 | tf_op jit(solution)/shard_map/ppermute | solution.py:365
  114.0 18.1 %collective-permute-start.40 = (bf16[80,2048]{1,0:T(8,128)(2,1)}, bf16[80,2048]{1,0:T(8,128)(2,1)}, u32[]{:S(2)}, u32[]{:S(2)}) collective-permute-start(bf16[80,2048]{1,0:T(8,128)(2,1)} %get-tuple-element.88), channel_id=1, source_target_pairs={{0,6},{1,7},{2,4},{3,5},{4,2},{5,3},{6,0},{7,1},{8,14},{9,15},{10,... | collective-permute-start | bytes 983048 | tf_op jit(solution)/shard_map/ppermute | solution.py:365
  126.0 1.7 collective-permute-start.33
  126.0 2.1 collective-permute-start.34
  128.6 17.0 %collective-permute-start.35 = (bf16[80,2048]{1,0:T(8,128)(2,1)S(1)}, bf16[80,2048]{1,0:T(8,128)(2,1)S(1)}, u32[]{:S(2)}, u32[]{:S(2)}) collective-permute-start(bf16[80,2048]{1,0:T(8,128)(2,1)S(1)} %get-tuple-element.83), channel_id=1, source_target_pairs={{0,2},{1,3},{2,0},{3,1},{4,6},{5,7},{6,4},{7,5},{8,10},{9,11},{10,... | collective-permute-start | bytes 983048 | tf_op jit(solution)/shard_map/ppermute | solution.py:365
  130.1 17.0 %collective-permute-start.36 = (bf16[80,2048]{1,0:T(8,128)(2,1)S(1)}, bf16[80,2048]{1,0:T(8,128)(2,1)S(1)}, u32[]{:S(2)}, u32[]{:S(2)}) collective-permute-start(bf16[80,2048]{1,0:T(8,128)(2,1)S(1)} %get-tuple-element.84), channel_id=1, source_target_pairs={{0,4},{1,5},{2,6},{3,7},{4,0},{5,1},{6,2},{7,3},{8,12},{9,13},{10,... | collective-permute-start | bytes 983048 | tf_op jit(solution)/shard_map/ppermute | solution.py:365
  130.7 16.4 %collective-permute-start.37 = (bf16[80,2048]{1,0:T(8,128)(2,1)S(1)}, bf16[80,2048]{1,0:T(8,128)(2,1)S(1)}, u32[]{:S(2)}, u32[]{:S(2)}) collective-permute-start(bf16[80,2048]{1,0:T(8,128)(2,1)S(1)} %get-tuple-element.85), channel_id=1, source_target_pairs={{0,6},{1,7},{2,4},{3,5},{4,2},{5,3},{6,0},{7,1},{8,14},{9,15},{10,... | collective-permute-start | bytes 983048 | tf_op jit(solution)/shard_map/ppermute | solution.py:365
  143.6 13.0 %collective-permute-start.44 = (bf16[80,2048]{1,0:T(8,128)(2,1)S(1)}, bf16[80,2048]{1,0:T(8,128)(2,1)S(1)}, u32[]{:S(2)}, u32[]{:S(2)}) collective-permute-start(bf16[80,2048]{1,0:T(8,128)(2,1)S(1)} %get-tuple-element.94), channel_id=1, source_target_pairs={{0,2},{1,3},{2,0},{3,1},{4,6},{5,7},{6,4},{7,5},{8,10},{9,11},{10,... | collective-permute-start | bytes 983048 | tf_op jit(solution)/shard_map/ppermute | solution.py:365
  145.1 15.7 %collective-permute-start.45 = (bf16[80,2048]{1,0:T(8,128)(2,1)S(1)}, bf16[80,2048]{1,0:T(8,128)(2,1)S(1)}, u32[]{:S(2)}, u32[]{:S(2)}) collective-permute-start(bf16[80,2048]{1,0:T(8,128)(2,1)S(1)} %get-tuple-element.95), channel_id=1, source_target_pairs={{0,4},{1,5},{2,6},{3,7},{4,0},{5,1},{6,2},{7,3},{8,12},{9,13},{10,... | collective-permute-start | bytes 983048 | tf_op jit(solution)/shard_map/ppermute | solution.py:365
  145.7 15.1 %collective-permute-start.46 = (bf16[80,2048]{1,0:T(8,128)(2,1)S(1)}, bf16[80,2048]{1,0:T(8,128)(2,1)S(1)}, u32[]{:S(2)}, u32[]{:S(2)}) collective-permute-start(bf16[80,2048]{1,0:T(8,128)(2,1)S(1)} %get-tuple-element.96), channel_id=1, source_target_pairs={{0,6},{1,7},{2,4},{3,5},{4,2},{5,3},{6,0},{7,1},{8,14},{9,15},{10,... | collective-permute-start | bytes 983048 | tf_op jit(solution)/shard_map/ppermute | solution.py:365
  162.5 3.6 %collective-permute-start.47 = (bf16[128,2048]{1,0:T(8,128)(2,1)S(1)}, bf16[128,2048]{1,0:T(8,128)(2,1)S(1)}, u32[]{:S(2)}, u32[]{:S(2)}) collective-permute-start(bf16[128,2048]{1,0:T(8,128)(2,1)S(1)} %get-tuple-element.98), channel_id=1, source_target_pairs={{0,1},{1,0},{2,3},{3,2},{4,5},{5,4},{6,7},{7,6},{8,9},{9,8},{10,11... | collective-permute-start | bytes 1572872 | tf_op jit(solution)/shard_map/ppermute | solution.py:368
  162.6 10.6 %collective-permute-start.41 = (bf16[80,2048]{1,0:T(8,128)(2,1)S(1)}, bf16[80,2048]{1,0:T(8,128)(2,1)S(1)}, u32[]{:S(2)}, u32[]{:S(2)}) collective-permute-start(bf16[80,2048]{1,0:T(8,128)(2,1)S(1)} %get-tuple-element.91), channel_id=1, source_target_pairs={{0,2},{1,3},{2,0},{3,1},{4,6},{5,7},{6,4},{7,5},{8,10},{9,11},{10,... | collective-permute-start | bytes 983048 | tf_op jit(solution)/shard_map/ppermute | solution.py:365
  163.2 16.8 %collective-permute-start.42 = (bf16[80,2048]{1,0:T(8,128)(2,1)S(1)}, bf16[80,2048]{1,0:T(8,128)(2,1)S(1)}, u32[]{:S(2)}, u32[]{:S(2)}) collective-permute-start(bf16[80,2048]{1,0:T(8,128)(2,1)S(1)} %get-tuple-element.92), channel_id=1, source_target_pairs={{0,4},{1,5},{2,6},{3,7},{4,0},{5,1},{6,2},{7,3},{8,12},{9,13},{10,... | collective-permute-start | bytes 983048 | tf_op jit(solution)/shard_map/ppermute | solution.py:365
  164.4 15.6 %collective-permute-start.43 = (bf16[80,2048]{1,0:T(8,128)(2,1)S(1)}, bf16[80,2048]{1,0:T(8,128)(2,1)S(1)}, u32[]{:S(2)}, u32[]{:S(2)}) collective-permute-start(bf16[80,2048]{1,0:T(8,128)(2,1)S(1)} %get-tuple-element.93), channel_id=1, source_target_pairs={{0,6},{1,7},{2,4},{3,5},{4,2},{5,3},{6,0},{7,1},{8,14},{9,15},{10,... | collective-permute-start | bytes 983048 | tf_op jit(solution)/shard_map/ppermute | solution.py:365
  166.3 15.6 %copy-start.10 = (bf16[80,2048]{1,0:T(8,128)(2,1)S(1)}, bf16[80,2048]{1,0:T(8,128)(2,1)}, u32[]{:S(2)}) copy-start(bf16[80,2048]{1,0:T(8,128)(2,1)} %copy-done.9) | copy-start | bytes 983044
  166.3 17.1 %copy-start.8 = (bf16[80,2048]{1,0:T(8,128)(2,1)S(1)}, bf16[80,2048]{1,0:T(8,128)(2,1)}, u32[]{:S(2)}) copy-start(bf16[80,2048]{1,0:T(8,128)(2,1)} %copy-done.7) | copy-start | bytes 983044
  166.3 17.7 %copy-start.6 = (bf16[80,2048]{1,0:T(8,128)(2,1)S(1)}, bf16[80,2048]{1,0:T(8,128)(2,1)}, u32[]{:S(2)}) copy-start(bf16[80,2048]{1,0:T(8,128)(2,1)} %copy-done.5) | copy-start | bytes 983044
  166.3 19.2 %collective-permute-start.49 = (bf16[128,2048]{1,0:T(8,128)(2,1)S(1)}, bf16[128,2048]{1,0:T(8,128)(2,1)S(1)}, u32[]{:S(2)}, u32[]{:S(2)}) collective-permute-start(bf16[128,2048]{1,0:T(8,128)(2,1)S(1)} %fusion.refs_4_), channel_id=1, source_target_pairs={{0,8},{24,16},{1,9},{25,17},{2,10},{26,18},{3,11},{27,19},{4,12},{... | collective-permute-start | bytes 1572872 | tf_op jit(solution)/shard_map/ppermute | solution.py:438
  181.8 3.8 %collective-permute-start.48 = (bf16[128,2048]{1,0:T(8,128)(2,1)S(1)}, bf16[128,2048]{1,0:T(8,128)(2,1)S(1)}, u32[]{:S(2)}, u32[]{:S(2)}) collective-permute-start(bf16[128,2048]{1,0:T(8,128)(2,1)S(1)} %get-tuple-element.100), channel_id=1, source_target_pairs={{0,1},{1,0},{2,3},{3,2},{4,5},{5,4},{6,7},{7,6},{8,9},{9,8},{10,11... | collective-permute-start | bytes 1572872 | tf_op jit(solution)/shard_map/ppermute | solution.py:368
  181.9 10.6 %collective-permute-start.28 = (bf16[80,2048]{1,0:T(8,128)(2,1)S(1)}, bf16[80,2048]{1,0:T(8,128)(2,1)S(1)}, u32[]{:S(2)}, u32[]{:S(2)}) collective-permute-start(bf16[80,2048]{1,0:T(8,128)(2,1)S(1)} %copy-done.10), channel_id=1, source_target_pairs={{0,2},{1,3},{2,0},{3,1},{4,6},{5,7},{6,4},{7,5},{8,10},{9,11},{10,... | collective-permute-start | bytes 983048 | tf_op jit(solution)/shard_map/ppermute | solution.py:365
  183.4 16.8 %collective-permute-start.29 = (bf16[80,2048]{1,0:T(8,128)(2,1)S(1)}, bf16[80,2048]{1,0:T(8,128)(2,1)S(1)}, u32[]{:S(2)}, u32[]{:S(2)}) collective-permute-start(bf16[80,2048]{1,0:T(8,128)(2,1)S(1)} %copy-done.8), channel_id=1, source_target_pairs={{0,4},{1,5},{2,6},{3,7},{4,0},{5,1},{6,2},{7,3},{8,12},{9,13},{10,... | collective-permute-start | bytes 983048 | tf_op jit(solution)/shard_map/ppermute | solution.py:365
  184.0 16.2 %collective-permute-start.30 = (bf16[80,2048]{1,0:T(8,128)(2,1)S(1)}, bf16[80,2048]{1,0:T(8,128)(2,1)S(1)}, u32[]{:S(2)}, u32[]{:S(2)}) collective-permute-start(bf16[80,2048]{1,0:T(8,128)(2,1)S(1)} %copy-done.6), channel_id=1, source_target_pairs={{0,6},{1,7},{2,4},{3,5},{4,2},{5,3},{6,0},{7,1},{8,14},{9,15},{10,... | collective-permute-start | bytes 983048 | tf_op jit(solution)/shard_map/ppermute | solution.py:365
  185.8 16.3 %copy-start.4 = (bf16[80,2048]{1,0:T(8,128)(2,1)S(1)}, bf16[80,2048]{1,0:T(8,128)(2,1)}, u32[]{:S(2)}) copy-start(bf16[80,2048]{1,0:T(8,128)(2,1)} %copy-done.3) | copy-start | bytes 983044
  202.0 4.3 %collective-permute-start.50 = (bf16[128,2048]{1,0:T(8,128)(2,1)S(1)}, bf16[128,2048]{1,0:T(8,128)(2,1)S(1)}, u32[]{:S(2)}, u32[]{:S(2)}) collective-permute-start(bf16[128,2048]{1,0:T(8,128)(2,1)S(1)} %get-tuple-element.102), channel_id=1, source_target_pairs={{0,1},{1,0},{2,3},{3,2},{4,5},{5,4},{6,7},{7,6},{8,9},{9,8},{10,11... | collective-permute-start | bytes 1572872 | tf_op jit(solution)/shard_map/ppermute | solution.py:368
  202.1 10.8 %collective-permute-start.18 = (bf16[80,2048]{1,0:T(8,128)(2,1)S(1)}, bf16[80,2048]{1,0:T(8,128)(2,1)S(1)}, u32[]{:S(2)}, u32[]{:S(2)}) collective-permute-start(bf16[80,2048]{1,0:T(8,128)(2,1)S(1)} %copy-done.4), channel_id=1, source_target_pairs={{0,2},{1,3},{2,0},{3,1},{4,6},{5,7},{6,4},{7,5},{8,10},{9,11},{10,... | collective-permute-start | bytes 983048 | tf_op jit(solution)/shard_map/ppermute | solution.py:365
  202.7 16.8 %collective-permute-start.19 = (bf16[80,2048]{1,0:T(8,128)(2,1)S(1)}, bf16[80,2048]{1,0:T(8,128)(2,1)S(1)}, u32[]{:S(2)}, u32[]{:S(2)}) collective-permute-start(bf16[80,2048]{1,0:T(8,128)(2,1)S(1)} %get-tuple-element.72), channel_id=1, source_target_pairs={{0,4},{1,5},{2,6},{3,7},{4,0},{5,1},{6,2},{7,3},{8,12},{9,13},{10,... | collective-permute-start | bytes 983048 | tf_op jit(solution)/shard_map/ppermute | solution.py:365
  203.9 15.6 %collective-permute-start.20 = (bf16[80,2048]{1,0:T(8,128)(2,1)S(1)}, bf16[80,2048]{1,0:T(8,128)(2,1)S(1)}, u32[]{:S(2)}, u32[]{:S(2)}) collective-permute-start(bf16[80,2048]{1,0:T(8,128)(2,1)S(1)} %get-tuple-element.73), channel_id=1, source_target_pairs={{0,6},{1,7},{2,4},{3,5},{4,2},{5,3},{6,0},{7,1},{8,14},{9,15},{10,... | collective-permute-start | bytes 983048 | tf_op jit(solution)/shard_map/ppermute | solution.py:365
  205.6 20.9 %collective-permute-start.53 = (bf16[128,2048]{1,0:T(8,128)(2,1)S(1)}, bf16[128,2048]{1,0:T(8,128)(2,1)S(1)}, u32[]{:S(2)}, u32[]{:S(2)}) collective-permute-start(bf16[128,2048]{1,0:T(8,128)(2,1)S(1)} %add_convert_fusion.3.refs_5_), channel_id=1, source_target_pairs={{8,16},{16,8},{9,17},{17,9},{10,18},{18,10},{11,19},{19,11},{12,20... | collective-permute-start | bytes 1572872 | tf_op jit(solution)/shard_map/ppermute | solution.py:438
  206.3 18.7 %collective-permute-start.54 = (bf16[128,2048]{1,0:T(8,128)(2,1)S(1)}, bf16[128,2048]{1,0:T(8,128)(2,1)S(1)}, u32[]{:S(2)}, u32[]{:S(2)}) collective-permute-start(bf16[128,2048]{1,0:T(8,128)(2,1)S(1)} %fusion.1.refs_4_), channel_id=1, source_target_pairs={{0,8},{24,16},{1,9},{25,17},{2,10},{26,18},{3,11},{27,19},{4,12},{... | collective-permute-start | bytes 1572872 | tf_op jit(solution)/shard_map/ppermute | solution.py:438
  212.9 21.7 %collective-permute-start.52 = (bf16[128,2048]{1,0:T(8,128)(2,1)S(1)}, bf16[128,2048]{1,0:T(8,128)(2,1)S(1)}, u32[]{:S(2)}, u32[]{:S(2)}) collective-permute-start(bf16[128,2048]{1,0:T(8,128)(2,1)S(1)} %add_convert_fusion.2.refs_4_), channel_id=1, source_target_pairs={{0,8},{8,0},{16,24},{24,16},{1,9},{9,1},{17,25},{25,17},{2,10},{10... | collective-permute-start | bytes 1572872 | tf_op jit(solution)/shard_map/ppermute | solution.py:438
  221.3 5.3 %collective-permute-start.51 = (bf16[128,2048]{1,0:T(8,128)(2,1)S(1)}, bf16[128,2048]{1,0:T(8,128)(2,1)S(1)}, u32[]{:S(2)}, u32[]{:S(2)}) collective-permute-start(bf16[128,2048]{1,0:T(8,128)(2,1)S(1)} %get-tuple-element.104), channel_id=1, source_target_pairs={{0,1},{1,0},{2,3},{3,2},{4,5},{5,4},{6,7},{7,6},{8,9},{9,8},{10,11... | collective-permute-start | bytes 1572872 | tf_op jit(solution)/shard_map/ppermute | solution.py:368
  225.3 13.4 %collective-permute-start.55 = (bf16[128,2048]{1,0:T(8,128)(2,1)S(1)}, bf16[128,2048]{1,0:T(8,128)(2,1)S(1)}, u32[]{:S(2)}, u32[]{:S(2)}) collective-permute-start(bf16[128,2048]{1,0:T(8,128)(2,1)S(1)} %add_convert_fusion.1), channel_id=1, source_target_pairs={{8,24},{16,0},{9,25},{17,1},{10,26},{18,2},{11,27},{19,3},{12,28},... | collective-permute-start | bytes 1572872 | tf_op jit(solution)/shard_map/ppermute | solution.py:438
  (8 other events, 38.5 us)
Sparse Core Ops, SparseCore 0:
  9.2 57.0 all-gather.1
